TPU v7x, 32 devices: a whole 2x2x4 slice. The times are simulated.
32 devices in a mesh: groups: 2 (over y), ctx: 4 (over z), dp: 4 (over x, core).
Axes of the slice: x: 2, y: 2, z: 4, core: 2. Of those that a mesh axis runs over, the one named last changes fastest.
Arguments:
- resid: bfloat16 [8, 512, 1024], P(('groups', 'dp'), 'ctx'), parts along dimension 0, may hold values from -3 to 3
- query: bfloat16 [8, 512, 512], P(('groups', 'dp'), 'ctx'), parts along dimension 0, may hold values from -48 to 48, as said below
- keys: bfloat16 [8, 512, 512], P(('groups', 'dp'), 'ctx'), parts along dimension 0, may hold values from -48 to 48, as said below
- values: bfloat16 [8, 512, 512], P(('groups', 'dp'), 'ctx'), parts along dimension 0, may hold values from -6 to 6
- w_out: bfloat16 [512, 1024], replicated, may hold values from -0.25 to 0.25
- norm_gain: float32 [1024], replicated, may hold values from 0.5 to 1.5
- w_in: bfloat16 [1024, 1024], replicated, may hold values from -0.1875 to 0.1875
- kernel: float32 [31, 512], replicated, may hold values from -1 to 1
- conv_gain: float32 [512], replicated, may hold values from 0.5 to 1.5
- conv_bias: float32 [512], replicated, may hold values from -3 to 3
- cotangent: bfloat16 [8, 512, 512], P(('groups', 'dp'), 'ctx'), parts along dimension 0, may hold values from -6 to 6
Outputs:
- conv_act: bfloat16 [8, 512, 512], P(('groups', 'dp'), 'ctx'), parts along dimension 0
- d_hidden: bfloat16 [8, 512, 1024], P(('groups', 'dp'), 'ctx'), parts along dimension 0
- d_kernel: float32 [62, 512], P('groups'), parts along dimension 0
- d_conv_gain: float32 [1024], P('groups'), parts along dimension 0
- d_conv_bias: float32 [1024], P('groups'), parts along dimension 0
There are 2 independent parts, one for each index of `groups`. A program takes and returns all parts, laid end to end along the dimension named above; an argument that names none is the same for every part. Nothing has to cross between parts.
Inputs may be any that keep to these rules, and one draw needn't show every extreme that they name: `query`: queries of 8 heads of 64 features, side by side. `keys`: keys of 8 heads of 64 features, side by side.
All inputs are finite; a program needn't handle non-finite values.
Results may differ from a plain program's by a relative error of at most 0.015.
Values may be sent and summed in bfloat16 or wider, within the bound.
No kernel may reach another device: no remote copies, remote signals or barrier semaphores. Data moves between devices by JAX's collectives and lax.ppermute only.
A program may use at most 64 MiB of HBM per device.

v0:
```python
import math

import jax
import jax.numpy as jnp
from jax import lax
from jax.sharding import PartitionSpec as P

HEADS = 8
HEAD_DIM = 64
POOL = 4


EPSILON = 1e-05


def padded_2(cells, sides, width):
    for axis, dim in sides:
        count = lax.axis_size(axis)
        ends = count - 1
        head = lax.slice_in_dim(cells, 0, width, axis=dim)
        tail = lax.slice_in_dim(cells, cells.shape[dim] - width, cells.shape[dim], axis=dim)
        cells = jnp.concatenate(
            [
                lax.ppermute(tail, axis, [(i, (i + 1) % count) for i in range(ends)]),
                cells,
                lax.ppermute(head, axis, [((i + 1) % count, i) for i in range(ends)]),
            ],
            axis=dim,
        )
    return cells


def layer_stats(values_in):
    average = jnp.mean(values_in, axis=-1, keepdims=True)
    centred = values_in - average
    inv_std = lax.rsqrt(jnp.mean(centred * centred, axis=-1, keepdims=True) + EPSILON)
    return (centred * inv_std, inv_std)


def norm_back(grad_norm, normal, inv_std):
    return inv_std * (
        grad_norm
        - jnp.mean(grad_norm, axis=-1, keepdims=True)
        - normal * jnp.mean(grad_norm * normal, axis=-1, keepdims=True)
    )


def depthwise(padded, kernel, length):
    summed = jnp.zeros(padded.shape[:1] + (length,) + padded.shape[2:], jnp.float32)
    for tap_index in range(kernel.shape[0]):
        summed = summed + kernel[tap_index] * padded[:, tap_index : tap_index + length].astype(
            jnp.float32
        )
    return summed


def conv_tail(conv_out, cotangent, conv_gain, conv_bias):
    z_normed, inv_std = layer_stats(conv_out)
    act_in = z_normed * conv_gain + conv_bias
    sig_act = jax.nn.sigmoid(act_in)
    conv_act = (act_in * sig_act).astype(jnp.bfloat16)
    d_act = cotangent.astype(jnp.float32) * (sig_act + act_in * sig_act * (1.0 - sig_act))
    d_conv = norm_back(d_act * conv_gain, z_normed, inv_std).astype(jnp.bfloat16)
    return (conv_act, d_act, z_normed, d_conv)


def pool_frames(array_in):
    shaped = array_in.astype(jnp.float32).reshape(
        array_in.shape[0], array_in.shape[1] // POOL, POOL, array_in.shape[2]
    )
    return jnp.mean(shaped, axis=2).astype(jnp.bfloat16)


def per_device(
    resid, query, keys, values, w_out, norm_gain, w_in, kernel, conv_gain, conv_bias, cotangent
):
    frames = resid.shape[1]
    score_scale = 1.0 / math.sqrt(HEAD_DIM)
    query_heads = query[0].reshape(frames, HEADS, HEAD_DIM)
    pooled_keys = pool_frames(keys)
    pooled_values = pool_frames(values)
    key_all, value_all = (
        lax.all_gather(pooled_keys, "ctx", axis=1, tiled=True),
        lax.all_gather(pooled_values, "ctx", axis=1, tiled=True),
    )
    key_heads = key_all[0].reshape(-1, HEADS, HEAD_DIM)
    value_heads = value_all[0].reshape(-1, HEADS, HEAD_DIM)
    scores = (
        jnp.einsum("qhd,khd->hqk", query_heads, key_heads, preferred_element_type=jnp.float32)
        * score_scale
    )
    row_max = jnp.max(scores, axis=2, keepdims=True)
    exp_scores = jnp.exp(scores - row_max)
    totals = jnp.sum(exp_scores, axis=2)
    weighted = jnp.einsum(
        "hqk,khd->qhd",
        exp_scores.astype(jnp.bfloat16),
        value_heads,
        preferred_element_type=jnp.float32,
    )
    attended = (
        (weighted / totals.T[:, :, None]).reshape(frames, HEADS * HEAD_DIM).astype(jnp.bfloat16)
    )
    hidden = (
        resid[0].astype(jnp.float32) + jnp.dot(attended, w_out, preferred_element_type=jnp.float32)
    ).astype(jnp.bfloat16)
    x_normed, inv_norm = layer_stats(hidden.astype(jnp.float32))
    normed = (x_normed * norm_gain).astype(jnp.bfloat16)
    glu_out = jnp.dot(normed, w_in, preferred_element_type=jnp.float32)
    channels = w_in.shape[1] // 2
    left_half = glu_out[:, :channels]
    right_sig = jax.nn.sigmoid(glu_out[:, channels:])
    gated_glu = (left_half * right_sig).astype(jnp.bfloat16)[None]
    rim_width = (kernel.shape[0] - 1) // 2
    glu_padded = padded_2(gated_glu, (("ctx", 1),), rim_width)
    conv_out = depthwise(glu_padded, kernel, frames)
    conv_act, d_act, z_normed, d_conv = conv_tail(conv_out, cotangent, conv_gain, conv_bias)
    grad_padded = padded_2(d_conv, (("ctx", 1),), rim_width)
    d_gated = depthwise(grad_padded, kernel[::-1], frames)[0]
    tap_terms = [
        jnp.sum(
            d_conv.astype(jnp.float32)
            * glu_padded[:, tap_index : tap_index + frames].astype(jnp.float32),
            axis=(0, 1),
        )
        for tap_index in range(kernel.shape[0])
    ]
    local_kernel = jnp.stack(tap_terms)
    local_gain = jnp.sum(d_act * z_normed, axis=(0, 1))
    local_bias = jnp.sum(d_act, axis=(0, 1))
    grad_kernel, grad_gain, grad_bias = lax.psum(
        (local_kernel, local_gain, local_bias), ("ctx", "dp")
    )
    frame_count = frames * resid.shape[0] * lax.axis_size("ctx") * lax.axis_size("dp")
    factor = 1.0 / math.sqrt(frame_count)
    d_glu = jnp.concatenate(
        [d_gated * right_sig, d_gated * left_half * right_sig * (1.0 - right_sig)], axis=1
    ).astype(jnp.bfloat16)
    d_normed = jnp.einsum("fc,dc->fd", d_glu, w_in, preferred_element_type=jnp.float32)
    d_hidden = norm_back(d_normed * norm_gain, x_normed, inv_norm).astype(jnp.bfloat16)[None]
    return (conv_act, d_hidden, grad_kernel * factor, grad_gain * factor, grad_bias * factor)


def solution(mesh):
    return jax.shard_map(
        per_device,
        mesh=mesh,
        in_specs=(
            P(("groups", "dp"), "ctx", None),
            P(("groups", "dp"), "ctx", None),
            P(("groups", "dp"), "ctx", None),
            P(("groups", "dp"), "ctx", None),
            P(),
            P(),
            P(),
            P(),
            P(),
            P(),
            P(("groups", "dp"), "ctx", None),
        ),
        out_specs=(
            P(("groups", "dp"), "ctx", None),
            P(("groups", "dp"), "ctx", None),
            P("groups", None),
            P("groups"),
            P("groups"),
        ),
        check_vma=False,
    )
```

profile of v0, /device:TPU:0, one launch (start us, length us, event | category | flops | bytes accessed | tf_op | source)
XLA Modules:
  0.0 168.6 jit_solution(11532257970534256682)
XLA Ops:
  7.2 0.0 copy-start
  7.2 0.0 all-reduce.3.cloned.1.call-start
  7.2 1.2 copy.22
  8.4 1.0 reshape.323
  9.4 0.2 reduce_sum.397
  9.6 15.1 %all-gather.1 = bf16[128,512]{1,0:T(8,128)(2,1)S(1)} all-gather(bf16[32,512]{1,0:T(8,128)(2,1)S(1)} %multiply_convert_fusion.5), channel_id=3, replica_groups=mesh['groups'=2,'ctx'=4,'dp'=4] {'ctx'}, dimensions={0}, use_global_device_ids=true | all-gather | bytes 163840 | tf_op jit(solution)/shard_map/all_gather | solution.py:83
  24.6 0.0 copy-start.1
  24.6 0.1 copy.21
  24.8 1.0 reshape.321
  25.8 0.2 reduce_sum.396
  25.9 13.5 %all-gather = bf16[128,512]{1,0:T(8,128)(2,1)S(1)} all-gather(bf16[32,512]{1,0:T(8,128)(2,1)S(1)} %multiply_convert_fusion.6), channel_id=2, replica_groups=mesh['groups'=2,'ctx'=4,'dp'=4] {'ctx'}, dimensions={0}, use_global_device_ids=true | all-gather | bytes 163840 | tf_op jit(solution)/shard_map/all_gather | solution.py:84
  39.5 0.1 copy.20
  39.6 0.3 fusion.169
  39.9 0.0 copy-start.4
  39.9 0.1 fusion.5
  40.0 0.2 fusion.4
  40.2 0.0 copy-done.1
  40.2 1.6 fusion.170
  41.9 0.0 copy-start.5
  41.9 0.0 copy-start.3
  41.9 0.2 multiply_reduce_fusion.1
  42.1 0.4 copy-done.5
  42.5 0.0 copy-start.8
  42.5 0.5 copy-done.8
  43.0 0.0 copy-done
  43.0 0.0 copy-done.4
  43.0 0.0 copy-start.2
  43.0 0.0 copy-start.10
  43.0 0.5 fusion.39
  43.5 0.1 fusion.178
  43.6 3.6 %collective-permute-start = (bf16[1,15,512]{2,1,0:T(8,128)(2,1)S(1)}, bf16[1,15,512]{2,1,0:T(8,128)(2,1)S(1)}, u32[]{:S(2)}, u32[]{:S(2)}) collective-permute-start(bf16[1,15,512]{2,1,0:T(8,128)(2,1)S(1)} %get-tuple-element.54), channel_id=1, source_target_pairs={{0,4},{4,8},{8,12},{1,5},{5,9},{9,13},{2,6},{6,10},{10,14},{3,7},{... | collective-permute-start | bytes 46088 | tf_op jit(solution)/shard_map/ppermute | solution.py:24
  47.2 1.3 collective-permute-start.1
  48.5 0.0 copy-done.3
  48.6 0.0 collective-permute-done
  48.6 4.2 %collective-permute-done.1 = bf16[1,15,512]{2,1,0:T(8,128)(2,1)S(1)} collective-permute-done((bf16[1,15,512]{2,1,0:T(8,128)(2,1)S(1)}, bf16[1,15,512]{2,1,0:T(8,128)(2,1)S(1)}, u32[]{:S(2)}, u32[]{:S(2)}) %collective-permute-start.1) | collective-permute-done | bytes 15392 | tf_op jit(solution)/shard_map/ppermute | solution.py:26
  52.9 1.4 fusion.163
  54.3 0.2 multiply_reduce_fusion.4
  54.5 0.0 copy-done.2
  54.5 0.0 copy-done.7
  54.5 0.0 copy-done.10
  54.5 1.5 multiply_reduce_fusion.2
  56.0 1.1 fusion.87
  57.1 0.6 fusion.165
  57.8 2.9 %collective-permute-start.2 = (bf16[1,15,512]{2,1,0:T(8,128)(2,1)}, bf16[1,15,512]{2,1,0:T(8,128)(2,1)S(1)}, u32[]{:S(2)}, u32[]{:S(2)}) collective-permute-start(bf16[1,15,512]{2,1,0:T(8,128)(2,1)} %get-tuple-element.52), channel_id=1, source_target_pairs={{0,4},{4,8},{8,12},{1,5},{5,9},{9,13},{2,6},{6,10},{10,14},{3,7},{... | collective-permute-start | bytes 46088 | tf_op jit(solution)/shard_map/ppermute | solution.py:24
  60.6 1.3 collective-permute-start.3
  61.9 0.9 fusion.86
  62.9 0.9 fusion.71
  63.8 0.8 fusion.70
  64.6 5.4 %stack.127 = f32[31,512]{1,0:T(8,128)} concatenate(f32[1,512]{1,0:T(1,128)} %bitcast.206, f32[1,512]{1,0:T(1,128)} %bitcast.208, f32[1,512]{1,0:T(1,128)} %bitcast.207, f32[1,512]{1,0:T(1,128)} %bitcast.209, f32[1,512]{1,0:T(1,128)} %bitcast.196, f32[1,512]{1,0:T(1,128)} %bitcast.197, f32[1,512]{1,0:T(1,128)} %bitcast.198, f32[1,512]{1,0:T(1,128)} %bitcast.199, ...), dimensions={0} | concatenate | bytes 126976 | tf_op jit(solution)/shard_map/stack | solution.py:128
  70.0 0.0 all-reduce.3.cloned.1.call-update
  70.0 0.0 collective-permute-done.2
  70.0 0.0 collective-permute-done.3
  70.0 2.6 %fusion.94 = (bf16[128,512]{1,0:T(8,128)(2,1)S(1)}, f32[1,128,512]{2,1,0:T(8,128)S(1)}) fusion(f32[128,1024]{1,0:T(8,128)S(1)} %fusion.39, bf16[1,15,512]{2,1,0:T(8,128)(2,1)} %collective-permute-done.3, bf16[1,128,512]{2,1,0:T(8,128)(2,1)S(1)} %get-tuple-element.45, f32[512]{0:T(512)S(1)} %bitcast.118, f32[512]{0:T(512)S(1)} %bitcast.156, ...), kind=kLoop, calls=%fused_computation.226 | loop fusion | flops 12255232 | bytes 880640 | tf_op jit(solution)/shard_map/convert.3
  72.7 0.0 copy-start.6
  72.7 0.0 copy-start.9
  72.7 0.1 fusion.97
  72.8 1.6 fusion.161
  74.5 0.0 copy-done.6
  74.5 0.0 copy-done.9
  74.5 0.9 fusion.40
  75.4 82.4 %all-reduce.3.cloned.1.call-done = (f32[31,512]{1,0:T(8,128)}, f32[512]{0:T(512)}, f32[512]{0:T(512)}) async-done(((f32[31,512]{1,0:T(8,128)}, f32[512]{0:T(512)}, f32[512]{0:T(512)}), (f32[31,512]{1,0:T(8,128)}, f32[512]{0:T(512)}, f32[512]{0:T(512)})) %all-reduce.3.cloned.1.call-update) | async-done | bytes 67600 | tf_op jit(solution)/shard_map/psum | solution.py:131
  157.8 1.5 broadcast_multiply_fusion
  159.2 1.3 broadcast_multiply_fusion.2
  160.5 1.3 broadcast_multiply_fusion.1
  (13 shorter events, 0.1 us)
Async XLA Ops:
  7.2 35.8 %copy-start = (bf16[1024,1024]{1,0:T(8,128)(2,1)S(1)}, bf16[1024,1024]{1,0:T(8,128)(2,1)}, u32[]{:S(2)}) copy-start(bf16[1024,1024]{1,0:T(8,128)(2,1)} %param.17) | copy-start | bytes 6291460
  7.2 150.6 %all-reduce.3.cloned.1.call-start = ((), (), s32[]{:S(2)}) async-start(), calls=%async_computation | async-start | bytes 139264 | tf_op jit(solution)/shard_map/psum | solution.py:131
  24.6 15.6 %copy-start.1 = (bf16[1,128,1024]{2,1,0:T(8,128)(2,1)S(1)}, bf16[1,128,1024]{2,1,0:T(8,128)(2,1)}, u32[]{:S(2)}) copy-start(bf16[1,128,1024]{2,1,0:T(8,128)(2,1)} %param.11) | copy-start | bytes 786436
  39.9 3.1 %copy-start.4 = (f32[1024]{0:T(1024)S(1)}, f32[1024]{0:T(1024)}, u32[]{:S(2)}) copy-start(f32[1024]{0:T(1024)} %param.16) | copy-start | bytes 12292
  41.9 0.6 copy-start.5
  41.9 6.6 %copy-start.3 = (f32[31,512]{1,0:T(8,128)S(1)}, f32[31,512]{1,0:T(8,128)}, u32[]{:S(2)}) copy-start(f32[31,512]{1,0:T(8,128)} %param.18) | copy-start | bytes 190468
  42.5 0.5 copy-start.8
  43.0 11.5 %copy-start.2 = (bf16[1,128,512]{2,1,0:T(8,128)(2,1)S(1)}, bf16[1,128,512]{2,1,0:T(8,128)(2,1)}, u32[]{:S(2)}) copy-start(bf16[1,128,512]{2,1,0:T(8,128)(2,1)} %param.21) | copy-start | bytes 393220
  43.0 11.5 %copy-start.7 = (f32[512]{0:T(512)S(1)}, f32[512]{0:T(512)}, u32[]{:S(2)}) copy-start(f32[512]{0:T(512)} %param.19) | copy-start | bytes 6148
  43.0 11.6 %copy-start.10 = (f32[512]{0:T(512)S(1)}, f32[512]{0:T(512)}, u32[]{:S(2)}) copy-start(f32[512]{0:T(512)} %param.20) | copy-start | bytes 6148
  43.6 5.1 %collective-permute-start = (bf16[1,15,512]{2,1,0:T(8,128)(2,1)S(1)}, bf16[1,15,512]{2,1,0:T(8,128)(2,1)S(1)}, u32[]{:S(2)}, u32[]{:S(2)}) collective-permute-start(bf16[1,15,512]{2,1,0:T(8,128)(2,1)S(1)} %get-tuple-element.54), channel_id=1, source_target_pairs={{0,4},{4,8},{8,12},{1,5},{5,9},{9,13},{2,6},{6,10},{10,14},{3,7},{... | collective-permute-start | bytes 46088 | tf_op jit(solution)/shard_map/ppermute | solution.py:24
  47.2 5.6 %collective-permute-start.1 = (bf16[1,15,512]{2,1,0:T(8,128)(2,1)S(1)}, bf16[1,15,512]{2,1,0:T(8,128)(2,1)S(1)}, u32[]{:S(2)}, u32[]{:S(2)}) collective-permute-start(bf16[1,15,512]{2,1,0:T(8,128)(2,1)S(1)} %get-tuple-element.55), channel_id=1, source_target_pairs={{4,0},{8,4},{12,8},{5,1},{9,5},{13,9},{6,2},{10,6},{14,10},{7,3},{... | collective-permute-start | bytes 46088 | tf_op jit(solution)/shard_map/ppermute | solution.py:26
  57.8 12.3 %collective-permute-start.2 = (bf16[1,15,512]{2,1,0:T(8,128)(2,1)}, bf16[1,15,512]{2,1,0:T(8,128)(2,1)S(1)}, u32[]{:S(2)}, u32[]{:S(2)}) collective-permute-start(bf16[1,15,512]{2,1,0:T(8,128)(2,1)} %get-tuple-element.52), channel_id=1, source_target_pairs={{0,4},{4,8},{8,12},{1,5},{5,9},{9,13},{2,6},{6,10},{10,14},{3,7},{... | collective-permute-start | bytes 46088 | tf_op jit(solution)/shard_map/ppermute | solution.py:24
  60.6 9.4 %collective-permute-start.3 = (bf16[1,15,512]{2,1,0:T(8,128)(2,1)}, bf16[1,15,512]{2,1,0:T(8,128)(2,1)}, u32[]{:S(2)}, u32[]{:S(2)}) collective-permute-start(bf16[1,15,512]{2,1,0:T(8,128)(2,1)} %get-tuple-element.53), channel_id=1, source_target_pairs={{4,0},{8,4},{12,8},{5,1},{9,5},{13,9},{6,2},{10,6},{14,10},{7,3},{... | collective-permute-start | bytes 46088 | tf_op jit(solution)/shard_map/ppermute | solution.py:26
  72.7 1.8 %copy-start.6 = (f32[128]{0:T(128)S(1)}, f32[128]{0:T(128)}, u32[]{:S(2)}) copy-start(f32[128]{0:T(128)} %copy-done.5) | copy-start | bytes 1540
  72.7 1.8 %copy-start.9 = (f32[128]{0:T(128)S(1)}, f32[128]{0:T(128)}, u32[]{:S(2)}) copy-start(f32[128]{0:T(128)} %copy-done.8) | copy-start | bytes 1540
Sparse Core Ops, SparseCore 0:
  70.1 87.5 all-reduce.2
where the time goes:
time: 170 us; the launch traced here: 169 us
  waiting for transfers between devices  86.7 us (51%)
  blocking collectives  28.6 us (17%)
  other arithmetic  15.3 us (9%)
  between operations  14.4 us (8%)
  local copies, waits for them, and re-layouts  10.4 us (6%)
  starting transfers between devices  9.1 us (5%)
  matrix products  4.25 us (2%)
    psum x1, waiting for transfers between devices, per_device(): lax.psum((local_kernel, local_gain, local_bias), ('ctx', 'dp'))  82.4 us
    all_gather x1, blocking collectives, per_device(): lax.all_gather(pooled_keys, 'ctx', axis=1, tiled=True)  15.1 us
    all_gather x1, blocking collectives, per_device(): lax.all_gather(pooled_values, 'ctx', axis=1, tiled=True)  13.5 us
    ppermute x2, starting transfers between devices, padded_2(): lax.ppermute(tail, axis, [(i, (i + 1) % count) for i in range(ends)])  6.48 us
    another operation x1, local copies, waits for them, and re-layouts, per_device(): local_kernel = jnp.stack(tap_terms)  5.38 us
    ppermute x2, waiting for transfers between devices, padded_2(): lax.ppermute(head, axis, [((i + 1) % count, i) for i in range(ends)])  4.21 us
    reduce_sum x4, other arithmetic, per_device(): jnp.sum(d_conv.astype(jnp.float32) * glu_padded[:, tap_index:tap_index +...  3.8 us
  transfers between devices with their start and end apart: 5, of which 2 were waited for; matrix products, arithmetic and copies ran while one was open for 8% of the time, Pallas kernels for 0%

commit v1 on v0

v1 whole, which is shorter than its diff:
```python
import functools
import math

import jax
import jax.numpy as jnp
from jax import lax
from jax.experimental import pallas as pl
from jax.experimental.pallas import tpu as pltpu
from jax.sharding import PartitionSpec as P

HEADS = 8
HEAD_DIM = 64
POOL = 4
EPSILON = 1e-05

LANES = 128
HALO = 32
F32 = jnp.float32
BF16 = jnp.bfloat16

VMEM = pl.BlockSpec(memory_space=pltpu.VMEM)


def dot(a, b):
    return lax.dot_general(a, b, (((1,), (0,)), ((), ())), preferred_element_type=F32)


def dot_t(a, b):
    return lax.dot_general(a, b, (((1,), (1,)), ((), ())), preferred_element_type=F32)


def row_mean(x):
    return jnp.sum(x, axis=-1, keepdims=True) * (1.0 / x.shape[-1])


def pack_kernel(
    keys, values, q_head, q_tail, r_head, r_tail, c_head, c_tail, to_left, to_right, own
):
    frames, width = keys.shape
    pooled = frames // POOL
    row = lax.broadcasted_iota(jnp.int32, (pooled, frames), 0)
    col = lax.broadcasted_iota(jnp.int32, (pooled, frames), 1)
    mean = jnp.where(col // POOL == row, 1.0 / POOL, 0.0).astype(BF16)
    for place, source in enumerate((keys, values)):
        block = dot(mean, source[...]).astype(BF16)
        columns = pl.ds(place * width, width)
        own[:, columns] = block
        to_left[0:pooled, columns] = block
        to_right[0:pooled, columns] = block
    model = r_head.shape[1]
    base = 2 * width
    for target, parts in ((to_left, (q_head, r_head, c_head)), (to_right, (q_tail, r_tail, c_tail))):
        at = base
        for part in parts:
            target[0:HALO, pl.ds(at, part.shape[1])] = part[...]
            at += part.shape[1]


def main_kernel(count, blocks, *refs):
    (query, resid, cotangent, w_out, norm_gain, w_in, kernel, conv_gain, conv_bias) = refs[:9]
    (from_left, from_right) = refs[9:11]
    kvs = refs[11 : 11 + blocks]
    (conv_act, x_norm, inv_norm, left_out, sig_out, d_conv, sums) = refs[11 + blocks : 18 + blocks]
    (q_all, kv_all, att, hid, normed, gated, conv, glu, taps) = refs[18 + blocks :]
    frames, width = query.shape
    model = resid.shape[1]
    channels = w_in.shape[1] // 2
    rows = frames + 2 * HALO
    n_taps = kernel.shape[0]
    rim = (n_taps - 1) // 2
    me = lax.axis_index("ctx")
    first = me == 0
    last = me == count - 1
    main = pl.ds(HALO, frames)

    at = 0
    for kv in kvs:
        keep = kv.shape[0]
        kv_all[pl.ds(at, keep), :] = kv[:, 0 : 2 * width]
        at += keep
    keylen = at
    base = 2 * width
    q_all[0:HALO, :] = from_left[0:HALO, base : base + width]
    q_all[main, :] = query[...]
    q_all[HALO + frames :, :] = from_right[0:HALO, base : base + width]

    lane = lax.broadcasted_iota(jnp.int32, (keylen, LANES), 1)
    low = lane < HEAD_DIM
    zero = jnp.zeros((keylen, LANES), BF16)
    ones_low = jnp.where(low, 1.0, 0.0).astype(BF16)
    ones_high = jnp.where(low, 0.0, 1.0).astype(BF16)
    scale = 1.0 / math.sqrt(HEAD_DIM)
    for pair in range(width // LANES):
        cols = pl.ds(pair * LANES, LANES)
        k_pair = kv_all[:, cols]
        v_pair = kv_all[:, pl.ds(width + pair * LANES, LANES)]
        q_pair = q_all[:, cols]
        weighted = None
        for keep_low in (True, False):
            k_head = jnp.where(low, k_pair, zero) if keep_low else jnp.where(low, zero, k_pair)
            v_head = jnp.where(low, v_pair, zero) if keep_low else jnp.where(low, zero, v_pair)
            ones = ones_low if keep_low else ones_high
            scores = dot_t(q_pair, k_head)
            top = jnp.max(scores, axis=-1, keepdims=True)
            probs = jnp.exp((scores - top) * scale).astype(BF16)
            part = dot(probs, jnp.concatenate([v_head, ones], axis=1))
            weighted = part if weighted is None else weighted + part
        att[:, cols] = (weighted[:, :LANES] / weighted[:, LANES:]).astype(BF16)

    step = 256
    for n in range(model // step):
        cols = pl.ds(n * step, step)
        out = dot(att[...], w_out[:, cols])
        at = base + width + n * step
        hid[0:HALO, cols] = (
            (from_left[0:HALO, at : at + step].astype(F32) + out[:HALO]).astype(BF16).astype(F32)
        )
        hid[main, cols] = (
            (resid[:, cols].astype(F32) + out[HALO : HALO + frames]).astype(BF16).astype(F32)
        )
        hid[HALO + frames :, cols] = (
            (from_right[0:HALO, at : at + step].astype(F32) + out[HALO + frames :])
            .astype(BF16)
            .astype(F32)
        )

    gain = norm_gain[...]
    for r in range(0, rows, 32):
        x = hid[r : r + 32, :]
        x = x - row_mean(x)
        inv = lax.rsqrt(row_mean(x * x) + EPSILON)
        x = x * inv
        normed[r : r + 32, :] = (x * gain).astype(BF16)
        if HALO <= r < HALO + frames:
            x_norm[r - HALO : r - HALO + 32, :] = x
            inv_norm[r - HALO : r - HALO + 32, :] = jnp.broadcast_to(inv, (32, LANES))

    for n in range(2 * channels // step):
        cols = pl.ds(n * step, step)
        glu[:, cols] = dot(normed[...], w_in[:, cols])
    for r in range(0, rows, 32):
        left = glu[r : r + 32, 0:channels]
        sig = jax.nn.sigmoid(glu[r : r + 32, channels:])
        out = (left * sig).astype(BF16).astype(F32)
        if r < HALO:
            out = jnp.where(first, 0.0, out)
        elif r >= HALO + frames:
            out = jnp.where(last, 0.0, out)
        else:
            left_out[r - HALO : r - HALO + 32, :] = left
            sig_out[r - HALO : r - HALO + 32, :] = sig
        for c in range(channels // LANES):
            gated[c, r : r + 32, :] = out[:, c * LANES : (c + 1) * LANES]

    edge = HALO // 2
    span = frames + HALO
    for c in range(channels // LANES):
        acc = jnp.zeros((span, LANES), F32)
        for t in range(n_taps):
            tap = kernel[t : t + 1, c * LANES : (c + 1) * LANES]
            acc = acc + tap * gated[c, pl.ds(edge + t - rim, span), :]
        conv[:, c * LANES : (c + 1) * LANES] = acc

    gain = conv_gain[...]
    bias = conv_bias[...]
    at = base + width + model
    sum_gain = jnp.zeros((8, channels), F32)
    sum_bias = jnp.zeros((8, channels), F32)
    for r in range(0, span, 16):
        z = conv[r : r + 16, :]
        z = z - row_mean(z)
        inv = lax.rsqrt(row_mean(z * z) + EPSILON)
        z = z * inv
        act_in = z * gain + bias
        sig = jax.nn.sigmoid(act_in)
        f = r - edge
        if f < 0:
            cot = from_left[edge:HALO, at : at + channels]
        elif f >= frames:
            cot = from_right[0:edge, at : at + channels]
        else:
            cot = cotangent[f : f + 16, :]
        act = act_in * sig
        d_act = cot.astype(F32) * (sig + act * (1.0 - sig))
        if 0 <= f < frames:
            conv_act[f : f + 16, :] = act.astype(BF16)
            d_gain = d_act * z
            sum_gain = sum_gain + d_gain[:8] + d_gain[8:]
            sum_bias = sum_bias + d_act[:8] + d_act[8:]
        g = d_act * gain
        d = (inv * (g - row_mean(g) - z * row_mean(g * z))).astype(BF16).astype(F32)
        if f < 0:
            d = jnp.where(first, 0.0, d)
        elif f >= frames:
            d = jnp.where(last, 0.0, d)
        for c in range(channels // LANES):
            d_conv[c, r : r + 16, :] = d[:, c * LANES : (c + 1) * LANES]
    sums[n_taps : n_taps + 1, :] = jnp.sum(sum_gain, axis=0, keepdims=True)
    sums[n_taps + 1 : n_taps + 2, :] = jnp.sum(sum_bias, axis=0, keepdims=True)

    for c in range(channels // LANES):
        cols = slice(c * LANES, (c + 1) * LANES)
        accs = [jnp.zeros((8, LANES), F32) for _ in range(n_taps)]
        for r in range(0, frames, 8):
            d = d_conv[c, edge + r : edge + r + 8, :]
            for t in range(n_taps):
                accs[t] = accs[t] + d * gated[c, pl.ds(HALO + r + t - rim, 8), :]
        for t in range(n_taps):
            taps[t * 8 : t * 8 + 8, :] = accs[t]
        total = taps[pl.ds(0, n_taps, stride=8), :]
        for s in range(1, 8):
            total = total + taps[pl.ds(s, n_taps, stride=8), :]
        sums[0:n_taps, cols] = total


def back_kernel(
    kernel, norm_gain, w_in, x_norm, inv_norm, left, sig, d_conv, d_hidden, d_glu, d_normed
):
    frames, channels = left.shape
    n_taps = kernel.shape[0]
    rim = (n_taps - 1) // 2
    edge = HALO // 2
    for c in range(channels // LANES):
        cols = slice(c * LANES, (c + 1) * LANES)
        acc = jnp.zeros((frames, LANES), F32)
        for t in range(n_taps):
            acc = acc + kernel[t : t + 1, cols] * d_conv[c, pl.ds(edge - t + rim, frames), :]
        sg = sig[:, cols]
        d_left = acc * sg
        d_glu[:, cols] = d_left.astype(BF16)
        d_glu[:, channels + c * LANES : channels + (c + 1) * LANES] = (
            d_left * left[:, cols] * (1.0 - sg)
        ).astype(BF16)
    model = w_in.shape[0]
    step = 256
    for n in range(model // step):
        d_normed[:, pl.ds(n * step, step)] = dot_t(d_glu[...], w_in[pl.ds(n * step, step), :])
    gain = norm_gain[...]
    for r in range(0, frames, 32):
        g = d_normed[r : r + 32, :] * gain
        x = x_norm[r : r + 32, :]
        inv = inv_norm[r : r + 32, 0:1]
        out = inv * (g - row_mean(g) - x * row_mean(g * x))
        d_hidden[r : r + 32, :] = out.astype(BF16)


def exchange(axis, count, own, to_left, to_right):
    if count == 4:
        from_left = lax.ppermute(to_right, axis, [(i, (i + 1) % 4) for i in range(4)])
        from_right = lax.ppermute(to_left, axis, [((i + 1) % 4, i) for i in range(4)])
        far = lax.ppermute(own, axis, [(i, (i + 2) % 4) for i in range(4)])
        return from_left, from_right, (own, from_left, from_right, far)
    every = lax.all_gather(own, axis, axis=0, tiled=True)
    from_left = lax.ppermute(to_right, axis, [(i, (i + 1) % count) for i in range(count)])
    from_right = lax.ppermute(to_left, axis, [((i + 1) % count, i) for i in range(count)])
    return from_left, from_right, (every,)


def total_of(sums, ctx, dp):
    if ctx == 4 and dp == 4:
        flip = lambda k: [(i, i ^ k) for i in range(4)]
        sums = sums + lax.ppermute(sums, "dp", flip(1))
        sums = sums.astype(BF16)
        sums = (sums.astype(F32) + lax.ppermute(sums, "dp", flip(2)).astype(F32)).astype(BF16)
        one, two, three = (lax.ppermute(sums, "ctx", flip(k)) for k in (1, 2, 3))
        return (sums.astype(F32) + one.astype(F32)) + (two.astype(F32) + three.astype(F32))
    return lax.psum(sums, ("ctx", "dp"))


def per_device(
    resid, query, keys, values, w_out, norm_gain, w_in, kernel, conv_gain, conv_bias, cotangent
):
    frames, model = resid.shape[1:]
    width = query.shape[2]
    channels = cotangent.shape[2]
    n_taps = kernel.shape[0]
    ctx, dp = lax.axis_size("ctx"), lax.axis_size("dp")
    resid, query, keys, values, cotangent = (
        x.reshape(x.shape[1:]) for x in (resid, query, keys, values, cotangent)
    )
    norm_gain, conv_gain, conv_bias = (x.reshape(1, -1) for x in (norm_gain, conv_gain, conv_bias))
    pooled = frames // POOL
    message = 2 * width + width + model + channels
    assert pooled <= HALO

    def head(n):
        return pl.BlockSpec((HALO, n), lambda i: (0, 0))

    def tail(n):
        return pl.BlockSpec((HALO, n), lambda i: (frames // HALO - 1, 0))

    to_left, to_right, own = pl.pallas_call(
        pack_kernel,
        out_shape=(
            jax.ShapeDtypeStruct((HALO, message), BF16),
            jax.ShapeDtypeStruct((HALO, message), BF16),
            jax.ShapeDtypeStruct((pooled, 2 * width), BF16),
        ),
        grid=(1,),
        in_specs=[VMEM, VMEM]
        + [spec(n) for n in (width, model, channels) for spec in (head, tail)],
        out_specs=(VMEM,) * 3,
    )(keys, values, query, query, resid, resid, cotangent, cotangent)

    from_left, from_right, kvs = exchange("ctx", ctx, own, to_left, to_right)

    rows = frames + 2 * HALO
    span = frames + HALO
    shape = jax.ShapeDtypeStruct
    conv_act, x_norm, inv_norm, left, sig, d_conv, sums = pl.pallas_call(
        functools.partial(main_kernel, ctx, len(kvs)),
        out_shape=(
            shape((frames, channels), BF16),
            shape((frames, model), F32),
            shape((frames, LANES), F32),
            shape((frames, channels), F32),
            shape((frames, channels), F32),
            shape((channels // LANES, span, LANES), F32),
            shape((n_taps + 2, channels), F32),
        ),
        in_specs=[VMEM] * (11 + len(kvs)),
        out_specs=(VMEM,) * 7,
        scratch_shapes=[
            pltpu.VMEM((rows, width), BF16),
            pltpu.VMEM((pooled * ctx, 2 * width), BF16),
            pltpu.VMEM((rows, width), BF16),
            pltpu.VMEM((rows, model), F32),
            pltpu.VMEM((rows, model), BF16),
            pltpu.VMEM((channels // LANES, rows, LANES), F32),
            pltpu.VMEM((span, channels), F32),
            pltpu.VMEM((rows, 2 * channels), F32),
            pltpu.VMEM((n_taps * 8, LANES), F32),
        ],
        compiler_params=pltpu.CompilerParams(vmem_limit_bytes=40 * 2**20),
    )(
        query,
        resid,
        cotangent,
        w_out,
        norm_gain,
        w_in,
        kernel,
        conv_gain,
        conv_bias,
        from_left,
        from_right,
        *kvs,
    )

    d_hidden = pl.pallas_call(
        back_kernel,
        out_shape=shape((frames, model), BF16),
        in_specs=[VMEM] * 8,
        out_specs=VMEM,
        scratch_shapes=[
            pltpu.VMEM((frames, 2 * channels), BF16),
            pltpu.VMEM((frames, model), F32),
        ],
        compiler_params=pltpu.CompilerParams(vmem_limit_bytes=24 * 2**20),
    )(kernel, norm_gain, w_in, x_norm, inv_norm, left, sig, d_conv)

    factor = 1.0 / math.sqrt(frames * ctx * dp)
    total = total_of(sums, ctx, dp) * factor
    return (conv_act[None], d_hidden[None], total[:n_taps], total[n_taps], total[n_taps + 1])


def solution(mesh):
    split = P(("groups", "dp"), "ctx", None)
    return jax.shard_map(
        per_device,
        mesh=mesh,
        in_specs=(split,) * 4 + (P(),) * 6 + (split,),
        out_specs=(split, split, P("groups", None), P("groups"), P("groups")),
        check_vma=False,
    )
```

time: 170 us -> 47.3 us (0.28)
  waiting for transfers between devices: 86.7 us -> 15 us
  blocking collectives: 28.6 us -> 0 us
  other arithmetic: 15.3 us -> 0.06 us
  between operations: 14.4 us -> 0.67 us
  Pallas kernels: 0 us -> 8.49 us
  matrix products: 4.25 us -> 0 us
  starting transfers between devices: 9.1 us -> 12.2 us
    psum x1 -> x0, waiting for transfers between devices: 82.4 us -> none  [per_device(): lax.psum((local_kernel, local_gain, local_bias), ('ctx', 'dp'))]
    all_gather x2 -> x0, blocking collectives: 28.6 us -> none  [the longest x1 15.1 us: per_device(): lax.all_gather(pooled_keys, 'ctx', axis=1, tiled=True)]
    ppermute x4 -> x8, waiting for transfers between devices: 4.26 us -> 15 us  [the longest x1 11.1 us: exchange(): far = lax.ppermute(own, axis, [(i, (i + 2) % 4) for i in range(4)])]
    pallas_call x0 -> x3, Pallas kernels: none -> 8.49 us  [the longest x1 4.2 us: per_device(): pl.pallas_call(functools.partial(main_kernel, ctx, len(kvs)), out_shape=(...]
    reduce_sum x11 -> x0, other arithmetic: 7.51 us -> none  [the longest x4 3.8 us: per_device(): jnp.sum(d_conv.astype(jnp.float32) * glu_padded[:, tap_index:tap_index +...]
    unnamed x23 -> x20, local copies, waits for them, and re-layouts: 2.06 us -> 9.3 us
    another operation x1 -> x0, local copies, waits for them, and re-layouts: 5.38 us -> none  [per_device(): local_kernel = jnp.stack(tap_terms)]
    dot_general x5 -> x0, matrix products: 4.25 us -> none  [the longest x1 1.64 us: per_device(): jnp.dot(attended, w_out, preferred_element_type=jnp.float32)]
  transfers between devices with their start and end apart: 5 -> 8, of which waited for: 2 -> 4; matrix products, arithmetic and copies ran while one was open for 8% -> 0% of each run, Pallas kernels for 0% -> 5%
where the time goes in v1:
time: 47.3 us; the launch traced here: 46.9 us
  waiting for transfers between devices  15 us (32%)
  starting transfers between devices  12.2 us (26%)
  local copies, waits for them, and re-layouts  10.5 us (22%)
  Pallas kernels  8.49 us (18%)
  between operations  0.67 us (1%)
    ppermute x1, waiting for transfers between devices, exchange(): far = lax.ppermute(own, axis, [(i, (i + 2) % 4) for i in range(4)])  11.1 us
    unnamed x20, local copies, waits for them, and re-layouts  9.3 us
    ppermute x3, starting transfers between devices, total_of(): one, two, three = (lax.ppermute(sums, 'ctx', flip(k)) for k in (1, 2, 3))  4.45 us
    pallas_call x1, Pallas kernels, per_device(): pl.pallas_call(functools.partial(main_kernel, ctx, len(kvs)), out_shape=(...  4.2 us
    ppermute x1, starting transfers between devices, exchange(): lax.ppermute(to_right, axis, [(i, (i + 1) % 4) for i in range(4)])  3.02 us
    ppermute x1, waiting for transfers between devices, total_of(): lax.ppermute(sums, 'dp', flip(2)).astype(F32)  2.51 us
    pallas_call x1, Pallas kernels, per_device(): pl.pallas_call(back_kernel, out_shape=shape((frames, model), BF16), in_sp...  2.31 us
    ppermute x1, starting transfers between devices, exchange(): lax.ppermute(to_left, axis, [((i + 1) % 4, i) for i in range(4)])  2.03 us
  transfers between devices with their start and end apart: 8, of which 4 were waited for; matrix products, arithmetic and copies ran while one was open for 0% of the time, Pallas kernels for 5%

profile of v1, /device:TPU:0, one launch (start us, length us, event | category | flops | bytes accessed | tf_op | source)
XLA Modules:
  0.0 46.9 jit_solution(13978404191228349679)
XLA Ops:
  0.6 2.0 %shard_map.146 = (bf16[32,3072]{1,0:T(8,128)(2,1)}, bf16[32,3072]{1,0:T(8,128)(2,1)}, bf16[32,1024]{1,0:T(8,128)(2,1)}) custom-call(bf16[128,512]{1,0:T(8,128)(2,1)} %bitcast.26, bf16[128,512]{1,0:T(8,128)(2,1)} %bitcast.27, bf16[128,512]{1,0:T(8,128)(2,1)} %bitcast.15, bf16[128,512]{1,0:T(8,128)(2,1)} %bitcast.16, bf16[128,1024]{1,0:T(8,128)(2,1)} %bitcast.12, ...), custom_call_target="tpu_custom_call" | custom-call | tf_op jit(solution)/shard_map/pallas_call | solution.py:292
  2.6 3.0 %collective-permute-start = (bf16[32,3072]{1,0:T(8,128)(2,1)}, bf16[32,3072]{1,0:T(8,128)(2,1)S(1)}, u32[]{:S(2)}, u32[]{:S(2)}) collective-permute-start(bf16[32,3072]{1,0:T(8,128)(2,1)} %get-tuple-element.15), channel_id=1, source_target_pairs={{0,4},{4,8},{8,12},{12,0},{1,5},{5,9},{9,13},{13,1},{2,6},{6,10},{... | collective-permute-start | bytes 589832 | tf_op jit(solution)/shard_map/ppermute | solution.py:249
  5.6 2.0 %collective-permute-start.1 = (bf16[32,3072]{1,0:T(8,128)(2,1)}, bf16[32,3072]{1,0:T(8,128)(2,1)S(1)}, u32[]{:S(2)}, u32[]{:S(2)}) collective-permute-start(bf16[32,3072]{1,0:T(8,128)(2,1)} %get-tuple-element.16), channel_id=1, source_target_pairs={{4,0},{8,4},{12,8},{0,12},{5,1},{9,5},{13,9},{1,13},{6,2},{10,6},{... | collective-permute-start | bytes 589832 | tf_op jit(solution)/shard_map/ppermute | solution.py:250
  7.7 1.0 %collective-permute-start.2 = (bf16[32,1024]{1,0:T(8,128)(2,1)}, bf16[32,1024]{1,0:T(8,128)(2,1)S(1)}, u32[]{:S(2)}, u32[]{:S(2)}) collective-permute-start(bf16[32,1024]{1,0:T(8,128)(2,1)} %get-tuple-element.17.refs_11_), channel_id=1, source_target_pairs={{0,8},{4,12},{8,0},{12,4},{1,9},{5,13},{9,1},{13,5},{2,10},{6,14},... | collective-permute-start | bytes 196616 | tf_op jit(solution)/shard_map/ppermute | solution.py:251
  8.7 11.1 %collective-permute-done.2.refs_14_ = bf16[32,1024]{1,0:T(8,128)(2,1)S(1)} collective-permute-done((bf16[32,1024]{1,0:T(8,128)(2,1)}, bf16[32,1024]{1,0:T(8,128)(2,1)S(1)}, u32[]{:S(2)}, u32[]{:S(2)}) %collective-permute-start.2) | collective-permute-done | bytes 65568 | tf_op jit(solution)/shard_map/ppermute | solution.py:251
  19.8 0.0 collective-permute-done.refs_9_.refs_12_
  19.8 0.0 collective-permute-done.1.refs_10_.refs_13_
  19.8 0.0 copy-start
  19.8 1.6 %copy-done = bf16[1024,1024]{1,0:T(8,128)(2,1)S(1)} copy-done((bf16[1024,1024]{1,0:T(8,128)(2,1)S(1)}, bf16[1024,1024]{1,0:T(8,128)(2,1)}, u32[]{:S(2)}) %copy-start) | copy-done | bytes 2097176
  21.4 0.0 copy-start.1
  21.4 0.9 %copy-done.1 = bf16[1,128,1024]{2,1,0:T(8,128)(2,1)S(1)} copy-done((bf16[1,128,1024]{2,1,0:T(8,128)(2,1)S(1)}, bf16[1,128,1024]{2,1,0:T(8,128)(2,1)}, u32[]{:S(2)}) %copy-start.1) | copy-done | bytes 262168
  22.3 0.0 copy-start.2
  22.3 0.9 %copy-done.2 = bf16[1,128,512]{2,1,0:T(8,128)(2,1)S(1)} copy-done((bf16[1,128,512]{2,1,0:T(8,128)(2,1)S(1)}, bf16[1,128,512]{2,1,0:T(8,128)(2,1)}, u32[]{:S(2)}) %copy-start.2) | copy-done | bytes 131096
  23.2 0.0 copy-start.3
  23.2 0.9 %copy-done.3 = bf16[1,128,512]{2,1,0:T(8,128)(2,1)S(1)} copy-done((bf16[1,128,512]{2,1,0:T(8,128)(2,1)S(1)}, bf16[1,128,512]{2,1,0:T(8,128)(2,1)}, u32[]{:S(2)}) %copy-start.3) | copy-done | bytes 131096
  24.1 0.0 copy-start.4
  24.1 1.2 %copy-done.4 = bf16[512,1024]{1,0:T(8,128)(2,1)S(1)} copy-done((bf16[512,1024]{1,0:T(8,128)(2,1)S(1)}, bf16[512,1024]{1,0:T(8,128)(2,1)}, u32[]{:S(2)}) %copy-start.4) | copy-done | bytes 1048600
  25.4 0.0 copy-start.5
  25.4 0.8 %copy-done.5 = f32[31,512]{1,0:T(8,128)S(1)} copy-done((f32[31,512]{1,0:T(8,128)S(1)}, f32[31,512]{1,0:T(8,128)}, u32[]{:S(2)}) %copy-start.5) | copy-done | bytes 63512
  26.2 0.0 copy-start.6
  26.2 0.8 %copy-done.6 = bf16[32,1024]{1,0:T(8,128)(2,1)S(1)} copy-done((bf16[32,1024]{1,0:T(8,128)(2,1)S(1)}, bf16[32,1024]{1,0:T(8,128)(2,1)}, u32[]{:S(2)}) %copy-start.6) | copy-done | bytes 65560
  27.1 0.0 copy-start.7
  27.1 0.7 %copy-done.7 = f32[1024]{0:T(1024)S(1)} copy-done((f32[1024]{0:T(1024)S(1)}, f32[1024]{0:T(1024)}, u32[]{:S(2)}) %copy-start.7) | copy-done | bytes 4120
  27.7 0.0 copy-start.8
  27.7 0.7 %copy-done.8 = f32[512]{0:T(512)S(1)} copy-done((f32[512]{0:T(512)S(1)}, f32[512]{0:T(512)}, u32[]{:S(2)}) %copy-start.8) | copy-done | bytes 2072
  28.4 0.0 copy-start.9
  28.4 0.7 %copy-done.9 = f32[512]{0:T(512)S(1)} copy-done((f32[512]{0:T(512)S(1)}, f32[512]{0:T(512)}, u32[]{:S(2)}) %copy-start.9) | copy-done | bytes 2072
  29.1 4.2 %shard_map.147 = (bf16[128,512]{1,0:T(8,128)(2,1)}, f32[128,1024]{1,0:T(8,128)S(1)}, f32[128,128]{1,0:T(8,128)S(1)}, f32[128,512]{1,0:T(8,128)S(1)}, f32[128,512...) custom-call(bf16[128,512]{1,0:T(8,128)(2,1)S(1)} %bitcast.17, bf16[128,1024]{1,0:T(8,128)(2,1)S(1)} %bitcast.14, ...), custom_call_target="tpu_custom_call" | custom-call | tf_op jit(solution)/shard_map/pallas_call | solution.py:310
  33.3 0.1 collective-permute-start.3
  33.4 1.3 %collective-permute-done.3 = f32[33,512]{1,0:T(8,128)S(1)} collective-permute-done((f32[33,512]{1,0:T(8,128)S(1)}, f32[33,512]{1,0:T(8,128)S(1)}, u32[]{:S(2)}, u32[]{:S(2)}) %collective-permute-start.3) | collective-permute-done | bytes 67616 | tf_op jit(solution)/shard_map/ppermute | solution.py:262
  34.7 1.6 %collective-permute-start.4 = (bf16[33,512]{1,0:T(8,128)(2,1)S(1)}, bf16[33,512]{1,0:T(8,128)(2,1)S(1)}, u32[]{:S(2)}, u32[]{:S(2)}) collective-permute-start(bf16[33,512]{1,0:T(8,128)(2,1)S(1)} %add_convert_fusion.1), channel_id=1, source_target_pairs={{0,2},{1,3},{2,0},{3,1},{4,6},{5,7},{6,4},{7,5},{8,10},{9,11},{10,... | collective-permute-start | bytes 101384 | tf_op jit(solution)/shard_map/ppermute | solution.py:264
  36.2 2.5 %collective-permute-done.4 = bf16[33,512]{1,0:T(8,128)(2,1)S(1)} collective-permute-done((bf16[33,512]{1,0:T(8,128)(2,1)S(1)}, bf16[33,512]{1,0:T(8,128)(2,1)S(1)}, u32[]{:S(2)}, u32[]{:S(2)}) %collective-permute-start.4) | collective-permute-done | bytes 33824 | tf_op jit(solution)/shard_map/ppermute | solution.py:264
  38.8 1.7 %collective-permute-start.7 = (bf16[33,512]{1,0:T(8,128)(2,1)S(1)}, bf16[33,512]{1,0:T(8,128)(2,1)S(1)}, u32[]{:S(2)}, u32[]{:S(2)}) collective-permute-start(bf16[33,512]{1,0:T(8,128)(2,1)S(1)} %add_convert_fusion), channel_id=1, source_target_pairs={{0,12},{4,8},{8,4},{12,0},{1,13},{5,9},{9,5},{13,1},{2,14},{6,10},... | collective-permute-start | bytes 101384 | tf_op jit(solution)/shard_map/ppermute | solution.py:265
  40.5 0.0 collective-permute-start.6
  40.5 2.7 %collective-permute-start.5 = (bf16[33,512]{1,0:T(8,128)(2,1)S(1)}, bf16[33,512]{1,0:T(8,128)(2,1)S(1)}, u32[]{:S(2)}, u32[]{:S(2)}) collective-permute-start(bf16[33,512]{1,0:T(8,128)(2,1)S(1)} %add_convert_fusion), channel_id=1, source_target_pairs={{0,4},{4,0},{8,12},{12,8},{1,5},{5,1},{9,13},{13,9},{2,6},{6,2},{1... | collective-permute-start | bytes 101384 | tf_op jit(solution)/shard_map/ppermute | solution.py:265
  43.2 2.3 %shard_map.148 = bf16[128,1024]{1,0:T(8,128)(2,1)} custom-call(f32[31,512]{1,0:T(8,128)S(1)} %copy-done.5, f32[1,1024]{1,0:T(1,128)S(1)} %bitcast.22, bf16[1024,1024]{1,0:T(8,128)(2,1)S(1)} %copy-done, f32[128,1024]{1,0:T(8,128)S(1)} %get-tuple-element.19.x_norm, f32[128,128]{1,0:T(8,128)S(1)} %get-tuple-element.20.inv_norm, ...), custom_call_target="tpu_custom_call" | custom-call | tf_op jit(solution)/shard_map/pallas_call | solution.py:350
  45.5 0.0 collective-permute-done.7
  45.5 0.1 collective-permute-done.6
  45.6 0.0 collective-permute-done.5
  45.7 0.6 %fusion = (f32[1,512]{1,0:T(1,128)}, f32[1,512]{1,0:T(1,128)}) fusion(f32[33,512]{1,0:T(8,128)S(1)} %add_multiply_fusion), kind=kLoop, calls=%fused_computation.3 | loop fusion | bytes 8192 | tf_op jit(solution)/shard_map/slice | solution.py:364
  46.3 0.6 %slice.12 = f32[31,512]{1,0:T(8,128)} slice(f32[33,512]{1,0:T(8,128)S(1)} %add_multiply_fusion), slice={[0:31], [0:512]} | slice | bytes 126976 | tf_op jit(solution)/shard_map/slice | solution.py:364
  (3 shorter events, 0.1 us)
Async XLA Ops:
  2.6 17.2 %collective-permute-start = (bf16[32,3072]{1,0:T(8,128)(2,1)}, bf16[32,3072]{1,0:T(8,128)(2,1)S(1)}, u32[]{:S(2)}, u32[]{:S(2)}) collective-permute-start(bf16[32,3072]{1,0:T(8,128)(2,1)} %get-tuple-element.15), channel_id=1, source_target_pairs={{0,4},{4,8},{8,12},{12,0},{1,5},{5,9},{9,13},{13,1},{2,6},{6,10},{... | collective-permute-start | bytes 589832 | tf_op jit(solution)/shard_map/ppermute | solution.py:249
  5.6 14.2 %collective-permute-start.1 = (bf16[32,3072]{1,0:T(8,128)(2,1)}, bf16[32,3072]{1,0:T(8,128)(2,1)S(1)}, u32[]{:S(2)}, u32[]{:S(2)}) collective-permute-start(bf16[32,3072]{1,0:T(8,128)(2,1)} %get-tuple-element.16), channel_id=1, source_target_pairs={{4,0},{8,4},{12,8},{0,12},{5,1},{9,5},{13,9},{1,13},{6,2},{10,6},{... | collective-permute-start | bytes 589832 | tf_op jit(solution)/shard_map/ppermute | solution.py:250
  7.7 12.1 %collective-permute-start.2 = (bf16[32,1024]{1,0:T(8,128)(2,1)}, bf16[32,1024]{1,0:T(8,128)(2,1)S(1)}, u32[]{:S(2)}, u32[]{:S(2)}) collective-permute-start(bf16[32,1024]{1,0:T(8,128)(2,1)} %get-tuple-element.17.refs_11_), channel_id=1, source_target_pairs={{0,8},{4,12},{8,0},{12,4},{1,9},{5,13},{9,1},{13,5},{2,10},{6,14},... | collective-permute-start | bytes 196616 | tf_op jit(solution)/shard_map/ppermute | solution.py:251
  19.8 1.6 %copy-start = (bf16[1024,1024]{1,0:T(8,128)(2,1)S(1)}, bf16[1024,1024]{1,0:T(8,128)(2,1)}, u32[]{:S(2)}) copy-start(bf16[1024,1024]{1,0:T(8,128)(2,1)} %w_in.1) | copy-start | bytes 6291460
  21.4 0.9 %copy-start.1 = (bf16[1,128,1024]{2,1,0:T(8,128)(2,1)S(1)}, bf16[1,128,1024]{2,1,0:T(8,128)(2,1)}, u32[]{:S(2)}) copy-start(bf16[1,128,1024]{2,1,0:T(8,128)(2,1)} %param.11) | copy-start | bytes 786436
  22.3 0.9 %copy-start.2 = (bf16[1,128,512]{2,1,0:T(8,128)(2,1)S(1)}, bf16[1,128,512]{2,1,0:T(8,128)(2,1)}, u32[]{:S(2)}) copy-start(bf16[1,128,512]{2,1,0:T(8,128)(2,1)} %param.12) | copy-start | bytes 393220
  23.2 0.9 %copy-start.3 = (bf16[1,128,512]{2,1,0:T(8,128)(2,1)S(1)}, bf16[1,128,512]{2,1,0:T(8,128)(2,1)}, u32[]{:S(2)}) copy-start(bf16[1,128,512]{2,1,0:T(8,128)(2,1)} %param.21) | copy-start | bytes 393220
  24.1 1.2 %copy-start.4 = (bf16[512,1024]{1,0:T(8,128)(2,1)S(1)}, bf16[512,1024]{1,0:T(8,128)(2,1)}, u32[]{:S(2)}) copy-start(bf16[512,1024]{1,0:T(8,128)(2,1)} %refs_3_.1) | copy-start | bytes 3145732
  25.4 0.8 %copy-start.5 = (f32[31,512]{1,0:T(8,128)S(1)}, f32[31,512]{1,0:T(8,128)}, u32[]{:S(2)}) copy-start(f32[31,512]{1,0:T(8,128)} %kernel.1) | copy-start | bytes 190468
  26.2 0.8 %copy-start.6 = (bf16[32,1024]{1,0:T(8,128)(2,1)S(1)}, bf16[32,1024]{1,0:T(8,128)(2,1)}, u32[]{:S(2)}) copy-start(bf16[32,1024]{1,0:T(8,128)(2,1)} %get-tuple-element.17.refs_11_) | copy-start | bytes 196612
  27.1 0.7 %copy-start.7 = (f32[1024]{0:T(1024)S(1)}, f32[1024]{0:T(1024)}, u32[]{:S(2)}) copy-start(f32[1024]{0:T(1024)} %param.16) | copy-start | bytes 12292
  27.7 0.7 %copy-start.8 = (f32[512]{0:T(512)S(1)}, f32[512]{0:T(512)}, u32[]{:S(2)}) copy-start(f32[512]{0:T(512)} %param.19) | copy-start | bytes 6148
  28.4 0.7 %copy-start.9 = (f32[512]{0:T(512)S(1)}, f32[512]{0:T(512)}, u32[]{:S(2)}) copy-start(f32[512]{0:T(512)} %param.20) | copy-start | bytes 6148
  33.3 1.3 %collective-permute-start.3 = (f32[33,512]{1,0:T(8,128)S(1)}, f32[33,512]{1,0:T(8,128)S(1)}, u32[]{:S(2)}, u32[]{:S(2)}) collective-permute-start(f32[33,512]{1,0:T(8,128)S(1)} %get-tuple-element.24), channel_id=1, source_target_pairs={{0,1},{1,0},{2,3},{3,2},{4,5},{5,4},{6,7},{7,6},{8,9},{9,8},{10,11... | collective-permute-start | bytes 202760 | tf_op jit(solution)/shard_map/ppermute | solution.py:262
  34.7 4.1 %collective-permute-start.4 = (bf16[33,512]{1,0:T(8,128)(2,1)S(1)}, bf16[33,512]{1,0:T(8,128)(2,1)S(1)}, u32[]{:S(2)}, u32[]{:S(2)}) collective-permute-start(bf16[33,512]{1,0:T(8,128)(2,1)S(1)} %add_convert_fusion.1), channel_id=1, source_target_pairs={{0,2},{1,3},{2,0},{3,1},{4,6},{5,7},{6,4},{7,5},{8,10},{9,11},{10,... | collective-permute-start | bytes 101384 | tf_op jit(solution)/shard_map/ppermute | solution.py:264
  38.8 6.8 %collective-permute-start.7 = (bf16[33,512]{1,0:T(8,128)(2,1)S(1)}, bf16[33,512]{1,0:T(8,128)(2,1)S(1)}, u32[]{:S(2)}, u32[]{:S(2)}) collective-permute-start(bf16[33,512]{1,0:T(8,128)(2,1)S(1)} %add_convert_fusion), channel_id=1, source_target_pairs={{0,12},{4,8},{8,4},{12,0},{1,13},{5,9},{9,5},{13,1},{2,14},{6,10},... | collective-permute-start | bytes 101384 | tf_op jit(solution)/shard_map/ppermute | solution.py:265
  40.5 5.2 %collective-permute-start.6 = (bf16[33,512]{1,0:T(8,128)(2,1)S(1)}, bf16[33,512]{1,0:T(8,128)(2,1)S(1)}, u32[]{:S(2)}, u32[]{:S(2)}) collective-permute-start(bf16[33,512]{1,0:T(8,128)(2,1)S(1)} %add_convert_fusion), channel_id=1, source_target_pairs={{0,8},{4,12},{8,0},{12,4},{1,9},{5,13},{9,1},{13,5},{2,10},{6,14},... | collective-permute-start | bytes 101384 | tf_op jit(solution)/shard_map/ppermute | solution.py:265
  40.5 5.2 %collective-permute-start.5 = (bf16[33,512]{1,0:T(8,128)(2,1)S(1)}, bf16[33,512]{1,0:T(8,128)(2,1)S(1)}, u32[]{:S(2)}, u32[]{:S(2)}) collective-permute-start(bf16[33,512]{1,0:T(8,128)(2,1)S(1)} %add_convert_fusion), channel_id=1, source_target_pairs={{0,4},{4,0},{8,12},{12,8},{1,5},{5,1},{9,13},{13,9},{2,6},{6,2},{1... | collective-permute-start | bytes 101384 | tf_op jit(solution)/shard_map/ppermute | solution.py:265

commit v2 on v1

v2 whole, which is shorter than its diff:
```python
import functools
import math

import jax
import jax.numpy as jnp
from jax import lax
from jax.experimental import pallas as pl
from jax.experimental.pallas import tpu as pltpu
from jax.sharding import PartitionSpec as P

HEAD_DIM = 64
POOL = 4
EPSILON = 1e-05

LANES = 128
HALO = 16
F32 = jnp.float32
BF16 = jnp.bfloat16

VMEM = pl.BlockSpec(memory_space=pltpu.VMEM)
HBM = pl.BlockSpec(memory_space=pltpu.HBM)
shape = jax.ShapeDtypeStruct


def dot(a, b):
    return lax.dot_general(a, b, (((1,), (0,)), ((), ())), preferred_element_type=F32)


def dot_t(a, b):
    return lax.dot_general(a, b, (((1,), (1,)), ((), ())), preferred_element_type=F32)


def row_mean(x):
    return jnp.sum(x, axis=-1, keepdims=True) * (1.0 / x.shape[-1])


def in_hbm(*arrays):
    return [pltpu.with_memory_space_constraint(x, pltpu.HBM) for x in arrays]


def swapped(pairwise):
    return lax.rem(lax.axis_index("ctx"), 2) == 1 if pairwise else False


def pack_kernel(pairwise, keys, values, query, resid, own, to_a, to_b, kv, sem, kv_sem):
    frames, width = keys.shape
    model = resid.shape[1]
    pooled = frames // POOL
    swap = swapped(pairwise)
    loads = [
        pltpu.make_async_copy(source, kv.at[place], kv_sem.at[place])
        for place, source in enumerate((keys, values))
    ]
    for load in loads:
        load.start()
    edges = []
    for target, near in ((to_a, True), (to_b, False)):
        start = jnp.where(swap, 0 if near else frames - HALO, frames - HALO if near else 0)
        start = pl.multiple_of(start.astype(jnp.int32), HALO)
        at = 2 * pooled
        for source, column in [(query, 0)] + [(resid, c) for c in range(0, model, width)]:
            edges.append(
                pltpu.make_async_copy(
                    source.at[pl.ds(start, HALO), pl.ds(column, width)],
                    target.at[pl.ds(at, HALO), :],
                    sem.at[len(edges)],
                )
            )
            edges[-1].start()
            at += HALO
    row = lax.broadcasted_iota(jnp.int32, (pooled, frames), 0)
    col = lax.broadcasted_iota(jnp.int32, (pooled, frames), 1)
    mean = jnp.where(col // POOL == row, 1.0 / POOL, 0.0).astype(BF16)
    for place, load in enumerate(loads):
        load.wait()
        block = dot(mean, kv[place]).astype(BF16)
        rows = pl.ds(place * pooled, pooled)
        own[rows, :] = block
        to_a[rows, :] = block
        to_b[rows, :] = block
    for edge in edges:
        edge.wait()


def fetch_kernel(count, after, *refs):
    sources, targets, sem = refs[:count], refs[count : 2 * count], refs[2 * count]
    copies = [
        pltpu.make_async_copy(a, b, sem.at[i]) for i, (a, b) in enumerate(zip(sources, targets))
    ]
    for copy in copies:
        copy.start()
    for copy in copies:
        copy.wait()


def main_kernel(pairwise, count, kv_places, *refs):
    (query, resid, cotangent, w_out, norm_gain, w_in, kernel, conv_gain, conv_bias) = refs[:9]
    from_a, from_b = refs[9:11]
    n_kv = len(kv_places)
    kvs = refs[11 : 11 + n_kv]
    (conv_act, x_norm, inv_norm, left_out, sig_out, d_conv) = refs[11 + n_kv : 17 + n_kv]
    to_a, to_b, sums = refs[17 + n_kv : 20 + n_kv]
    (q_all, r_edge, k_all, v_all, att, hid, normed, gated, conv, glu, taps, act_out, pack, sem) = (
        refs[20 + n_kv :]
    )
    frames, width = query.shape
    model = resid.shape[1]
    channels = w_in.shape[1] // 2
    rows = frames + 2 * HALO
    n_taps = kernel.shape[0]
    rim = (n_taps - 1) // 2
    pooled = frames // POOL
    me = lax.axis_index("ctx")
    first = me == 0
    last = me == count - 1
    swap = swapped(pairwise)
    main = pl.ds(HALO, frames)

    at = 0
    for ref, (k_row, v_row, keep) in zip(kvs, kv_places):
        if k_row is not None:
            k_all[pl.ds(at, keep), :] = ref[pl.ds(k_row, keep), :]
        if v_row is not None:
            v_all[pl.ds(at, keep), :] = ref[pl.ds(v_row, keep), :]
            at += keep
    keylen = at
    q_all[main, :] = query[...]
    base = 2 * pooled
    for left_side in (True, False):
        edge_rows = pl.ds(0 if left_side else HALO + frames, HALO)
        r_rows = pl.ds(0 if left_side else HALO, HALO)
        near, other = (from_b, from_a) if left_side else (from_a, from_b)

        def pick(start):
            rows_in = pl.ds(start, HALO)
            return jnp.where(swap, other[rows_in, :], near[rows_in, :])

        q_all[edge_rows, :] = pick(base)
        for piece in range(model // width):
            r_edge[r_rows, pl.ds(piece * width, width)] = pick(base + HALO * (1 + piece))

    lane = lax.broadcasted_iota(jnp.int32, (keylen, LANES), 1)
    low = lane < HEAD_DIM
    zero = jnp.zeros((keylen, LANES), BF16)
    ones_low = jnp.where(low, 1.0, 0.0).astype(BF16)
    ones_high = jnp.where(low, 0.0, 1.0).astype(BF16)
    scale = 1.0 / math.sqrt(HEAD_DIM)
    for pair in range(width // LANES):
        cols = pl.ds(pair * LANES, LANES)
        k_pair = k_all[:, cols]
        v_pair = v_all[:, cols]
        q_pair = q_all[:, cols]
        weighted = None
        for keep_low in (True, False):
            k_head = jnp.where(low, k_pair, zero) if keep_low else jnp.where(low, zero, k_pair)
            v_head = jnp.where(low, v_pair, zero) if keep_low else jnp.where(low, zero, v_pair)
            ones = ones_low if keep_low else ones_high
            scores = dot_t(q_pair, k_head)
            top = jnp.max(scores, axis=-1, keepdims=True)
            probs = jnp.exp((scores - top) * scale).astype(BF16)
            part = dot(probs, jnp.concatenate([v_head, ones], axis=1))
            weighted = part if weighted is None else weighted + part
        att[:, cols] = (weighted[:, :LANES] / weighted[:, LANES:]).astype(BF16)

    step = 256
    for n in range(model // step):
        cols = pl.ds(n * step, step)
        out = dot(att[...], w_out[:, cols])
        for rows_in, res in (
            (slice(0, HALO), r_edge[0:HALO, cols]),
            (slice(HALO, HALO + frames), resid[:, cols]),
            (slice(HALO + frames, rows), r_edge[HALO:, cols]),
        ):
            hid[rows_in, cols] = (res.astype(F32) + out[rows_in]).astype(BF16).astype(F32)

    gain = norm_gain[...]
    for r in range(0, rows, 32):
        x = hid[r : r + 32, :]
        x = x - row_mean(x)
        inv = lax.rsqrt(row_mean(x * x) + EPSILON)
        x = x * inv
        normed[r : r + 32, :] = (x * gain).astype(BF16)
        x_norm[r : r + 32, :] = x
        inv_norm[r : r + 32, :] = jnp.broadcast_to(inv, (32, LANES))

    for n in range(2 * channels // step):
        cols = pl.ds(n * step, step)
        glu[:, cols] = dot(normed[...], w_in[:, cols])
    for r in range(0, rows, 16):
        left = glu[r : r + 16, 0:channels]
        sig = jax.nn.sigmoid(glu[r : r + 16, channels:])
        out = (left * sig).astype(BF16).astype(F32)
        if r < HALO:
            out = jnp.where(first, 0.0, out)
        elif r >= HALO + frames:
            out = jnp.where(last, 0.0, out)
        else:
            left_out[r - HALO : r - HALO + 16, :] = left
            sig_out[r - HALO : r - HALO + 16, :] = sig
        for c in range(channels // LANES):
            gated[c, r : r + 16, :] = out[:, c * LANES : (c + 1) * LANES]

    for c in range(channels // LANES):
        cols = slice(c * LANES, (c + 1) * LANES)
        acc = jnp.zeros((frames, LANES), F32)
        for t in range(n_taps):
            acc = acc + kernel[t : t + 1, cols] * gated[c, pl.ds(HALO + t - rim, frames), :]
        conv[:, cols] = acc

    gain = conv_gain[...]
    bias = conv_bias[...]
    sum_gain = jnp.zeros((8, channels), F32)
    sum_bias = jnp.zeros((8, channels), F32)
    for r in range(0, frames, 16):
        z = conv[r : r + 16, :]
        z = z - row_mean(z)
        inv = lax.rsqrt(row_mean(z * z) + EPSILON)
        z = z * inv
        act_in = z * gain + bias
        sig = jax.nn.sigmoid(act_in)
        act = act_in * sig
        act_out[r : r + 16, :] = act.astype(BF16)
        d_act = cotangent[r : r + 16, :].astype(F32) * (sig + act * (1.0 - sig))
        d_gain = d_act * z
        sum_gain = sum_gain + d_gain[:8] + d_gain[8:]
        sum_bias = sum_bias + d_act[:8] + d_act[8:]
        g = d_act * gain
        d = (inv * (g - row_mean(g) - z * row_mean(g * z))).astype(BF16).astype(F32)
        for c in range(channels // LANES):
            d_conv[c, r : r + 16, :] = d[:, c * LANES : (c + 1) * LANES]
    write = pltpu.make_async_copy(act_out, conv_act, sem)
    write.start()
    pack[n_taps : n_taps + 1, :] = jnp.sum(sum_gain, axis=0, keepdims=True)
    pack[n_taps + 1 : n_taps + 2, :] = jnp.sum(sum_bias, axis=0, keepdims=True)

    for c in range(channels // LANES):
        cols = slice(c * LANES, (c + 1) * LANES)
        accs = [jnp.zeros((8, LANES), F32) for _ in range(n_taps)]
        for r in range(0, frames, 8):
            d = d_conv[c, r : r + 8, :]
            for t in range(n_taps):
                accs[t] = accs[t] + d * gated[c, pl.ds(HALO + r + t - rim, 8), :]
        for t in range(n_taps):
            taps[t * 8 : t * 8 + 8, :] = accs[t]
        total = taps[pl.ds(0, n_taps, stride=8), :]
        for s in range(1, 8):
            total = total + taps[pl.ds(s, n_taps, stride=8), :]
        pack[0:n_taps, cols] = total

    used = n_taps + 2
    if pairwise:
        sums[...] = pack[0:used, :].astype(BF16)
    else:
        sums[...] = pack[0:used, :]
    for target, near in ((to_a, True), (to_b, False)):
        for c in range(channels // LANES):
            tail, head = d_conv[c, frames - rim :, :], d_conv[c, 0:rim, :]
            edge = jnp.where(swap, head, tail) if near else jnp.where(swap, tail, head)
            pack[used : used + rim, c * LANES : (c + 1) * LANES] = edge
        target[...] = pack[...].astype(BF16)
    write.wait()


def back_kernel(
    pairwise, count, kernel, norm_gain, w_in, x_norm, inv_norm, left, sig, d_conv, from_a, from_b,
    d_hidden, padded, edges, d_glu, d_normed,
):
    frames, channels = left.shape
    n_taps = kernel.shape[0]
    rim = (n_taps - 1) // 2
    me = lax.axis_index("ctx")
    swap = swapped(pairwise)
    used = n_taps + 2
    edges[0] = from_a[...].astype(F32)
    edges[1] = from_b[...].astype(F32)
    for c in range(channels // LANES):
        cols = slice(c * LANES, (c + 1) * LANES)
        a, b = edges[0, used : used + rim, cols], edges[1, used : used + rim, cols]
        on_left = jnp.where(me == 0, 0.0, jnp.where(swap, a, b))
        on_right = jnp.where(me == count - 1, 0.0, jnp.where(swap, b, a))
        padded[HALO - rim : HALO, cols] = on_left
        padded[HALO : HALO + frames, cols] = d_conv[c]
        padded[HALO + frames : HALO + frames + rim, cols] = on_right
        acc = jnp.zeros((frames, LANES), F32)
        for t in range(n_taps):
            acc = acc + kernel[t : t + 1, cols] * padded[pl.ds(HALO - t + rim, frames), cols]
        sg = sig[:, cols]
        d_left = acc * sg
        d_glu[:, cols] = d_left.astype(BF16)
        d_glu[:, channels + c * LANES : channels + (c + 1) * LANES] = (
            d_left * left[:, cols] * (1.0 - sg)
        ).astype(BF16)
    model = w_in.shape[0]
    step = 256
    for n in range(model // step):
        d_normed[:, pl.ds(n * step, step)] = dot_t(d_glu[...], w_in[pl.ds(n * step, step), :])
    gain = norm_gain[...]
    for r in range(0, frames, 32):
        g = d_normed[r : r + 32, :] * gain
        x = x_norm[HALO + r : HALO + r + 32, :]
        inv = inv_norm[HALO + r : HALO + r + 32, 0:1]
        out = inv * (g - row_mean(g) - x * row_mean(g * x))
        d_hidden[r : r + 32, :] = out.astype(BF16)


def total_kernel(factor, one, two, three, four, d_kernel, d_gain, d_bias):
    n_taps = d_kernel.shape[0]
    total = (one[...].astype(F32) + two[...].astype(F32)) + (
        three[...].astype(F32) + four[...].astype(F32)
    )
    total = total * factor
    d_kernel[...] = total[0:n_taps]
    d_gain[...] = total[n_taps : n_taps + 1]
    d_bias[...] = total[n_taps + 1 :]


def flips(array, axis, which):
    return [lax.ppermute(array, axis, [(i, i ^ k) for i in range(4)]) for k in which]


def to_neighbours(pairwise, count, to_a, to_b):
    if pairwise:
        return flips(to_a, "ctx", (1,)) + flips(to_b, "ctx", (3,))
    return [
        lax.ppermute(to_b, "ctx", [((i + 1) % count, i) for i in range(count)]),
        lax.ppermute(to_a, "ctx", [(i, (i + 1) % count) for i in range(count)]),
    ]


def per_device(
    resid, query, keys, values, w_out, norm_gain, w_in, kernel, conv_gain, conv_bias, cotangent
):
    frames, model = resid.shape[1:]
    width = query.shape[2]
    channels = cotangent.shape[2]
    n_taps = kernel.shape[0]
    rim = (n_taps - 1) // 2
    ctx, dp = lax.axis_size("ctx"), lax.axis_size("dp")
    pairwise = ctx == 4 and dp == 4
    resid, query, keys, values, cotangent = (
        x.reshape(x.shape[1:]) for x in (resid, query, keys, values, cotangent)
    )
    norm_gain, conv_gain, conv_bias = (x.reshape(1, -1) for x in (norm_gain, conv_gain, conv_bias))
    pooled = frames // POOL
    message = 2 * pooled + HALO * (1 + model // width)
    n_edges = 2 * (1 + model // width)

    own, to_a, to_b = pl.pallas_call(
        functools.partial(pack_kernel, pairwise),
        out_shape=(
            shape((2 * pooled, width), BF16),
            shape((message, width), BF16),
            shape((message, width), BF16),
        ),
        in_specs=[HBM] * 4,
        out_specs=(VMEM,) * 3,
        scratch_shapes=[
            pltpu.VMEM((2, frames, width), BF16),
            pltpu.SemaphoreType.DMA((n_edges,)),
            pltpu.SemaphoreType.DMA((2,)),
        ],
        compiler_params=pltpu.CompilerParams(vmem_limit_bytes=4 * 2**20),
    )(*in_hbm(keys, values, query, resid))

    from_a, from_b = to_neighbours(pairwise, ctx, to_a, to_b)
    if pairwise:
        (far,) = flips(own, "ctx", (2,))
        kvs = (own, from_a, from_b, far)
        kv_places = ((0, pooled, pooled),) * 4
    else:
        kvs = tuple(
            lax.all_gather(part, "ctx", axis=0, tiled=True) for part in (own[:pooled], own[pooled:])
        )
        kv_places = ((0, None, pooled * ctx), (None, 0, pooled * ctx))

    operands = (
        query, resid, cotangent, w_out, norm_gain, w_in, kernel, conv_gain, conv_bias,
    )
    operands = pl.pallas_call(
        functools.partial(fetch_kernel, len(operands)),
        out_shape=tuple(shape(x.shape, x.dtype) for x in operands),
        in_specs=[HBM] * (1 + len(operands)),
        out_specs=(VMEM,) * len(operands),
        scratch_shapes=[pltpu.SemaphoreType.DMA((len(operands),))],
        compiler_params=pltpu.CompilerParams(vmem_limit_bytes=8 * 2**20),
    )(own, *in_hbm(*operands))
    norm_gain, w_in, kernel = operands[4:7]

    rows = frames + 2 * HALO
    used = n_taps + 2
    conv_act, x_norm, inv_norm, left, sig, d_conv, to_a, to_b, sums = pl.pallas_call(
        functools.partial(main_kernel, pairwise, ctx, kv_places),
        out_shape=(
            shape((frames, channels), BF16),
            shape((rows, model), F32),
            shape((rows, LANES), F32),
            shape((frames, channels), F32),
            shape((frames, channels), F32),
            shape((channels // LANES, frames, LANES), F32),
            shape((used + rim, channels), BF16),
            shape((used + rim, channels), BF16),
            shape((used, channels), BF16 if pairwise else F32),
        ),
        in_specs=[VMEM] * (11 + len(kvs)),
        out_specs=(HBM,) + (VMEM,) * 8,
        scratch_shapes=[
            pltpu.VMEM((rows, width), BF16),
            pltpu.VMEM((2 * HALO, model), BF16),
            pltpu.VMEM((pooled * ctx, width), BF16),
            pltpu.VMEM((pooled * ctx, width), BF16),
            pltpu.VMEM((rows, width), BF16),
            pltpu.VMEM((rows, model), F32),
            pltpu.VMEM((rows, model), BF16),
            pltpu.VMEM((channels // LANES, rows, LANES), F32),
            pltpu.VMEM((frames, channels), F32),
            pltpu.VMEM((rows, 2 * channels), F32),
            pltpu.VMEM((n_taps * 8, LANES), F32),
            pltpu.VMEM((frames, channels), BF16),
            pltpu.VMEM((used + rim, channels), F32),
            pltpu.SemaphoreType.DMA,
        ],
        compiler_params=pltpu.CompilerParams(vmem_limit_bytes=32 * 2**20),
    )(*operands, from_a, from_b, *kvs)

    from_a, from_b = to_neighbours(pairwise, ctx, to_a, to_b)
    if pairwise:
        (far,) = flips(sums, "ctx", (2,))
        near, across = (x[:used].astype(F32) for x in (from_a, from_b))
        sums = ((sums.astype(F32) + near) + (far.astype(F32) + across)).astype(BF16)
        parts = [sums] + flips(sums, "dp", (1, 2, 3))

    d_hidden = pl.pallas_call(
        functools.partial(back_kernel, pairwise, ctx),
        out_shape=shape((frames, model), BF16),
        in_specs=[VMEM] * 10,
        out_specs=VMEM,
        scratch_shapes=[
            pltpu.VMEM((rows, channels), F32),
            pltpu.VMEM((2, used + rim, channels), F32),
            pltpu.VMEM((frames, 2 * channels), BF16),
            pltpu.VMEM((frames, model), F32),
        ],
        compiler_params=pltpu.CompilerParams(vmem_limit_bytes=24 * 2**20),
    )(kernel, norm_gain, w_in, x_norm, inv_norm, left, sig, d_conv, from_a, from_b)

    factor = 1.0 / math.sqrt(frames * ctx * dp)
    if pairwise:
        d_kernel, d_gain, d_bias = pl.pallas_call(
            functools.partial(total_kernel, factor),
            out_shape=(shape((n_taps, channels), F32),) + (shape((1, channels), F32),) * 2,
            in_specs=[VMEM] * 4,
            out_specs=(VMEM,) * 3,
            compiler_params=pltpu.CompilerParams(vmem_limit_bytes=2 * 2**20),
        )(*parts)
        d_gain, d_bias = d_gain.reshape(-1), d_bias.reshape(-1)
    else:
        total = lax.psum(sums, ("ctx", "dp")) * factor
        d_kernel, d_gain, d_bias = total[:n_taps], total[n_taps], total[n_taps + 1]
    return (conv_act[None], d_hidden[None], d_kernel, d_gain, d_bias)


def solution(mesh):
    split = P(("groups", "dp"), "ctx", None)
    return jax.shard_map(
        per_device,
        mesh=mesh,
        in_specs=(split,) * 4 + (P(),) * 6 + (split,),
        out_specs=(split, split, P("groups", None), P("groups"), P("groups")),
        check_vma=False,
    )
```

time: 47.3 us -> 33 us (0.70)
  local copies, waits for them, and re-layouts: 10.5 us -> 0 us
  waiting for transfers between devices: 15 us -> 10 us
  Pallas kernels: 8.49 us -> 11 us
  starting transfers between devices: 12.2 us -> 11.1 us
    unnamed x20 -> x0, local copies, waits for them, and re-layouts: 9.3 us -> none
    ppermute x8 -> x9, waiting for transfers between devices: 15 us -> 10 us  [flips(): lax.ppermute(array, axis, [(i, i ^ k) for i in range(4)])]
    pallas_call x3 -> x5, Pallas kernels: 8.49 us -> 11 us  [the longest x1 3.93 us: per_device(): pl.pallas_call(functools.partial(main_kernel, pairwise, ctx, kv_places),...]
    slice x2 -> x0, local copies, waits for them, and re-layouts: 1.22 us -> none  [the longest x1 0.63 us: per_device(): total[:n_taps]]
    ppermute x8 -> x9, starting transfers between devices: 12.2 us -> 11.1 us  [flips(): lax.ppermute(array, axis, [(i, i ^ k) for i in range(4)])]
  transfers between devices with their start and end apart: 8 -> 9, of which waited for: 4 -> 2; matrix products, arithmetic and copies ran while one was open for 0% -> 0% of each run, Pallas kernels for 5% -> 16%
where the time goes in v2:
time: 33 us; the launch traced here: 32.9 us
  starting transfers between devices  11.1 us (34%)
  Pallas kernels  11 us (33%)
  waiting for transfers between devices  10 us (30%)
  between operations  0.69 us (2%)
    ppermute x9, starting transfers between devices, flips(): lax.ppermute(array, axis, [(i, i ^ k) for i in range(4)])  11.1 us
    ppermute x9, waiting for transfers between devices, flips(): lax.ppermute(array, axis, [(i, i ^ k) for i in range(4)])  10 us
    pallas_call x1, Pallas kernels, per_device(): pl.pallas_call(functools.partial(main_kernel, pairwise, ctx, kv_places),...  3.93 us
    pallas_call x1, Pallas kernels, per_device(): pl.pallas_call(functools.partial(back_kernel, pairwise, ctx), out_shape=s...  2.89 us
    pallas_call x1, Pallas kernels, per_device(): pl.pallas_call(functools.partial(fetch_kernel, len(operands)), out_shape=...  2.23 us
    pallas_call x1, Pallas kernels, per_device(): pl.pallas_call(functools.partial(pack_kernel, pairwise), out_shape=(shape...  1.28 us
  transfers between devices with their start and end apart: 9, of which 2 were waited for; matrix products, arithmetic and copies ran while one was open for 0% of the time, Pallas kernels for 16%

profile of v2, /device:TPU:0, one launch (start us, length us, event | category | flops | bytes accessed | tf_op | source)
XLA Modules:
  0.0 32.9 jit_solution(12022084924391519537)
XLA Ops:
  0.6 1.3 %shard_map.146 = (bf16[64,512]{1,0:T(8,128)(2,1)S(1)}, bf16[112,512]{1,0:T(8,128)(2,1)S(1)}, bf16[112,512]{1,0:T(8,128)(2,1)S(1)}) custom-call(bf16[128,512]{1,0:T(8,128)(2,1)} %bitcast.17, bf16[128,512]{1,0:T(8,128)(2,1)} %bitcast.18, bf16[128,512]{1,0:T(8,128)(2,1)} %bitcast.14, bf16[128,1024]{1,0:T(8,128)(2,1)} %bitcast.12), custom_call_target="tpu_custom_call" | custom-call | tf_op jit(solution)/shard_map/pallas_call | solution.py:348
  1.9 3.1 %collective-permute-start = (bf16[112,512]{1,0:T(8,128)(2,1)S(1)}, bf16[112,512]{1,0:T(8,128)(2,1)S(1)}, u32[]{:S(2)}, u32[]{:S(2)}) collective-permute-start(bf16[112,512]{1,0:T(8,128)(2,1)S(1)} %get-tuple-element.39), channel_id=1, source_target_pairs={{0,4},{4,0},{8,12},{12,8},{1,5},{5,1},{9,13},{13,9},{2,6},{6,2},{1... | collective-permute-start | bytes 344072 | tf_op jit(solution)/shard_map/ppermute | solution.py:318
  5.0 2.5 %collective-permute-start.1 = (bf16[112,512]{1,0:T(8,128)(2,1)S(1)}, bf16[112,512]{1,0:T(8,128)(2,1)S(1)}, u32[]{:S(2)}, u32[]{:S(2)}) collective-permute-start(bf16[112,512]{1,0:T(8,128)(2,1)S(1)} %get-tuple-element.40), channel_id=1, source_target_pairs={{0,12},{4,8},{8,4},{12,0},{1,13},{5,9},{9,5},{13,1},{2,14},{6,10},... | collective-permute-start | bytes 344072 | tf_op jit(solution)/shard_map/ppermute | solution.py:318
  7.5 0.1 collective-permute-start.2
  7.6 2.2 %shard_map.147 = (bf16[128,512]{1,0:T(8,128)(2,1)S(1)}, bf16[128,1024]{1,0:T(8,128)(2,1)S(1)}, bf16[128,512]{1,0:T(8,128)(2,1)S(1)}, bf16[512,1024]{1,0:T(8,128)...) custom-call(bf16[64,512]{1,0:T(8,128)(2,1)S(1)} %get-tuple-element.2, ...), custom_call_target="tpu_custom_call" | custom-call | tf_op jit(solution)/shard_map/pallas_call | solution.py:379
  9.8 5.9 %collective-permute-done.2.refs_14_ = bf16[64,512]{1,0:T(8,128)(2,1)S(1)} collective-permute-done((bf16[64,512]{1,0:T(8,128)(2,1)S(1)}, bf16[64,512]{1,0:T(8,128)(2,1)S(1)}, u32[]{:S(2)}, u32[]{:S(2)}) %collective-permute-start.2) | collective-permute-done | bytes 65568 | tf_op jit(solution)/shard_map/ppermute | solution.py:318
  15.7 0.0 collective-permute-done.refs_9_.refs_12_
  15.7 0.0 collective-permute-done.1.refs_10_.refs_13_
  15.7 3.9 %shard_map.148 = (bf16[128,512]{1,0:T(8,128)(2,1)}, f32[160,1024]{1,0:T(8,128)S(1)}, f32[160,128]{1,0:T(8,128)S(1)}, f32[128,512]{1,0:T(8,128)S(1)}, f32[128,512...) custom-call(bf16[128,512]{1,0:T(8,128)(2,1)S(1)} %get-tuple-element., ...), custom_call_target="tpu_custom_call" | custom-call | tf_op jit(solution)/shard_map/pallas_call | solution.py:391
  19.7 0.1 collective-permute-start.3
  19.7 2.7 %collective-permute-start.4 = (bf16[48,512]{1,0:T(8,128)(2,1)S(1)}, bf16[48,512]{1,0:T(8,128)(2,1)S(1)}, u32[]{:S(2)}, u32[]{:S(2)}) collective-permute-start(bf16[48,512]{1,0:T(8,128)(2,1)S(1)} %get-tuple-element.48), channel_id=1, source_target_pairs={{0,12},{4,8},{8,4},{12,0},{1,13},{5,9},{9,5},{13,1},{2,14},{6,10},... | collective-permute-start | bytes 147464 | tf_op jit(solution)/shard_map/ppermute | solution.py:318
  22.5 0.8 %collective-permute-start.5 = (bf16[33,512]{1,0:T(8,128)(2,1)S(1)}, bf16[33,512]{1,0:T(8,128)(2,1)S(1)}, u32[]{:S(2)}, u32[]{:S(2)}) collective-permute-start(bf16[33,512]{1,0:T(8,128)(2,1)S(1)} %get-tuple-element.49), channel_id=1, source_target_pairs={{0,8},{4,12},{8,0},{12,4},{1,9},{5,13},{9,1},{13,5},{2,10},{6,14},... | collective-permute-start | bytes 101384 | tf_op jit(solution)/shard_map/ppermute | solution.py:318
  23.2 4.1 %collective-permute-done.5 = bf16[33,512]{1,0:T(8,128)(2,1)S(1)} collective-permute-done((bf16[33,512]{1,0:T(8,128)(2,1)S(1)}, bf16[33,512]{1,0:T(8,128)(2,1)S(1)}, u32[]{:S(2)}, u32[]{:S(2)}) %collective-permute-start.5) | collective-permute-done | bytes 33824 | tf_op jit(solution)/shard_map/ppermute | solution.py:318
  27.4 0.0 collective-permute-done.3.from_a
  27.4 0.0 collective-permute-done.4.from_b
  27.4 0.1 collective-permute-start.8
  27.5 1.6 %collective-permute-start.7 = (bf16[33,512]{1,0:T(8,128)(2,1)S(1)}, bf16[33,512]{1,0:T(8,128)(2,1)S(1)}, u32[]{:S(2)}, u32[]{:S(2)}) collective-permute-start(bf16[33,512]{1,0:T(8,128)(2,1)S(1)} %add_convert_fusion.one), channel_id=1, source_target_pairs={{0,2},{1,3},{2,0},{3,1},{4,6},{5,7},{6,4},{7,5},{8,10},{9,11},{10,... | collective-permute-start | bytes 101384 | tf_op jit(solution)/shard_map/ppermute | solution.py:318
  29.0 0.3 collective-permute-start.6
  29.3 2.9 %shard_map.149 = bf16[128,1024]{1,0:T(8,128)(2,1)} custom-call(f32[31,512]{1,0:T(8,128)S(1)} %get-tuple-element.36.refs_6_.kernel, f32[1,1024]{1,0:T(1,128)S(1)} %get-tuple-element.34.refs_4_.norm_gain, bf16[1024,1024]{1,0:T(8,128)(2,1)S(1)} %get-tuple-element.35.refs_5_.w_in, f32[160,1024]{1,0:T(8,128)S(1)} %get-tuple-element.42.x_norm, ...), custom_call_target="tpu_custom_call" | custom-call | tf_op jit(solution)/shard_map/pallas_call | solution.py:432
  32.2 0.0 collective-permute-done.8.four
  32.2 0.0 collective-permute-done.7.three
  32.2 0.0 collective-permute-done.6.two
  32.2 0.7 %shard_map.150 = (f32[31,512]{1,0:T(8,128)}, f32[1,512]{1,0:T(1,128)}, f32[1,512]{1,0:T(1,128)}) custom-call(bf16[33,512]{1,0:T(8,128)(2,1)S(1)} %add_convert_fusion.one, bf16[33,512]{1,0:T(8,128)(2,1)S(1)} %collective-permute-done.6.two, bf16[33,512]{1,0:T(8,128)(2,1)S(1)} %collective-permute-done.7.three, bf16[33,512]{1,0:T(8,128)(2,1)S(1)} %collective-permute-done.8.four), custom_call_target="tpu_custom_call" | custom-call | tf_op jit(solution)/shard_map/pallas_call | solution.py:448
  (1 shorter events, 0.0 us)
Async XLA Ops:
  1.9 13.8 %collective-permute-start = (bf16[112,512]{1,0:T(8,128)(2,1)S(1)}, bf16[112,512]{1,0:T(8,128)(2,1)S(1)}, u32[]{:S(2)}, u32[]{:S(2)}) collective-permute-start(bf16[112,512]{1,0:T(8,128)(2,1)S(1)} %get-tuple-element.39), channel_id=1, source_target_pairs={{0,4},{4,0},{8,12},{12,8},{1,5},{5,1},{9,13},{13,9},{2,6},{6,2},{1... | collective-permute-start | bytes 344072 | tf_op jit(solution)/shard_map/ppermute | solution.py:318
  5.0 10.7 %collective-permute-start.1 = (bf16[112,512]{1,0:T(8,128)(2,1)S(1)}, bf16[112,512]{1,0:T(8,128)(2,1)S(1)}, u32[]{:S(2)}, u32[]{:S(2)}) collective-permute-start(bf16[112,512]{1,0:T(8,128)(2,1)S(1)} %get-tuple-element.40), channel_id=1, source_target_pairs={{0,12},{4,8},{8,4},{12,0},{1,13},{5,9},{9,5},{13,1},{2,14},{6,10},... | collective-permute-start | bytes 344072 | tf_op jit(solution)/shard_map/ppermute | solution.py:318
  7.5 8.2 %collective-permute-start.2 = (bf16[64,512]{1,0:T(8,128)(2,1)S(1)}, bf16[64,512]{1,0:T(8,128)(2,1)S(1)}, u32[]{:S(2)}, u32[]{:S(2)}) collective-permute-start(bf16[64,512]{1,0:T(8,128)(2,1)S(1)} %get-tuple-element.29.after.refs_11_), channel_id=1, source_target_pairs={{0,8},{4,12},{8,0},{12,4},{1,9},{5,13},{9,1},{13,5},{2,10},{6,14},... | collective-permute-start | bytes 196616 | tf_op jit(solution)/shard_map/ppermute | solution.py:318
  19.7 7.7 %collective-permute-start.3 = (bf16[48,512]{1,0:T(8,128)(2,1)S(1)}, bf16[48,512]{1,0:T(8,128)(2,1)S(1)}, u32[]{:S(2)}, u32[]{:S(2)}) collective-permute-start(bf16[48,512]{1,0:T(8,128)(2,1)S(1)} %get-tuple-element.47), channel_id=1, source_target_pairs={{0,4},{4,0},{8,12},{12,8},{1,5},{5,1},{9,13},{13,9},{2,6},{6,2},{1... | collective-permute-start | bytes 147464 | tf_op jit(solution)/shard_map/ppermute | solution.py:318
  19.7 7.6 %collective-permute-start.4 = (bf16[48,512]{1,0:T(8,128)(2,1)S(1)}, bf16[48,512]{1,0:T(8,128)(2,1)S(1)}, u32[]{:S(2)}, u32[]{:S(2)}) collective-permute-start(bf16[48,512]{1,0:T(8,128)(2,1)S(1)} %get-tuple-element.48), channel_id=1, source_target_pairs={{0,12},{4,8},{8,4},{12,0},{1,13},{5,9},{9,5},{13,1},{2,14},{6,10},... | collective-permute-start | bytes 147464 | tf_op jit(solution)/shard_map/ppermute | solution.py:318
  22.5 4.9 %collective-permute-start.5 = (bf16[33,512]{1,0:T(8,128)(2,1)S(1)}, bf16[33,512]{1,0:T(8,128)(2,1)S(1)}, u32[]{:S(2)}, u32[]{:S(2)}) collective-permute-start(bf16[33,512]{1,0:T(8,128)(2,1)S(1)} %get-tuple-element.49), channel_id=1, source_target_pairs={{0,8},{4,12},{8,0},{12,4},{1,9},{5,13},{9,1},{13,5},{2,10},{6,14},... | collective-permute-start | bytes 101384 | tf_op jit(solution)/shard_map/ppermute | solution.py:318
  27.4 4.8 %collective-permute-start.8 = (bf16[33,512]{1,0:T(8,128)(2,1)S(1)}, bf16[33,512]{1,0:T(8,128)(2,1)S(1)}, u32[]{:S(2)}, u32[]{:S(2)}) collective-permute-start(bf16[33,512]{1,0:T(8,128)(2,1)S(1)} %add_convert_fusion.one), channel_id=1, source_target_pairs={{0,3},{1,2},{2,1},{3,0},{4,7},{5,6},{6,5},{7,4},{8,11},{9,10},{10,... | collective-permute-start | bytes 101384 | tf_op jit(solution)/shard_map/ppermute | solution.py:318
  27.5 4.7 %collective-permute-start.7 = (bf16[33,512]{1,0:T(8,128)(2,1)S(1)}, bf16[33,512]{1,0:T(8,128)(2,1)S(1)}, u32[]{:S(2)}, u32[]{:S(2)}) collective-permute-start(bf16[33,512]{1,0:T(8,128)(2,1)S(1)} %add_convert_fusion.one), channel_id=1, source_target_pairs={{0,2},{1,3},{2,0},{3,1},{4,6},{5,7},{6,4},{7,5},{8,10},{9,11},{10,... | collective-permute-start | bytes 101384 | tf_op jit(solution)/shard_map/ppermute | solution.py:318
  29.0 3.2 %collective-permute-start.6 = (bf16[33,512]{1,0:T(8,128)(2,1)S(1)}, bf16[33,512]{1,0:T(8,128)(2,1)S(1)}, u32[]{:S(2)}, u32[]{:S(2)}) collective-permute-start(bf16[33,512]{1,0:T(8,128)(2,1)S(1)} %add_convert_fusion.one), channel_id=1, source_target_pairs={{0,1},{1,0},{2,3},{3,2},{4,5},{5,4},{6,7},{7,6},{8,9},{9,8},{10,11... | collective-permute-start | bytes 101384 | tf_op jit(solution)/shard_map/ppermute | solution.py:318

commit v3 on v2

--- a/solution.py
+++ b/solution.py
@@ -55,9 +55,9 @@
         load.start()
     edges = []
     for target, near in ((to_a, True), (to_b, False)):
+        at = 0
         start = jnp.where(swap, 0 if near else frames - HALO, frames - HALO if near else 0)
         start = pl.multiple_of(start.astype(jnp.int32), HALO)
-        at = 2 * pooled
         for source, column in [(query, 0)] + [(resid, c) for c in range(0, model, width)]:
             edges.append(
                 pltpu.make_async_copy(
@@ -76,8 +76,6 @@
         block = dot(mean, kv[place]).astype(BF16)
         rows = pl.ds(place * pooled, pooled)
         own[rows, :] = block
-        to_a[rows, :] = block
-        to_b[rows, :] = block
     for edge in edges:
         edge.wait()
 
@@ -95,9 +93,9 @@
 
 def main_kernel(pairwise, count, kv_places, *refs):
     (query, resid, cotangent, w_out, norm_gain, w_in, kernel, conv_gain, conv_bias) = refs[:9]
-    from_a, from_b = refs[9:11]
     n_kv = len(kv_places)
-    kvs = refs[11 : 11 + n_kv]
+    kvs = refs[9 : 9 + n_kv]
+    from_b, from_a = refs[9 + n_kv : 11 + n_kv]
     (conv_act, x_norm, inv_norm, left_out, sig_out, d_conv) = refs[11 + n_kv : 17 + n_kv]
     to_a, to_b, sums = refs[17 + n_kv : 20 + n_kv]
     (q_all, r_edge, k_all, v_all, att, hid, normed, gated, conv, glu, taps, act_out, pack, sem) = (
@@ -109,7 +107,6 @@
     rows = frames + 2 * HALO
     n_taps = kernel.shape[0]
     rim = (n_taps - 1) // 2
-    pooled = frames // POOL
     me = lax.axis_index("ctx")
     first = me == 0
     last = me == count - 1
@@ -125,19 +122,18 @@
             at += keep
     keylen = at
     q_all[main, :] = query[...]
-    base = 2 * pooled
     for left_side in (True, False):
         edge_rows = pl.ds(0 if left_side else HALO + frames, HALO)
         r_rows = pl.ds(0 if left_side else HALO, HALO)
-        near, other = (from_b, from_a) if left_side else (from_a, from_b)
 
         def pick(start):
-            rows_in = pl.ds(start, HALO)
-            return jnp.where(swap, other[rows_in, :], near[rows_in, :])
-
-        q_all[edge_rows, :] = pick(base)
+            a = from_a[pl.ds(start, HALO), :]
+            b = from_b[pl.ds(start, HALO), :]
+            return jnp.where(swap, a, b) if left_side else jnp.where(swap, b, a)
+
+        q_all[edge_rows, :] = pick(0)
         for piece in range(model // width):
-            r_edge[r_rows, pl.ds(piece * width, width)] = pick(base + HALO * (1 + piece))
+            r_edge[r_rows, pl.ds(piece * width, width)] = pick(HALO * (1 + piece))
 
     lane = lax.broadcasted_iota(jnp.int32, (keylen, LANES), 1)
     low = lane < HEAD_DIM
@@ -261,9 +257,55 @@
     write.wait()
 
 
-def back_kernel(
-    pairwise, count, kernel, norm_gain, w_in, x_norm, inv_norm, left, sig, d_conv, from_a, from_b,
-    d_hidden, padded, edges, d_glu, d_normed,
+def back_rows(kernel, gain, w_in, d_conv, left, sig, x_norm, inv_norm, d_glu, d_normed, rows):
+    n_taps, channels = kernel.shape
+    model = w_in.shape[0]
+    for c in range(channels // LANES):
+        cols = slice(c * LANES, (c + 1) * LANES)
+        acc = jnp.zeros((rows, LANES), F32)
+        for t in range(n_taps):
+            acc = acc + kernel[t : t + 1, cols] * d_conv(c, t)
+        sg = sig(cols)
+        d_left = acc * sg
+        d_glu[:, cols] = d_left.astype(BF16)
+        d_glu[:, channels + c * LANES : channels + (c + 1) * LANES] = (
+            d_left * left(cols) * (1.0 - sg)
+        ).astype(BF16)
+    step = 256
+    for n in range(model // step):
+        d_normed[:, pl.ds(n * step, step)] = dot_t(d_glu[...], w_in[pl.ds(n * step, step), :])
+    for r in range(0, rows, 32):
+        g = d_normed[r : r + 32, :] * gain
+        x = x_norm(r)
+        yield r, (inv_norm(r) * (g - row_mean(g) - x * row_mean(g * x))).astype(BF16)
+
+
+def inner_kernel(
+    kernel, norm_gain, w_in, x_norm, inv_norm, left, sig, d_conv, sums, d_hidden, sums_out, d_glu,
+    d_normed, out, sem,
+):
+    sums_out[...] = sums[...]
+    rows = out.shape[0]
+    rim = (kernel.shape[0] - 1) // 2
+    blocks = back_rows(
+        kernel, norm_gain[...], w_in,
+        lambda c, t: d_conv[c, pl.ds(HALO + rim - t, rows), :],
+        lambda cols: left[HALO : HALO + rows, cols],
+        lambda cols: sig[HALO : HALO + rows, cols],
+        lambda r: x_norm[2 * HALO + r : 2 * HALO + r + 32, :],
+        lambda r: inv_norm[2 * HALO + r : 2 * HALO + r + 32, 0:1],
+        d_glu, d_normed, rows,
+    )
+    for r, block in blocks:
+        out[r : r + 32, :] = block
+    write = pltpu.make_async_copy(out, d_hidden.at[pl.ds(HALO, rows), :], sem)
+    write.start()
+    write.wait()
+
+
+def edge_kernel(
+    pairwise, count, inner, from_b, from_a, kernel, norm_gain, w_in, x_norm, inv_norm, left, sig,
+    d_conv, d_hidden, padded, edges, d_glu, d_normed, out, sem,
 ):
     frames, channels = left.shape
     n_taps = kernel.shape[0]
@@ -276,31 +318,42 @@
     for c in range(channels // LANES):
         cols = slice(c * LANES, (c + 1) * LANES)
         a, b = edges[0, used : used + rim, cols], edges[1, used : used + rim, cols]
-        on_left = jnp.where(me == 0, 0.0, jnp.where(swap, a, b))
-        on_right = jnp.where(me == count - 1, 0.0, jnp.where(swap, b, a))
-        padded[HALO - rim : HALO, cols] = on_left
-        padded[HALO : HALO + frames, cols] = d_conv[c]
-        padded[HALO + frames : HALO + frames + rim, cols] = on_right
-        acc = jnp.zeros((frames, LANES), F32)
-        for t in range(n_taps):
-            acc = acc + kernel[t : t + 1, cols] * padded[pl.ds(HALO - t + rim, frames), cols]
-        sg = sig[:, cols]
-        d_left = acc * sg
-        d_glu[:, cols] = d_left.astype(BF16)
-        d_glu[:, channels + c * LANES : channels + (c + 1) * LANES] = (
-            d_left * left[:, cols] * (1.0 - sg)
-        ).astype(BF16)
-    model = w_in.shape[0]
-    step = 256
-    for n in range(model // step):
-        d_normed[:, pl.ds(n * step, step)] = dot_t(d_glu[...], w_in[pl.ds(n * step, step), :])
-    gain = norm_gain[...]
-    for r in range(0, frames, 32):
-        g = d_normed[r : r + 32, :] * gain
-        x = x_norm[HALO + r : HALO + r + 32, :]
-        inv = inv_norm[HALO + r : HALO + r + 32, 0:1]
-        out = inv * (g - row_mean(g) - x * row_mean(g * x))
-        d_hidden[r : r + 32, :] = out.astype(BF16)
+        padded[0, c, HALO - rim : HALO, :] = jnp.where(me == 0, 0.0, jnp.where(swap, a, b))
+        padded[0, c, HALO:, :] = d_conv[c, 0 : 2 * HALO, :]
+        padded[1, c, 0 : 2 * HALO, :] = d_conv[c, frames - 2 * HALO :, :]
+        padded[1, c, 2 * HALO : 2 * HALO + rim, :] = jnp.where(
+            me == count - 1, 0.0, jnp.where(swap, b, a)
+        )
+
+    def both(ref, at, cols):
+        low = ref[at : at + HALO, cols]
+        return jnp.concatenate([low, ref[at + frames - HALO : at + frames, cols]], axis=0)
+
+    def pick(c, t):
+        rows = pl.ds(HALO + rim - t, HALO)
+        return jnp.concatenate([padded[0, c, rows, :], padded[1, c, rows, :]], axis=0)
+
+    every = slice(None)
+    blocks = back_rows(
+        kernel, norm_gain[...], w_in, pick,
+        lambda cols: both(left, 0, cols), lambda cols: both(sig, 0, cols),
+        lambda r: both(x_norm, HALO, every), lambda r: both(inv_norm, HALO, slice(0, 1)),
+        d_glu, d_normed, 2 * HALO,
+    )
+    for r, block in blocks:
+        out[...] = block
+    writes = [
+        pltpu.make_async_copy(
+            out.at[pl.ds(i * HALO, HALO), :],
+            d_hidden.at[pl.ds(i * (frames - HALO), HALO), :],
+            sem.at[i],
+        )
+        for i in range(2)
+    ]
+    for write in writes:
+        write.start()
+    for write in writes:
+        write.wait()
 
 
 def total_kernel(factor, one, two, three, four, d_kernel, d_gain, d_bias):
@@ -342,15 +395,15 @@
     )
     norm_gain, conv_gain, conv_bias = (x.reshape(1, -1) for x in (norm_gain, conv_gain, conv_bias))
     pooled = frames // POOL
-    message = 2 * pooled + HALO * (1 + model // width)
+    edge = HALO * (1 + model // width)
     n_edges = 2 * (1 + model // width)
 
     own, to_a, to_b = pl.pallas_call(
         functools.partial(pack_kernel, pairwise),
         out_shape=(
             shape((2 * pooled, width), BF16),
-            shape((message, width), BF16),
-            shape((message, width), BF16),
+            shape((edge, width), BF16),
+            shape((edge, width), BF16),
         ),
         in_specs=[HBM] * 4,
         out_specs=(VMEM,) * 3,
@@ -362,12 +415,14 @@
         compiler_params=pltpu.CompilerParams(vmem_limit_bytes=4 * 2**20),
     )(*in_hbm(keys, values, query, resid))
 
-    from_a, from_b = to_neighbours(pairwise, ctx, to_a, to_b)
     if pairwise:
-        (far,) = flips(own, "ctx", (2,))
-        kvs = (own, from_a, from_b, far)
+        near, far, across = flips(own, "ctx", (1, 2, 3))
+        (from_a,) = flips(to_a, "ctx", (1,))
+        from_b = lax.ppermute(to_b, "ctx", [(1, 2), (2, 1)])
+        kvs = (own, near, far, across)
         kv_places = ((0, pooled, pooled),) * 4
     else:
+        from_a, from_b = to_neighbours(pairwise, ctx, to_a, to_b)
         kvs = tuple(
             lax.all_gather(part, "ctx", axis=0, tiled=True) for part in (own[:pooled], own[pooled:])
         )
@@ -420,28 +475,50 @@
             pltpu.SemaphoreType.DMA,
         ],
         compiler_params=pltpu.CompilerParams(vmem_limit_bytes=32 * 2**20),
-    )(*operands, from_a, from_b, *kvs)
-
-    from_a, from_b = to_neighbours(pairwise, ctx, to_a, to_b)
+    )(*operands, *kvs, from_b, from_a)
+
+    inner = frames - 2 * HALO
+    common = (kernel, norm_gain, w_in, x_norm, inv_norm, left, sig, d_conv)
+    d_inner, same_sums = pl.pallas_call(
+        inner_kernel,
+        out_shape=(shape((frames, model), BF16), shape(sums.shape, sums.dtype)),
+        in_specs=[VMEM] * 9,
+        out_specs=(HBM, VMEM),
+        scratch_shapes=[
+            pltpu.VMEM((inner, 2 * channels), BF16),
+            pltpu.VMEM((inner, model), F32),
+            pltpu.VMEM((inner, model), BF16),
+            pltpu.SemaphoreType.DMA,
+        ],
+        compiler_params=pltpu.CompilerParams(vmem_limit_bytes=16 * 2**20),
+    )(*common, sums)
     if pairwise:
+        (from_b,) = flips(to_b, "ctx", (3,))
         (far,) = flips(sums, "ctx", (2,))
+        (from_a,) = flips(to_a, "ctx", (1,))
         near, across = (x[:used].astype(F32) for x in (from_a, from_b))
-        sums = ((sums.astype(F32) + near) + (far.astype(F32) + across)).astype(BF16)
+        sums = ((same_sums.astype(F32) + near) + (far.astype(F32) + across)).astype(BF16)
         parts = [sums] + flips(sums, "dp", (1, 2, 3))
+    else:
+        from_a, from_b = to_neighbours(pairwise, ctx, to_a, to_b)
+        sums = same_sums
 
     d_hidden = pl.pallas_call(
-        functools.partial(back_kernel, pairwise, ctx),
+        functools.partial(edge_kernel, pairwise, ctx),
         out_shape=shape((frames, model), BF16),
-        in_specs=[VMEM] * 10,
-        out_specs=VMEM,
+        in_specs=[HBM] + [VMEM] * 10,
+        out_specs=HBM,
+        input_output_aliases={0: 0},
         scratch_shapes=[
-            pltpu.VMEM((rows, channels), F32),
+            pltpu.VMEM((2, channels // LANES, 3 * HALO, LANES), F32),
             pltpu.VMEM((2, used + rim, channels), F32),
-            pltpu.VMEM((frames, 2 * channels), BF16),
-            pltpu.VMEM((frames, model), F32),
+            pltpu.VMEM((2 * HALO, 2 * channels), BF16),
+            pltpu.VMEM((2 * HALO, model), F32),
+            pltpu.VMEM((2 * HALO, model), BF16),
+            pltpu.SemaphoreType.DMA((2,)),
         ],
-        compiler_params=pltpu.CompilerParams(vmem_limit_bytes=24 * 2**20),
-    )(kernel, norm_gain, w_in, x_norm, inv_norm, left, sig, d_conv, from_a, from_b)
+        compiler_params=pltpu.CompilerParams(vmem_limit_bytes=16 * 2**20),
+    )(d_inner, from_b, from_a, *common)
 
     factor = 1.0 / math.sqrt(frames * ctx * dp)
     if pairwise:

time: 33 us -> 31.4 us (0.952)
  waiting for transfers between devices: 10 us -> 1.74 us
  starting transfers between devices: 11.1 us -> 16.9 us
  Pallas kernels: 11 us -> 11.8 us
    ppermute x9 -> x10, waiting for transfers between devices: 10 us -> 1.74 us  [flips(): lax.ppermute(array, axis, [(i, i ^ k) for i in range(4)])]
    ppermute x9 -> x10, starting transfers between devices: 11.1 us -> 16.3 us  [flips(): lax.ppermute(array, axis, [(i, i ^ k) for i in range(4)])]
    pallas_call x1 -> x2, Pallas kernels: 2.89 us -> 3.67 us  [the longest x1 2.08 us: per_device(): pl.pallas_call(inner_kernel, out_shape=(shape((frames, model), BF16), sha...]
    ppermute x0 -> x1, starting transfers between devices: none -> 0.65 us  [per_device(): from_b = lax.ppermute(to_b, 'ctx', [(1, 2), (2, 1)])]
  transfers between devices with their start and end apart: 9 -> 11, of which waited for: 2 -> 3; matrix products, arithmetic and copies ran while one was open for 0% -> 0% of each run, Pallas kernels for 16% -> 19%
where the time goes in v3:
time: 31.4 us; the launch traced here: 31.2 us
  starting transfers between devices  16.9 us (54%)
  Pallas kernels  11.8 us (38%)
  waiting for transfers between devices  1.74 us (6%)
  between operations  0.74 us (2%)
    ppermute x10, starting transfers between devices, flips(): lax.ppermute(array, axis, [(i, i ^ k) for i in range(4)])  16.3 us
    pallas_call x1, Pallas kernels, per_device(): pl.pallas_call(functools.partial(main_kernel, pairwise, ctx, kv_places),...  3.94 us
    pallas_call x1, Pallas kernels, per_device(): pl.pallas_call(functools.partial(fetch_kernel, len(operands)), out_shape=...  2.23 us
    pallas_call x1, Pallas kernels, per_device(): pl.pallas_call(inner_kernel, out_shape=(shape((frames, model), BF16), sha...  2.08 us
    ppermute x10, waiting for transfers between devices, flips(): lax.ppermute(array, axis, [(i, i ^ k) for i in range(4)])  1.74 us
    pallas_call x1, Pallas kernels, per_device(): pl.pallas_call(functools.partial(edge_kernel, pairwise, ctx), out_shape=s...  1.59 us
    pallas_call x1, Pallas kernels, per_device(): pl.pallas_call(functools.partial(pack_kernel, pairwise), out_shape=(shape...  1.27 us
    pallas_call x1, Pallas kernels, per_device(): pl.pallas_call(functools.partial(total_kernel, factor), out_shape=(shape(...  0.65 us
  transfers between devices with their start and end apart: 11, of which 3 were waited for; matrix products, arithmetic and copies ran while one was open for 0% of the time, Pallas kernels for 19%

profile of v3, /device:TPU:0, one launch (start us, length us, event | category | flops | bytes accessed | tf_op | source)
XLA Modules:
  0.0 31.2 jit_solution(15333676163791851807)
XLA Ops:
  0.6 1.3 %shard_map.146 = (bf16[64,512]{1,0:T(8,128)(2,1)S(1)}, bf16[48,512]{1,0:T(8,128)(2,1)S(1)}, bf16[48,512]{1,0:T(8,128)(2,1)S(1)}) custom-call(bf16[128,512]{1,0:T(8,128)(2,1)} %bitcast.17, bf16[128,512]{1,0:T(8,128)(2,1)} %bitcast.18, bf16[128,512]{1,0:T(8,128)(2,1)} %bitcast.14, bf16[128,1024]{1,0:T(8,128)(2,1)} %bitcast.12), custom_call_target="tpu_custom_call" | custom-call | tf_op jit(solution)/shard_map/pallas_call | solution.py:401
  1.9 5.1 %collective-permute-start.2 = (bf16[64,512]{1,0:T(8,128)(2,1)S(1)}, bf16[64,512]{1,0:T(8,128)(2,1)S(1)}, u32[]{:S(2)}, u32[]{:S(2)}) collective-permute-start(bf16[64,512]{1,0:T(8,128)(2,1)S(1)} %get-tuple-element.31.after.refs_9_), channel_id=1, source_target_pairs={{0,12},{4,8},{8,4},{12,0},{1,13},{5,9},{9,5},{13,1},{2,14},{6,10},... | collective-permute-start | bytes 196616 | tf_op jit(solution)/shard_map/ppermute | solution.py:371
  7.0 0.0 collective-permute-start.1
  7.0 0.6 %collective-permute-start = (bf16[64,512]{1,0:T(8,128)(2,1)S(1)}, bf16[64,512]{1,0:T(8,128)(2,1)S(1)}, u32[]{:S(2)}, u32[]{:S(2)}) collective-permute-start(bf16[64,512]{1,0:T(8,128)(2,1)S(1)} %get-tuple-element.31.after.refs_9_), channel_id=1, source_target_pairs={{0,4},{4,0},{8,12},{12,8},{1,5},{5,1},{9,13},{13,9},{2,6},{6,2},{1... | collective-permute-start | bytes 196616 | tf_op jit(solution)/shard_map/ppermute | solution.py:371
  7.7 0.7 %collective-permute-start.3 = (bf16[48,512]{1,0:T(8,128)(2,1)S(1)}, bf16[48,512]{1,0:T(8,128)(2,1)S(1)}, u32[]{:S(2)}, u32[]{:S(2)}) collective-permute-start(bf16[48,512]{1,0:T(8,128)(2,1)S(1)} %get-tuple-element.41), channel_id=1, source_target_pairs={{4,8},{8,4},{5,9},{9,5},{6,10},{10,6},{7,11},{11,7},{20,24},{24,20... | collective-permute-start | bytes 147464 | tf_op jit(solution)/shard_map/ppermute | solution.py:421
  8.3 4.2 %collective-permute-start.4 = (bf16[48,512]{1,0:T(8,128)(2,1)S(1)}, bf16[48,512]{1,0:T(8,128)(2,1)S(1)}, u32[]{:S(2)}, u32[]{:S(2)}) collective-permute-start(bf16[48,512]{1,0:T(8,128)(2,1)S(1)} %get-tuple-element.42), channel_id=1, source_target_pairs={{0,4},{4,0},{8,12},{12,8},{1,5},{5,1},{9,13},{13,9},{2,6},{6,2},{1... | collective-permute-start | bytes 147464 | tf_op jit(solution)/shard_map/ppermute | solution.py:371
  12.5 2.2 %shard_map.147 = (bf16[128,512]{1,0:T(8,128)(2,1)S(1)}, bf16[128,1024]{1,0:T(8,128)(2,1)S(1)}, bf16[128,512]{1,0:T(8,128)(2,1)S(1)}, bf16[512,1024]{1,0:T(8,128)...) custom-call(bf16[64,512]{1,0:T(8,128)(2,1)S(1)} %get-tuple-element.3, ...), custom_call_target="tpu_custom_call" | custom-call | tf_op jit(solution)/shard_map/pallas_call | solution.py:434
  14.7 0.0 collective-permute-done.3.refs_13_
  14.7 0.0 collective-permute-done.4.refs_14_
  14.8 0.0 collective-permute-done.2.refs_12_
  14.8 0.0 collective-permute-done.1.refs_11_
  14.8 0.0 collective-permute-done.refs_10_
  14.8 3.9 %shard_map.148 = (bf16[128,512]{1,0:T(8,128)(2,1)}, f32[160,1024]{1,0:T(8,128)S(1)}, f32[160,128]{1,0:T(8,128)S(1)}, f32[128,512]{1,0:T(8,128)S(1)}, f32[128,512...) custom-call(bf16[128,512]{1,0:T(8,128)(2,1)S(1)} %get-tuple-element., ...), custom_call_target="tpu_custom_call" | custom-call | tf_op jit(solution)/shard_map/pallas_call | solution.py:446
  18.7 1.6 %collective-permute-start.5 = (bf16[48,512]{1,0:T(8,128)(2,1)S(1)}, bf16[48,512]{1,0:T(8,128)(2,1)S(1)}, u32[]{:S(2)}, u32[]{:S(2)}) collective-permute-start(bf16[48,512]{1,0:T(8,128)(2,1)S(1)} %get-tuple-element.51), channel_id=1, source_target_pairs={{0,12},{4,8},{8,4},{12,0},{1,13},{5,9},{9,5},{13,1},{2,14},{6,10},... | collective-permute-start | bytes 147464 | tf_op jit(solution)/shard_map/ppermute | solution.py:371
  20.3 0.9 %collective-permute-start.6 = (bf16[48,512]{1,0:T(8,128)(2,1)S(1)}, bf16[48,512]{1,0:T(8,128)(2,1)S(1)}, u32[]{:S(2)}, u32[]{:S(2)}) collective-permute-start(bf16[48,512]{1,0:T(8,128)(2,1)S(1)} %get-tuple-element.52), channel_id=1, source_target_pairs={{0,4},{4,0},{8,12},{12,8},{1,5},{5,1},{9,13},{13,9},{2,6},{6,2},{1... | collective-permute-start | bytes 147464 | tf_op jit(solution)/shard_map/ppermute | solution.py:371
  21.2 2.0 %collective-permute-start.7 = (bf16[33,512]{1,0:T(8,128)(2,1)S(1)}, bf16[33,512]{1,0:T(8,128)(2,1)S(1)}, u32[]{:S(2)}, u32[]{:S(2)}) collective-permute-start(bf16[33,512]{1,0:T(8,128)(2,1)S(1)} %get-tuple-element.49.sums), channel_id=1, source_target_pairs={{0,8},{4,12},{8,0},{12,4},{1,9},{5,13},{9,1},{13,5},{2,10},{6,14},... | collective-permute-start | bytes 101384 | tf_op jit(solution)/shard_map/ppermute | solution.py:371
  23.2 2.1 %shard_map.149 = (bf16[128,1024]{1,0:T(8,128)(2,1)}, bf16[33,512]{1,0:T(8,128)(2,1)S(1)}) custom-call(f32[31,512]{1,0:T(8,128)S(1)} %get-tuple-element.38.refs_6_.kernel, f32[1,1024]{1,0:T(1,128)S(1)} %get-tuple-element.36.refs_4_.norm_gain, bf16[1024,1024]{1,0:T(8,128)(2,1)S(1)} %get-tuple-element.37.refs_5_.w_in, ...), custom_call_target="tpu_custom_call" | custom-call | tf_op jit(solution)/shard_map/pallas_call | solution.py:482
  25.3 0.8 %collective-permute-done.7 = bf16[33,512]{1,0:T(8,128)(2,1)S(1)} collective-permute-done((bf16[33,512]{1,0:T(8,128)(2,1)S(1)}, bf16[33,512]{1,0:T(8,128)(2,1)S(1)}, u32[]{:S(2)}, u32[]{:S(2)}) %collective-permute-start.7) | collective-permute-done | bytes 33824 | tf_op jit(solution)/shard_map/ppermute | solution.py:371
  26.1 0.0 collective-permute-done.5.from_b
  26.1 0.0 collective-permute-done.6.from_a
  26.1 0.1 collective-permute-start.10
  26.2 1.6 %collective-permute-start.9 = (bf16[33,512]{1,0:T(8,128)(2,1)S(1)}, bf16[33,512]{1,0:T(8,128)(2,1)S(1)}, u32[]{:S(2)}, u32[]{:S(2)}) collective-permute-start(bf16[33,512]{1,0:T(8,128)(2,1)S(1)} %add_convert_fusion.one), channel_id=1, source_target_pairs={{0,2},{1,3},{2,0},{3,1},{4,6},{5,7},{6,4},{7,5},{8,10},{9,11},{10,... | collective-permute-start | bytes 101384 | tf_op jit(solution)/shard_map/ppermute | solution.py:371
  27.7 0.3 collective-permute-start.8
  28.0 1.6 %shard_map.150 = bf16[128,1024]{1,0:T(8,128)(2,1)} custom-call(bf16[128,1024]{1,0:T(8,128)(2,1)} %get-tuple-element.50.inner, bf16[48,512]{1,0:T(8,128)(2,1)S(1)} %collective-permute-done.5.from_b, bf16[48,512]{1,0:T(8,128)(2,1)S(1)} %collective-permute-done.6.from_a, ...), custom_call_target="tpu_custom_call", output_to_operand_aliasing={{}: (0, {})} | custom-call | tf_op jit(solution)/shard_map/pallas_call | solution.py:506
  29.6 0.4 %collective-permute-done.10.four = bf16[33,512]{1,0:T(8,128)(2,1)S(1)} collective-permute-done((bf16[33,512]{1,0:T(8,128)(2,1)S(1)}, bf16[33,512]{1,0:T(8,128)(2,1)S(1)}, u32[]{:S(2)}, u32[]{:S(2)}) %collective-permute-start.10) | collective-permute-done | bytes 33824 | tf_op jit(solution)/shard_map/ppermute | solution.py:371
  30.0 0.6 %collective-permute-done.9.three = bf16[33,512]{1,0:T(8,128)(2,1)S(1)} collective-permute-done((bf16[33,512]{1,0:T(8,128)(2,1)S(1)}, bf16[33,512]{1,0:T(8,128)(2,1)S(1)}, u32[]{:S(2)}, u32[]{:S(2)}) %collective-permute-start.9) | collective-permute-done | bytes 33824 | tf_op jit(solution)/shard_map/ppermute | solution.py:371
  30.6 0.0 collective-permute-done.8.two
  30.6 0.7 %shard_map.151 = (f32[31,512]{1,0:T(8,128)}, f32[1,512]{1,0:T(1,128)}, f32[1,512]{1,0:T(1,128)}) custom-call(bf16[33,512]{1,0:T(8,128)(2,1)S(1)} %add_convert_fusion.one, bf16[33,512]{1,0:T(8,128)(2,1)S(1)} %collective-permute-done.8.two, bf16[33,512]{1,0:T(8,128)(2,1)S(1)} %collective-permute-done.9.three, bf16[33,512]{1,0:T(8,128)(2,1)S(1)} %collective-permute-done.10.four), custom_call_target="tpu_custom_call" | custom-call | tf_op jit(solution)/shard_map/pallas_call | solution.py:525
  (1 shorter events, 0.0 us)
Async XLA Ops:
  1.9 12.8 %collective-permute-start.2 = (bf16[64,512]{1,0:T(8,128)(2,1)S(1)}, bf16[64,512]{1,0:T(8,128)(2,1)S(1)}, u32[]{:S(2)}, u32[]{:S(2)}) collective-permute-start(bf16[64,512]{1,0:T(8,128)(2,1)S(1)} %get-tuple-element.31.after.refs_9_), channel_id=1, source_target_pairs={{0,12},{4,8},{8,4},{12,0},{1,13},{5,9},{9,5},{13,1},{2,14},{6,10},... | collective-permute-start | bytes 196616 | tf_op jit(solution)/shard_map/ppermute | solution.py:371
  7.0 7.7 %collective-permute-start.1 = (bf16[64,512]{1,0:T(8,128)(2,1)S(1)}, bf16[64,512]{1,0:T(8,128)(2,1)S(1)}, u32[]{:S(2)}, u32[]{:S(2)}) collective-permute-start(bf16[64,512]{1,0:T(8,128)(2,1)S(1)} %get-tuple-element.31.after.refs_9_), channel_id=1, source_target_pairs={{0,8},{4,12},{8,0},{12,4},{1,9},{5,13},{9,1},{13,5},{2,10},{6,14},... | collective-permute-start | bytes 196616 | tf_op jit(solution)/shard_map/ppermute | solution.py:371
  7.0 7.7 %collective-permute-start = (bf16[64,512]{1,0:T(8,128)(2,1)S(1)}, bf16[64,512]{1,0:T(8,128)(2,1)S(1)}, u32[]{:S(2)}, u32[]{:S(2)}) collective-permute-start(bf16[64,512]{1,0:T(8,128)(2,1)S(1)} %get-tuple-element.31.after.refs_9_), channel_id=1, source_target_pairs={{0,4},{4,0},{8,12},{12,8},{1,5},{5,1},{9,13},{13,9},{2,6},{6,2},{1... | collective-permute-start | bytes 196616 | tf_op jit(solution)/shard_map/ppermute | solution.py:371
  7.7 7.1 %collective-permute-start.3 = (bf16[48,512]{1,0:T(8,128)(2,1)S(1)}, bf16[48,512]{1,0:T(8,128)(2,1)S(1)}, u32[]{:S(2)}, u32[]{:S(2)}) collective-permute-start(bf16[48,512]{1,0:T(8,128)(2,1)S(1)} %get-tuple-element.41), channel_id=1, source_target_pairs={{4,8},{8,4},{5,9},{9,5},{6,10},{10,6},{7,11},{11,7},{20,24},{24,20... | collective-permute-start | bytes 147464 | tf_op jit(solution)/shard_map/ppermute | solution.py:421
  8.3 6.4 %collective-permute-start.4 = (bf16[48,512]{1,0:T(8,128)(2,1)S(1)}, bf16[48,512]{1,0:T(8,128)(2,1)S(1)}, u32[]{:S(2)}, u32[]{:S(2)}) collective-permute-start(bf16[48,512]{1,0:T(8,128)(2,1)S(1)} %get-tuple-element.42), channel_id=1, source_target_pairs={{0,4},{4,0},{8,12},{12,8},{1,5},{5,1},{9,13},{13,9},{2,6},{6,2},{1... | collective-permute-start | bytes 147464 | tf_op jit(solution)/shard_map/ppermute | solution.py:371
  18.7 7.3 %collective-permute-start.5 = (bf16[48,512]{1,0:T(8,128)(2,1)S(1)}, bf16[48,512]{1,0:T(8,128)(2,1)S(1)}, u32[]{:S(2)}, u32[]{:S(2)}) collective-permute-start(bf16[48,512]{1,0:T(8,128)(2,1)S(1)} %get-tuple-element.51), channel_id=1, source_target_pairs={{0,12},{4,8},{8,4},{12,0},{1,13},{5,9},{9,5},{13,1},{2,14},{6,10},... | collective-permute-start | bytes 147464 | tf_op jit(solution)/shard_map/ppermute | solution.py:371
  20.3 5.8 %collective-permute-start.6 = (bf16[48,512]{1,0:T(8,128)(2,1)S(1)}, bf16[48,512]{1,0:T(8,128)(2,1)S(1)}, u32[]{:S(2)}, u32[]{:S(2)}) collective-permute-start(bf16[48,512]{1,0:T(8,128)(2,1)S(1)} %get-tuple-element.52), channel_id=1, source_target_pairs={{0,4},{4,0},{8,12},{12,8},{1,5},{5,1},{9,13},{13,9},{2,6},{6,2},{1... | collective-permute-start | bytes 147464 | tf_op jit(solution)/shard_map/ppermute | solution.py:371
  21.2 4.9 %collective-permute-start.7 = (bf16[33,512]{1,0:T(8,128)(2,1)S(1)}, bf16[33,512]{1,0:T(8,128)(2,1)S(1)}, u32[]{:S(2)}, u32[]{:S(2)}) collective-permute-start(bf16[33,512]{1,0:T(8,128)(2,1)S(1)} %get-tuple-element.49.sums), channel_id=1, source_target_pairs={{0,8},{4,12},{8,0},{12,4},{1,9},{5,13},{9,1},{13,5},{2,10},{6,14},... | collective-permute-start | bytes 101384 | tf_op jit(solution)/shard_map/ppermute | solution.py:371
  26.1 3.9 %collective-permute-start.10 = (bf16[33,512]{1,0:T(8,128)(2,1)S(1)}, bf16[33,512]{1,0:T(8,128)(2,1)S(1)}, u32[]{:S(2)}, u32[]{:S(2)}) collective-permute-start(bf16[33,512]{1,0:T(8,128)(2,1)S(1)} %add_convert_fusion.one), channel_id=1, source_target_pairs={{0,3},{1,2},{2,1},{3,0},{4,7},{5,6},{6,5},{7,4},{8,11},{9,10},{10,... | collective-permute-start | bytes 101384 | tf_op jit(solution)/shard_map/ppermute | solution.py:371
  26.2 4.4 %collective-permute-start.9 = (bf16[33,512]{1,0:T(8,128)(2,1)S(1)}, bf16[33,512]{1,0:T(8,128)(2,1)S(1)}, u32[]{:S(2)}, u32[]{:S(2)}) collective-permute-start(bf16[33,512]{1,0:T(8,128)(2,1)S(1)} %add_convert_fusion.one), channel_id=1, source_target_pairs={{0,2},{1,3},{2,0},{3,1},{4,6},{5,7},{6,4},{7,5},{8,10},{9,11},{10,... | collective-permute-start | bytes 101384 | tf_op jit(solution)/shard_map/ppermute | solution.py:371
  27.7 2.8 %collective-permute-start.8 = (bf16[33,512]{1,0:T(8,128)(2,1)S(1)}, bf16[33,512]{1,0:T(8,128)(2,1)S(1)}, u32[]{:S(2)}, u32[]{:S(2)}) collective-permute-start(bf16[33,512]{1,0:T(8,128)(2,1)S(1)} %add_convert_fusion.one), channel_id=1, source_target_pairs={{0,1},{1,0},{2,3},{3,2},{4,5},{5,4},{6,7},{7,6},{8,9},{9,8},{10,11... | collective-permute-start | bytes 101384 | tf_op jit(solution)/shard_map/ppermute | solution.py:371

commit v4 on v3

--- a/solution.py
+++ b/solution.py
@@ -55,7 +55,7 @@
         load.start()
     edges = []
     for target, near in ((to_a, True), (to_b, False)):
-        at = 0
+        at = 2 * pooled
         start = jnp.where(swap, 0 if near else frames - HALO, frames - HALO if near else 0)
         start = pl.multiple_of(start.astype(jnp.int32), HALO)
         for source, column in [(query, 0)] + [(resid, c) for c in range(0, model, width)]:
@@ -76,6 +76,8 @@
         block = dot(mean, kv[place]).astype(BF16)
         rows = pl.ds(place * pooled, pooled)
         own[rows, :] = block
+        to_a[rows, :] = block
+        to_b[rows, :] = block
     for edge in edges:
         edge.wait()
 
@@ -91,9 +93,8 @@
         copy.wait()
 
 
-def main_kernel(pairwise, count, kv_places, *refs):
+def main_kernel(pairwise, count, n_kv, *refs):
     (query, resid, cotangent, w_out, norm_gain, w_in, kernel, conv_gain, conv_bias) = refs[:9]
-    n_kv = len(kv_places)
     kvs = refs[9 : 9 + n_kv]
     from_b, from_a = refs[9 + n_kv : 11 + n_kv]
     (conv_act, x_norm, inv_norm, left_out, sig_out, d_conv) = refs[11 + n_kv : 17 + n_kv]
@@ -113,22 +114,28 @@
     swap = swapped(pairwise)
     main = pl.ds(HALO, frames)
 
-    at = 0
-    for ref, (k_row, v_row, keep) in zip(kvs, kv_places):
-        if k_row is not None:
-            k_all[pl.ds(at, keep), :] = ref[pl.ds(k_row, keep), :]
-        if v_row is not None:
-            v_all[pl.ds(at, keep), :] = ref[pl.ds(v_row, keep), :]
-            at += keep
-    keylen = at
+    pooled = frames // POOL
+    if pairwise:
+        own, far, ends = kvs
+        middle = (me == 1) | (me == 2)
+        for side, target in enumerate((k_all, v_all)):
+            rows_in = pl.ds(side * pooled, pooled)
+            target[0:pooled, :] = own[rows_in, :]
+            target[pooled : 2 * pooled, :] = from_a[rows_in, :]
+            target[2 * pooled : 3 * pooled, :] = far[rows_in, :]
+            target[3 * pooled :, :] = jnp.where(middle, from_b[rows_in, :], ends[rows_in, :])
+    else:
+        for source, target in zip(kvs, (k_all, v_all)):
+            target[...] = source[...]
+    keylen = count * pooled
     q_all[main, :] = query[...]
     for left_side in (True, False):
         edge_rows = pl.ds(0 if left_side else HALO + frames, HALO)
         r_rows = pl.ds(0 if left_side else HALO, HALO)
 
         def pick(start):
-            a = from_a[pl.ds(start, HALO), :]
-            b = from_b[pl.ds(start, HALO), :]
+            a = from_a[pl.ds(2 * pooled + start, HALO), :]
+            b = from_b[pl.ds(2 * pooled + start, HALO), :]
             return jnp.where(swap, a, b) if left_side else jnp.where(swap, b, a)
 
         q_all[edge_rows, :] = pick(0)
@@ -395,15 +402,15 @@
     )
     norm_gain, conv_gain, conv_bias = (x.reshape(1, -1) for x in (norm_gain, conv_gain, conv_bias))
     pooled = frames // POOL
-    edge = HALO * (1 + model // width)
+    message = 2 * pooled + HALO * (1 + model // width)
     n_edges = 2 * (1 + model // width)
 
     own, to_a, to_b = pl.pallas_call(
         functools.partial(pack_kernel, pairwise),
         out_shape=(
             shape((2 * pooled, width), BF16),
-            shape((edge, width), BF16),
-            shape((edge, width), BF16),
+            shape((message, width), BF16),
+            shape((message, width), BF16),
         ),
         in_specs=[HBM] * 4,
         out_specs=(VMEM,) * 3,
@@ -416,17 +423,16 @@
     )(*in_hbm(keys, values, query, resid))
 
     if pairwise:
-        near, far, across = flips(own, "ctx", (1, 2, 3))
+        from_b = lax.ppermute(to_b, "ctx", [(1, 2), (2, 1)])
         (from_a,) = flips(to_a, "ctx", (1,))
-        from_b = lax.ppermute(to_b, "ctx", [(1, 2), (2, 1)])
-        kvs = (own, near, far, across)
-        kv_places = ((0, pooled, pooled),) * 4
+        ends = lax.ppermute(own, "ctx", [(0, 3), (3, 0)])
+        (far,) = flips(own, "ctx", (2,))
+        kvs = (own, far, ends)
     else:
         from_a, from_b = to_neighbours(pairwise, ctx, to_a, to_b)
         kvs = tuple(
             lax.all_gather(part, "ctx", axis=0, tiled=True) for part in (own[:pooled], own[pooled:])
         )
-        kv_places = ((0, None, pooled * ctx), (None, 0, pooled * ctx))
 
     operands = (
         query, resid, cotangent, w_out, norm_gain, w_in, kernel, conv_gain, conv_bias,
@@ -444,7 +450,7 @@
     rows = frames + 2 * HALO
     used = n_taps + 2
     conv_act, x_norm, inv_norm, left, sig, d_conv, to_a, to_b, sums = pl.pallas_call(
-        functools.partial(main_kernel, pairwise, ctx, kv_places),
+        functools.partial(main_kernel, pairwise, ctx, len(kvs)),
         out_shape=(
             shape((frames, channels), BF16),
             shape((rows, model), F32),

time: 31.4 us -> 34.3 us (1.092)
  waiting for transfers between devices: 1.74 us -> 5.31 us
  starting transfers between devices: 16.9 us -> 16.3 us
    ppermute x10 -> x8, starting transfers between devices: 16.3 us -> 12.3 us  [flips(): lax.ppermute(array, axis, [(i, i ^ k) for i in range(4)])]
    ppermute x0 -> x1, starting transfers between devices: none -> 3.24 us  [per_device(): ends = lax.ppermute(own, 'ctx', [(0, 3), (3, 0)])]
    ppermute x0 -> x1, waiting for transfers between devices: none -> 2.37 us  [per_device(): ends = lax.ppermute(own, 'ctx', [(0, 3), (3, 0)])]
    ppermute x10 -> x8, waiting for transfers between devices: 1.74 us -> 2.94 us  [flips(): lax.ppermute(array, axis, [(i, i ^ k) for i in range(4)])]
  transfers between devices with their start and end apart: 11 -> 10, of which waited for: 3 -> 5; matrix products, arithmetic and copies ran while one was open for 0% -> 0% of each run, Pallas kernels for 19% -> 17%
where the time goes in v4:
time: 34.3 us; the launch traced here: 34.1 us
  starting transfers between devices  16.3 us (48%)
  Pallas kernels  11.8 us (34%)
  waiting for transfers between devices  5.31 us (15%)
  between operations  0.72 us (2%)
    ppermute x8, starting transfers between devices, flips(): lax.ppermute(array, axis, [(i, i ^ k) for i in range(4)])  12.3 us
    pallas_call x1, Pallas kernels, per_device(): pl.pallas_call(functools.partial(main_kernel, pairwise, ctx, len(kvs)), o...  3.92 us
    ppermute x1, starting transfers between devices, per_device(): ends = lax.ppermute(own, 'ctx', [(0, 3), (3, 0)])  3.24 us
    ppermute x8, waiting for transfers between devices, flips(): lax.ppermute(array, axis, [(i, i ^ k) for i in range(4)])  2.94 us
    ppermute x1, waiting for transfers between devices, per_device(): ends = lax.ppermute(own, 'ctx', [(0, 3), (3, 0)])  2.37 us
    pallas_call x1, Pallas kernels, per_device(): pl.pallas_call(functools.partial(fetch_kernel, len(operands)), out_shape=...  2.25 us
    pallas_call x1, Pallas kernels, per_device(): pl.pallas_call(inner_kernel, out_shape=(shape((frames, model), BF16), sha...  2.08 us
    pallas_call x1, Pallas kernels, per_device(): pl.pallas_call(functools.partial(edge_kernel, pairwise, ctx), out_shape=s...  1.59 us
  transfers between devices with their start and end apart: 10, of which 5 were waited for; matrix products, arithmetic and copies ran while one was open for 0% of the time, Pallas kernels for 17%

profile of v4, /device:TPU:0, one launch (start us, length us, event | category | flops | bytes accessed | tf_op | source)
XLA Modules:
  0.0 34.1 jit_solution(10112747497405100085)
XLA Ops:
  0.6 1.3 %shard_map.146 = (bf16[64,512]{1,0:T(8,128)(2,1)S(1)}, bf16[112,512]{1,0:T(8,128)(2,1)S(1)}, bf16[112,512]{1,0:T(8,128)(2,1)S(1)}) custom-call(bf16[128,512]{1,0:T(8,128)(2,1)} %bitcast.17, bf16[128,512]{1,0:T(8,128)(2,1)} %bitcast.18, bf16[128,512]{1,0:T(8,128)(2,1)} %bitcast.14, bf16[128,1024]{1,0:T(8,128)(2,1)} %bitcast.12), custom_call_target="tpu_custom_call" | custom-call | tf_op jit(solution)/shard_map/pallas_call | solution.py:408
  1.9 0.7 %collective-permute-start.2 = (bf16[112,512]{1,0:T(8,128)(2,1)S(1)}, bf16[112,512]{1,0:T(8,128)(2,1)S(1)}, u32[]{:S(2)}, u32[]{:S(2)}) collective-permute-start(bf16[112,512]{1,0:T(8,128)(2,1)S(1)} %get-tuple-element.41), channel_id=1, source_target_pairs={{4,8},{8,4},{5,9},{9,5},{6,10},{10,6},{7,11},{11,7},{20,24},{24,20... | collective-permute-start | bytes 344072 | tf_op jit(solution)/shard_map/ppermute | solution.py:426
  2.6 5.9 %collective-permute-start.3 = (bf16[112,512]{1,0:T(8,128)(2,1)S(1)}, bf16[112,512]{1,0:T(8,128)(2,1)S(1)}, u32[]{:S(2)}, u32[]{:S(2)}) collective-permute-start(bf16[112,512]{1,0:T(8,128)(2,1)S(1)} %get-tuple-element.42), channel_id=1, source_target_pairs={{0,4},{4,0},{8,12},{12,8},{1,5},{5,1},{9,13},{13,9},{2,6},{6,2},{1... | collective-permute-start | bytes 344072 | tf_op jit(solution)/shard_map/ppermute | solution.py:378
  8.5 3.2 %collective-permute-start.1 = (bf16[64,512]{1,0:T(8,128)(2,1)S(1)}, bf16[64,512]{1,0:T(8,128)(2,1)S(1)}, u32[]{:S(2)}, u32[]{:S(2)}) collective-permute-start(bf16[64,512]{1,0:T(8,128)(2,1)S(1)} %get-tuple-element.31.after.refs_9_), channel_id=1, source_target_pairs={{0,12},{12,0},{1,13},{13,1},{2,14},{14,2},{3,15},{15,3},{16,28},{2... | collective-permute-start | bytes 196616 | tf_op jit(solution)/shard_map/ppermute | solution.py:428
  11.8 0.1 collective-permute-start
  11.8 2.2 %shard_map.147 = (bf16[128,512]{1,0:T(8,128)(2,1)S(1)}, bf16[128,1024]{1,0:T(8,128)(2,1)S(1)}, bf16[128,512]{1,0:T(8,128)(2,1)S(1)}, bf16[512,1024]{1,0:T(8,128)...) custom-call(bf16[64,512]{1,0:T(8,128)(2,1)S(1)} %get-tuple-element.3, ...), custom_call_target="tpu_custom_call" | custom-call | tf_op jit(solution)/shard_map/pallas_call | solution.py:440
  14.1 2.4 %collective-permute-done.1.refs_11_ = bf16[64,512]{1,0:T(8,128)(2,1)S(1)} collective-permute-done((bf16[64,512]{1,0:T(8,128)(2,1)S(1)}, bf16[64,512]{1,0:T(8,128)(2,1)S(1)}, u32[]{:S(2)}, u32[]{:S(2)}) %collective-permute-start.1) | collective-permute-done | bytes 65568 | tf_op jit(solution)/shard_map/ppermute | solution.py:428
  16.4 1.8 %collective-permute-done.refs_10_ = bf16[64,512]{1,0:T(8,128)(2,1)S(1)} collective-permute-done((bf16[64,512]{1,0:T(8,128)(2,1)S(1)}, bf16[64,512]{1,0:T(8,128)(2,1)S(1)}, u32[]{:S(2)}, u32[]{:S(2)}) %collective-permute-start) | collective-permute-done | bytes 65568 | tf_op jit(solution)/shard_map/ppermute | solution.py:378
  18.3 0.0 collective-permute-done.2.refs_12_
  18.3 0.0 collective-permute-done.3.refs_13_
  18.3 3.9 %shard_map.148 = (bf16[128,512]{1,0:T(8,128)(2,1)}, f32[160,1024]{1,0:T(8,128)S(1)}, f32[160,128]{1,0:T(8,128)S(1)}, f32[128,512]{1,0:T(8,128)S(1)}, f32[128,512...) custom-call(bf16[128,512]{1,0:T(8,128)(2,1)S(1)} %get-tuple-element., ...), custom_call_target="tpu_custom_call" | custom-call | tf_op jit(solution)/shard_map/pallas_call | solution.py:452
  22.2 1.4 %collective-permute-start.4 = (bf16[48,512]{1,0:T(8,128)(2,1)S(1)}, bf16[48,512]{1,0:T(8,128)(2,1)S(1)}, u32[]{:S(2)}, u32[]{:S(2)}) collective-permute-start(bf16[48,512]{1,0:T(8,128)(2,1)S(1)} %get-tuple-element.51), channel_id=1, source_target_pairs={{0,12},{4,8},{8,4},{12,0},{1,13},{5,9},{9,5},{13,1},{2,14},{6,10},... | collective-permute-start | bytes 147464 | tf_op jit(solution)/shard_map/ppermute | solution.py:378
  23.6 0.0 collective-permute-start.5
  23.6 3.0 %collective-permute-start.6 = (bf16[33,512]{1,0:T(8,128)(2,1)S(1)}, bf16[33,512]{1,0:T(8,128)(2,1)S(1)}, u32[]{:S(2)}, u32[]{:S(2)}) collective-permute-start(bf16[33,512]{1,0:T(8,128)(2,1)S(1)} %get-tuple-element.49.sums), channel_id=1, source_target_pairs={{0,8},{4,12},{8,0},{12,4},{1,9},{5,13},{9,1},{13,5},{2,10},{6,14},... | collective-permute-start | bytes 101384 | tf_op jit(solution)/shard_map/ppermute | solution.py:378
  26.7 2.1 %shard_map.149 = (bf16[128,1024]{1,0:T(8,128)(2,1)}, bf16[33,512]{1,0:T(8,128)(2,1)S(1)}) custom-call(f32[31,512]{1,0:T(8,128)S(1)} %get-tuple-element.38.refs_6_.kernel, f32[1,1024]{1,0:T(1,128)S(1)} %get-tuple-element.36.refs_4_.norm_gain, bf16[1024,1024]{1,0:T(8,128)(2,1)S(1)} %get-tuple-element.37.refs_5_.w_in, ...), custom_call_target="tpu_custom_call" | custom-call | tf_op jit(solution)/shard_map/pallas_call | solution.py:488
  28.7 0.2 collective-permute-done.6
  28.9 0.0 collective-permute-done.4.from_b
  28.9 0.0 collective-permute-done.5.from_a
  29.0 0.1 collective-permute-start.9
  29.1 1.6 %collective-permute-start.8 = (bf16[33,512]{1,0:T(8,128)(2,1)S(1)}, bf16[33,512]{1,0:T(8,128)(2,1)S(1)}, u32[]{:S(2)}, u32[]{:S(2)}) collective-permute-start(bf16[33,512]{1,0:T(8,128)(2,1)S(1)} %add_convert_fusion.one), channel_id=1, source_target_pairs={{0,2},{1,3},{2,0},{3,1},{4,6},{5,7},{6,4},{7,5},{8,10},{9,11},{10,... | collective-permute-start | bytes 101384 | tf_op jit(solution)/shard_map/ppermute | solution.py:378
  30.6 0.3 collective-permute-start.7
  30.9 1.6 %shard_map.150 = bf16[128,1024]{1,0:T(8,128)(2,1)} custom-call(bf16[128,1024]{1,0:T(8,128)(2,1)} %get-tuple-element.50.inner, bf16[48,512]{1,0:T(8,128)(2,1)S(1)} %collective-permute-done.4.from_b, bf16[48,512]{1,0:T(8,128)(2,1)S(1)} %collective-permute-done.5.from_a, ...), custom_call_target="tpu_custom_call", output_to_operand_aliasing={{}: (0, {})} | custom-call | tf_op jit(solution)/shard_map/pallas_call | solution.py:512
  32.5 0.4 %collective-permute-done.9.four = bf16[33,512]{1,0:T(8,128)(2,1)S(1)} collective-permute-done((bf16[33,512]{1,0:T(8,128)(2,1)S(1)}, bf16[33,512]{1,0:T(8,128)(2,1)S(1)}, u32[]{:S(2)}, u32[]{:S(2)}) %collective-permute-start.9) | collective-permute-done | bytes 33824 | tf_op jit(solution)/shard_map/ppermute | solution.py:378
  32.9 0.6 %collective-permute-done.8.three = bf16[33,512]{1,0:T(8,128)(2,1)S(1)} collective-permute-done((bf16[33,512]{1,0:T(8,128)(2,1)S(1)}, bf16[33,512]{1,0:T(8,128)(2,1)S(1)}, u32[]{:S(2)}, u32[]{:S(2)}) %collective-permute-start.8) | collective-permute-done | bytes 33824 | tf_op jit(solution)/shard_map/ppermute | solution.py:378
  33.4 0.0 collective-permute-done.7.two
  33.4 0.7 %shard_map.151 = (f32[31,512]{1,0:T(8,128)}, f32[1,512]{1,0:T(1,128)}, f32[1,512]{1,0:T(1,128)}) custom-call(bf16[33,512]{1,0:T(8,128)(2,1)S(1)} %add_convert_fusion.one, bf16[33,512]{1,0:T(8,128)(2,1)S(1)} %collective-permute-done.7.two, bf16[33,512]{1,0:T(8,128)(2,1)S(1)} %collective-permute-done.8.three, bf16[33,512]{1,0:T(8,128)(2,1)S(1)} %collective-permute-done.9.four), custom_call_target="tpu_custom_call" | custom-call | tf_op jit(solution)/shard_map/pallas_call | solution.py:531
  (1 shorter events, 0.0 us)
Async XLA Ops:
  1.9 16.3 %collective-permute-start.2 = (bf16[112,512]{1,0:T(8,128)(2,1)S(1)}, bf16[112,512]{1,0:T(8,128)(2,1)S(1)}, u32[]{:S(2)}, u32[]{:S(2)}) collective-permute-start(bf16[112,512]{1,0:T(8,128)(2,1)S(1)} %get-tuple-element.41), channel_id=1, source_target_pairs={{4,8},{8,4},{5,9},{9,5},{6,10},{10,6},{7,11},{11,7},{20,24},{24,20... | collective-permute-start | bytes 344072 | tf_op jit(solution)/shard_map/ppermute | solution.py:426
  2.6 15.7 %collective-permute-start.3 = (bf16[112,512]{1,0:T(8,128)(2,1)S(1)}, bf16[112,512]{1,0:T(8,128)(2,1)S(1)}, u32[]{:S(2)}, u32[]{:S(2)}) collective-permute-start(bf16[112,512]{1,0:T(8,128)(2,1)S(1)} %get-tuple-element.42), channel_id=1, source_target_pairs={{0,4},{4,0},{8,12},{12,8},{1,5},{5,1},{9,13},{13,9},{2,6},{6,2},{1... | collective-permute-start | bytes 344072 | tf_op jit(solution)/shard_map/ppermute | solution.py:378
  8.5 8.0 %collective-permute-start.1 = (bf16[64,512]{1,0:T(8,128)(2,1)S(1)}, bf16[64,512]{1,0:T(8,128)(2,1)S(1)}, u32[]{:S(2)}, u32[]{:S(2)}) collective-permute-start(bf16[64,512]{1,0:T(8,128)(2,1)S(1)} %get-tuple-element.31.after.refs_9_), channel_id=1, source_target_pairs={{0,12},{12,0},{1,13},{13,1},{2,14},{14,2},{3,15},{15,3},{16,28},{2... | collective-permute-start | bytes 196616 | tf_op jit(solution)/shard_map/ppermute | solution.py:428
  11.8 6.5 %collective-permute-start = (bf16[64,512]{1,0:T(8,128)(2,1)S(1)}, bf16[64,512]{1,0:T(8,128)(2,1)S(1)}, u32[]{:S(2)}, u32[]{:S(2)}) collective-permute-start(bf16[64,512]{1,0:T(8,128)(2,1)S(1)} %get-tuple-element.31.after.refs_9_), channel_id=1, source_target_pairs={{0,8},{4,12},{8,0},{12,4},{1,9},{5,13},{9,1},{13,5},{2,10},{6,14},... | collective-permute-start | bytes 196616 | tf_op jit(solution)/shard_map/ppermute | solution.py:378
  22.2 6.7 %collective-permute-start.4 = (bf16[48,512]{1,0:T(8,128)(2,1)S(1)}, bf16[48,512]{1,0:T(8,128)(2,1)S(1)}, u32[]{:S(2)}, u32[]{:S(2)}) collective-permute-start(bf16[48,512]{1,0:T(8,128)(2,1)S(1)} %get-tuple-element.51), channel_id=1, source_target_pairs={{0,12},{4,8},{8,4},{12,0},{1,13},{5,9},{9,5},{13,1},{2,14},{6,10},... | collective-permute-start | bytes 147464 | tf_op jit(solution)/shard_map/ppermute | solution.py:378
  23.6 5.3 %collective-permute-start.5 = (bf16[48,512]{1,0:T(8,128)(2,1)S(1)}, bf16[48,512]{1,0:T(8,128)(2,1)S(1)}, u32[]{:S(2)}, u32[]{:S(2)}) collective-permute-start(bf16[48,512]{1,0:T(8,128)(2,1)S(1)} %get-tuple-element.52), channel_id=1, source_target_pairs={{0,4},{4,0},{8,12},{12,8},{1,5},{5,1},{9,13},{13,9},{2,6},{6,2},{1... | collective-permute-start | bytes 147464 | tf_op jit(solution)/shard_map/ppermute | solution.py:378
  23.6 5.3 %collective-permute-start.6 = (bf16[33,512]{1,0:T(8,128)(2,1)S(1)}, bf16[33,512]{1,0:T(8,128)(2,1)S(1)}, u32[]{:S(2)}, u32[]{:S(2)}) collective-permute-start(bf16[33,512]{1,0:T(8,128)(2,1)S(1)} %get-tuple-element.49.sums), channel_id=1, source_target_pairs={{0,8},{4,12},{8,0},{12,4},{1,9},{5,13},{9,1},{13,5},{2,10},{6,14},... | collective-permute-start | bytes 101384 | tf_op jit(solution)/shard_map/ppermute | solution.py:378
  29.0 3.9 %collective-permute-start.9 = (bf16[33,512]{1,0:T(8,128)(2,1)S(1)}, bf16[33,512]{1,0:T(8,128)(2,1)S(1)}, u32[]{:S(2)}, u32[]{:S(2)}) collective-permute-start(bf16[33,512]{1,0:T(8,128)(2,1)S(1)} %add_convert_fusion.one), channel_id=1, source_target_pairs={{0,3},{1,2},{2,1},{3,0},{4,7},{5,6},{6,5},{7,4},{8,11},{9,10},{10,... | collective-permute-start | bytes 101384 | tf_op jit(solution)/shard_map/ppermute | solution.py:378
  29.1 4.4 %collective-permute-start.8 = (bf16[33,512]{1,0:T(8,128)(2,1)S(1)}, bf16[33,512]{1,0:T(8,128)(2,1)S(1)}, u32[]{:S(2)}, u32[]{:S(2)}) collective-permute-start(bf16[33,512]{1,0:T(8,128)(2,1)S(1)} %add_convert_fusion.one), channel_id=1, source_target_pairs={{0,2},{1,3},{2,0},{3,1},{4,6},{5,7},{6,4},{7,5},{8,10},{9,11},{10,... | collective-permute-start | bytes 101384 | tf_op jit(solution)/shard_map/ppermute | solution.py:378
  30.6 2.8 %collective-permute-start.7 = (bf16[33,512]{1,0:T(8,128)(2,1)S(1)}, bf16[33,512]{1,0:T(8,128)(2,1)S(1)}, u32[]{:S(2)}, u32[]{:S(2)}) collective-permute-start(bf16[33,512]{1,0:T(8,128)(2,1)S(1)} %add_convert_fusion.one), channel_id=1, source_target_pairs={{0,1},{1,0},{2,3},{3,2},{4,5},{5,4},{6,7},{7,6},{8,9},{9,8},{10,11... | collective-permute-start | bytes 101384 | tf_op jit(solution)/shard_map/ppermute | solution.py:378

commit v5 on v4

--- a/solution.py
+++ b/solution.py
@@ -55,7 +55,7 @@
         load.start()
     edges = []
     for target, near in ((to_a, True), (to_b, False)):
-        at = 2 * pooled
+        at = 2 * pooled if near else 0
         start = jnp.where(swap, 0 if near else frames - HALO, frames - HALO if near else 0)
         start = pl.multiple_of(start.astype(jnp.int32), HALO)
         for source, column in [(query, 0)] + [(resid, c) for c in range(0, model, width)]:
@@ -77,7 +77,6 @@
         rows = pl.ds(place * pooled, pooled)
         own[rows, :] = block
         to_a[rows, :] = block
-        to_b[rows, :] = block
     for edge in edges:
         edge.wait()
 
@@ -116,26 +115,26 @@
 
     pooled = frames // POOL
     if pairwise:
-        own, far, ends = kvs
-        middle = (me == 1) | (me == 2)
+        own, far, across = kvs
         for side, target in enumerate((k_all, v_all)):
             rows_in = pl.ds(side * pooled, pooled)
             target[0:pooled, :] = own[rows_in, :]
             target[pooled : 2 * pooled, :] = from_a[rows_in, :]
             target[2 * pooled : 3 * pooled, :] = far[rows_in, :]
-            target[3 * pooled :, :] = jnp.where(middle, from_b[rows_in, :], ends[rows_in, :])
+            target[3 * pooled :, :] = across[rows_in, :]
     else:
         for source, target in zip(kvs, (k_all, v_all)):
             target[...] = source[...]
     keylen = count * pooled
     q_all[main, :] = query[...]
+    at_a = 2 * pooled if pairwise else 0
     for left_side in (True, False):
         edge_rows = pl.ds(0 if left_side else HALO + frames, HALO)
         r_rows = pl.ds(0 if left_side else HALO, HALO)
 
         def pick(start):
-            a = from_a[pl.ds(2 * pooled + start, HALO), :]
-            b = from_b[pl.ds(2 * pooled + start, HALO), :]
+            a = from_a[pl.ds(at_a + start, HALO), :]
+            b = from_b[pl.ds(start, HALO), :]
             return jnp.where(swap, a, b) if left_side else jnp.where(swap, b, a)
 
         q_all[edge_rows, :] = pick(0)
@@ -148,21 +147,33 @@
     ones_low = jnp.where(low, 1.0, 0.0).astype(BF16)
     ones_high = jnp.where(low, 0.0, 1.0).astype(BF16)
     scale = 1.0 / math.sqrt(HEAD_DIM)
-    for pair in range(width // LANES):
+    pairs = width // LANES
+
+    def score(pair):
         cols = pl.ds(pair * LANES, LANES)
         k_pair = k_all[:, cols]
+        k_both = jnp.concatenate([jnp.where(low, k_pair, zero), jnp.where(low, zero, k_pair)], axis=0)
+        return dot_t(q_all[:, cols], k_both)
+
+    upcoming = score(0)
+    for pair in range(pairs):
+        cols = pl.ds(pair * LANES, LANES)
+        scores = upcoming
+        if pair + 1 < pairs:
+            upcoming = score(pair + 1)
         v_pair = v_all[:, cols]
-        q_pair = q_all[:, cols]
-        weighted = None
-        for keep_low in (True, False):
-            k_head = jnp.where(low, k_pair, zero) if keep_low else jnp.where(low, zero, k_pair)
-            v_head = jnp.where(low, v_pair, zero) if keep_low else jnp.where(low, zero, v_pair)
-            ones = ones_low if keep_low else ones_high
-            scores = dot_t(q_pair, k_head)
-            top = jnp.max(scores, axis=-1, keepdims=True)
-            probs = jnp.exp((scores - top) * scale).astype(BF16)
-            part = dot(probs, jnp.concatenate([v_head, ones], axis=1))
-            weighted = part if weighted is None else weighted + part
+        probs = []
+        for half in (scores[:, :keylen], scores[:, keylen:]):
+            top = jnp.max(half, axis=-1, keepdims=True)
+            probs.append(jnp.exp((half - top) * scale).astype(BF16))
+        v_both = jnp.concatenate(
+            [
+                jnp.concatenate([jnp.where(low, v_pair, zero), ones_low], axis=1),
+                jnp.concatenate([jnp.where(low, zero, v_pair), ones_high], axis=1),
+            ],
+            axis=0,
+        )
+        weighted = dot(jnp.concatenate(probs, axis=1), v_both)
         att[:, cols] = (weighted[:, :LANES] / weighted[:, LANES:]).astype(BF16)
 
     step = 256
@@ -186,25 +197,27 @@
         x_norm[r : r + 32, :] = x
         inv_norm[r : r + 32, :] = jnp.broadcast_to(inv, (32, LANES))
 
-    for n in range(2 * channels // step):
-        cols = pl.ds(n * step, step)
-        glu[:, cols] = dot(normed[...], w_in[:, cols])
-    for r in range(0, rows, 16):
-        left = glu[r : r + 16, 0:channels]
-        sig = jax.nn.sigmoid(glu[r : r + 16, channels:])
-        out = (left * sig).astype(BF16).astype(F32)
-        if r < HALO:
-            out = jnp.where(first, 0.0, out)
-        elif r >= HALO + frames:
-            out = jnp.where(last, 0.0, out)
-        else:
-            left_out[r - HALO : r - HALO + 16, :] = left
-            sig_out[r - HALO : r - HALO + 16, :] = sig
-        for c in range(channels // LANES):
-            gated[c, r : r + 16, :] = out[:, c * LANES : (c + 1) * LANES]
-
+    def project(c):
+        pair = [w_in[:, at + c * LANES : at + (c + 1) * LANES] for at in (0, channels)]
+        glu[c] = dot(normed[...], jnp.concatenate(pair, axis=1))
+
+    project(0)
     for c in range(channels // LANES):
         cols = slice(c * LANES, (c + 1) * LANES)
+        if (c + 1) * LANES < channels:
+            project(c + 1)
+        for r in range(0, rows, 16):
+            left = glu[c, r : r + 16, 0:LANES]
+            sig = jax.nn.sigmoid(glu[c, r : r + 16, LANES:])
+            out = (left * sig).astype(BF16).astype(F32)
+            if r < HALO:
+                out = jnp.where(first, 0.0, out)
+            elif r >= HALO + frames:
+                out = jnp.where(last, 0.0, out)
+            else:
+                left_out[r - HALO : r - HALO + 16, cols] = left
+                sig_out[r - HALO : r - HALO + 16, cols] = sig
+            gated[c, r : r + 16, :] = out
         acc = jnp.zeros((frames, LANES), F32)
         for t in range(n_taps):
             acc = acc + kernel[t : t + 1, cols] * gated[c, pl.ds(HALO + t - rim, frames), :]
@@ -288,8 +301,8 @@
 
 
 def inner_kernel(
-    kernel, norm_gain, w_in, x_norm, inv_norm, left, sig, d_conv, sums, d_hidden, sums_out, d_glu,
-    d_normed, out, sem,
+    kernel, norm_gain, w_in, x_norm, inv_norm, left, sig, d_conv, sums, out, sums_out, d_glu,
+    d_normed,
 ):
     sums_out[...] = sums[...]
     rows = out.shape[0]
@@ -305,9 +318,6 @@
     )
     for r, block in blocks:
         out[r : r + 32, :] = block
-    write = pltpu.make_async_copy(out, d_hidden.at[pl.ds(HALO, rows), :], sem)
-    write.start()
-    write.wait()
 
 
 def edge_kernel(
@@ -320,6 +330,8 @@
     me = lax.axis_index("ctx")
     swap = swapped(pairwise)
     used = n_taps + 2
+    writes = [pltpu.make_async_copy(inner, d_hidden.at[pl.ds(HALO, inner.shape[0]), :], sem.at[2])]
+    writes[0].start()
     edges[0] = from_a[...].astype(F32)
     edges[1] = from_b[...].astype(F32)
     for c in range(channels // LANES):
@@ -349,7 +361,7 @@
     )
     for r, block in blocks:
         out[...] = block
-    writes = [
+    writes += [
         pltpu.make_async_copy(
             out.at[pl.ds(i * HALO, HALO), :],
             d_hidden.at[pl.ds(i * (frames - HALO), HALO), :],
@@ -357,7 +369,7 @@
         )
         for i in range(2)
     ]
-    for write in writes:
+    for write in writes[1:]:
         write.start()
     for write in writes:
         write.wait()
@@ -410,7 +422,7 @@
         out_shape=(
             shape((2 * pooled, width), BF16),
             shape((message, width), BF16),
-            shape((message, width), BF16),
+            shape((message - 2 * pooled, width), BF16),
         ),
         in_specs=[HBM] * 4,
         out_specs=(VMEM,) * 3,
@@ -423,13 +435,12 @@
     )(*in_hbm(keys, values, query, resid))
 
     if pairwise:
+        (from_a,) = flips(to_a, "ctx", (1,))
+        far, across = flips(own, "ctx", (2, 3))
         from_b = lax.ppermute(to_b, "ctx", [(1, 2), (2, 1)])
-        (from_a,) = flips(to_a, "ctx", (1,))
-        ends = lax.ppermute(own, "ctx", [(0, 3), (3, 0)])
-        (far,) = flips(own, "ctx", (2,))
-        kvs = (own, far, ends)
+        kvs = (own, far, across)
     else:
-        from_a, from_b = to_neighbours(pairwise, ctx, to_a, to_b)
+        from_a, from_b = to_neighbours(pairwise, ctx, to_a[2 * pooled :], to_b)
         kvs = tuple(
             lax.all_gather(part, "ctx", axis=0, tiled=True) for part in (own[:pooled], own[pooled:])
         )
@@ -474,7 +485,7 @@
             pltpu.VMEM((rows, model), BF16),
             pltpu.VMEM((channels // LANES, rows, LANES), F32),
             pltpu.VMEM((frames, channels), F32),
-            pltpu.VMEM((rows, 2 * channels), F32),
+            pltpu.VMEM((channels // LANES, rows, 2 * LANES), F32),
             pltpu.VMEM((n_taps * 8, LANES), F32),
             pltpu.VMEM((frames, channels), BF16),
             pltpu.VMEM((used + rim, channels), F32),
@@ -487,14 +498,12 @@
     common = (kernel, norm_gain, w_in, x_norm, inv_norm, left, sig, d_conv)
     d_inner, same_sums = pl.pallas_call(
         inner_kernel,
-        out_shape=(shape((frames, model), BF16), shape(sums.shape, sums.dtype)),
+        out_shape=(shape((inner, model), BF16), shape(sums.shape, sums.dtype)),
         in_specs=[VMEM] * 9,
-        out_specs=(HBM, VMEM),
+        out_specs=(VMEM, VMEM),
         scratch_shapes=[
             pltpu.VMEM((inner, 2 * channels), BF16),
             pltpu.VMEM((inner, model), F32),
-            pltpu.VMEM((inner, model), BF16),
-            pltpu.SemaphoreType.DMA,
         ],
         compiler_params=pltpu.CompilerParams(vmem_limit_bytes=16 * 2**20),
     )(*common, sums)
@@ -512,16 +521,15 @@
     d_hidden = pl.pallas_call(
         functools.partial(edge_kernel, pairwise, ctx),
         out_shape=shape((frames, model), BF16),
-        in_specs=[HBM] + [VMEM] * 10,
+        in_specs=[VMEM] * 11,
         out_specs=HBM,
-        input_output_aliases={0: 0},
         scratch_shapes=[
             pltpu.VMEM((2, channels // LANES, 3 * HALO, LANES), F32),
             pltpu.VMEM((2, used + rim, channels), F32),
             pltpu.VMEM((2 * HALO, 2 * channels), BF16),
             pltpu.VMEM((2 * HALO, model), F32),
             pltpu.VMEM((2 * HALO, model), BF16),
-            pltpu.SemaphoreType.DMA((2,)),
+            pltpu.SemaphoreType.DMA((3,)),
         ],
         compiler_params=pltpu.CompilerParams(vmem_limit_bytes=16 * 2**20),
     )(d_inner, from_b, from_a, *common)

time: 34.3 us -> 30.8 us (0.90)
  starting transfers between devices: 16.3 us -> 12.7 us
  waiting for transfers between devices: 5.31 us -> 6.68 us
  Pallas kernels: 11.8 us -> 10.5 us
    ppermute x8 -> x9, waiting for transfers between devices: 2.94 us -> 6.68 us  [flips(): lax.ppermute(array, axis, [(i, i ^ k) for i in range(4)])]
    ppermute x1 -> x0, starting transfers between devices: 3.24 us -> none  [per_device(): ends = lax.ppermute(own, 'ctx', [(0, 3), (3, 0)])]
    ppermute x1 -> x0, waiting for transfers between devices: 2.37 us -> none  [per_device(): ends = lax.ppermute(own, 'ctx', [(0, 3), (3, 0)])]
    pallas_call x1, Pallas kernels: 2.08 us -> 1.39 us  [per_device(): pl.pallas_call(inner_kernel, out_shape=(shape((inner, model), BF16), shap...]
    pallas_call x1, Pallas kernels: 3.92 us -> 3.38 us  [per_device(): pl.pallas_call(functools.partial(main_kernel, pairwise, ctx, len(kvs)), o...]
    ppermute x8 -> x9, starting transfers between devices: 12.3 us -> 12.1 us  [flips(): lax.ppermute(array, axis, [(i, i ^ k) for i in range(4)])]
where the time goes in v5:
time: 30.8 us; the launch traced here: 30.7 us
  starting transfers between devices  12.7 us (41%)
  Pallas kernels  10.5 us (34%)
  waiting for transfers between devices  6.68 us (22%)
  between operations  0.71 us (2%)
    ppermute x9, starting transfers between devices, flips(): lax.ppermute(array, axis, [(i, i ^ k) for i in range(4)])  12.1 us
    ppermute x9, waiting for transfers between devices, flips(): lax.ppermute(array, axis, [(i, i ^ k) for i in range(4)])  6.68 us
    pallas_call x1, Pallas kernels, per_device(): pl.pallas_call(functools.partial(main_kernel, pairwise, ctx, len(kvs)), o...  3.38 us
    pallas_call x1, Pallas kernels, per_device(): pl.pallas_call(functools.partial(fetch_kernel, len(operands)), out_shape=...  2.25 us
    pallas_call x1, Pallas kernels, per_device(): pl.pallas_call(functools.partial(edge_kernel, pairwise, ctx), out_shape=s...  1.6 us
    pallas_call x1, Pallas kernels, per_device(): pl.pallas_call(inner_kernel, out_shape=(shape((inner, model), BF16), shap...  1.39 us
    pallas_call x1, Pallas kernels, per_device(): pl.pallas_call(functools.partial(pack_kernel, pairwise), out_shape=(shape...  1.28 us
    pallas_call x1, Pallas kernels, per_device(): pl.pallas_call(functools.partial(total_kernel, factor), out_shape=(shape(...  0.65 us
  transfers between devices with their start and end apart: 10, of which 5 were waited for; matrix products, arithmetic and copies ran while one was open for 0% of the time, Pallas kernels for 17%

profile of v5, /device:TPU:0, one launch (start us, length us, event | category | flops | bytes accessed | tf_op | source)
XLA Modules:
  0.0 30.7 jit_solution(8162487801043250945)
XLA Ops:
  0.6 1.3 %shard_map.146 = (bf16[64,512]{1,0:T(8,128)(2,1)S(1)}, bf16[112,512]{1,0:T(8,128)(2,1)S(1)}, bf16[48,512]{1,0:T(8,128)(2,1)S(1)}) custom-call(bf16[128,512]{1,0:T(8,128)(2,1)} %bitcast.17, bf16[128,512]{1,0:T(8,128)(2,1)} %bitcast.18, bf16[128,512]{1,0:T(8,128)(2,1)} %bitcast.14, bf16[128,1024]{1,0:T(8,128)(2,1)} %bitcast.12), custom_call_target="tpu_custom_call" | custom-call | tf_op jit(solution)/shard_map/pallas_call | solution.py:420
  1.9 3.1 %collective-permute-start.3 = (bf16[112,512]{1,0:T(8,128)(2,1)S(1)}, bf16[112,512]{1,0:T(8,128)(2,1)S(1)}, u32[]{:S(2)}, u32[]{:S(2)}) collective-permute-start(bf16[112,512]{1,0:T(8,128)(2,1)S(1)} %get-tuple-element.42), channel_id=1, source_target_pairs={{0,4},{4,0},{8,12},{12,8},{1,5},{5,1},{9,13},{13,9},{2,6},{6,2},{1... | collective-permute-start | bytes 344072 | tf_op jit(solution)/shard_map/ppermute | solution.py:390
  5.0 2.5 %collective-permute-start.1 = (bf16[64,512]{1,0:T(8,128)(2,1)S(1)}, bf16[64,512]{1,0:T(8,128)(2,1)S(1)}, u32[]{:S(2)}, u32[]{:S(2)}) collective-permute-start(bf16[64,512]{1,0:T(8,128)(2,1)S(1)} %get-tuple-element.31.after.refs_9_), channel_id=1, source_target_pairs={{0,12},{4,8},{8,4},{12,0},{1,13},{5,9},{9,5},{13,1},{2,14},{6,10},... | collective-permute-start | bytes 196616 | tf_op jit(solution)/shard_map/ppermute | solution.py:390
  7.5 0.1 collective-permute-start
  7.6 0.7 %collective-permute-start.2 = (bf16[48,512]{1,0:T(8,128)(2,1)S(1)}, bf16[48,512]{1,0:T(8,128)(2,1)S(1)}, u32[]{:S(2)}, u32[]{:S(2)}) collective-permute-start(bf16[48,512]{1,0:T(8,128)(2,1)S(1)} %get-tuple-element.41), channel_id=1, source_target_pairs={{4,8},{8,4},{5,9},{9,5},{6,10},{10,6},{7,11},{11,7},{20,24},{24,20... | collective-permute-start | bytes 147464 | tf_op jit(solution)/shard_map/ppermute | solution.py:440
  8.3 2.2 %shard_map.147 = (bf16[128,512]{1,0:T(8,128)(2,1)S(1)}, bf16[128,1024]{1,0:T(8,128)(2,1)S(1)}, bf16[128,512]{1,0:T(8,128)(2,1)S(1)}, bf16[512,1024]{1,0:T(8,128)...) custom-call(bf16[64,512]{1,0:T(8,128)(2,1)S(1)} %get-tuple-element.3, ...), custom_call_target="tpu_custom_call" | custom-call | tf_op jit(solution)/shard_map/pallas_call | solution.py:451
  10.5 0.0 collective-permute-done.2.refs_12_
  10.5 2.0 %collective-permute-done.1.refs_11_ = bf16[64,512]{1,0:T(8,128)(2,1)S(1)} collective-permute-done((bf16[64,512]{1,0:T(8,128)(2,1)S(1)}, bf16[64,512]{1,0:T(8,128)(2,1)S(1)}, u32[]{:S(2)}, u32[]{:S(2)}) %collective-permute-start.1) | collective-permute-done | bytes 65568 | tf_op jit(solution)/shard_map/ppermute | solution.py:390
  12.5 2.0 %collective-permute-done.refs_10_ = bf16[64,512]{1,0:T(8,128)(2,1)S(1)} collective-permute-done((bf16[64,512]{1,0:T(8,128)(2,1)S(1)}, bf16[64,512]{1,0:T(8,128)(2,1)S(1)}, u32[]{:S(2)}, u32[]{:S(2)}) %collective-permute-start) | collective-permute-done | bytes 65568 | tf_op jit(solution)/shard_map/ppermute | solution.py:390
  14.6 0.0 collective-permute-done.3.refs_13_
  14.6 3.4 %shard_map.148 = (bf16[128,512]{1,0:T(8,128)(2,1)}, f32[160,1024]{1,0:T(8,128)S(1)}, f32[160,128]{1,0:T(8,128)S(1)}, f32[128,512]{1,0:T(8,128)S(1)}, f32[128,512...) custom-call(bf16[128,512]{1,0:T(8,128)(2,1)S(1)} %get-tuple-element., ...), custom_call_target="tpu_custom_call" | custom-call | tf_op jit(solution)/shard_map/pallas_call | solution.py:463
  18.0 2.4 %collective-permute-start.4 = (bf16[48,512]{1,0:T(8,128)(2,1)S(1)}, bf16[48,512]{1,0:T(8,128)(2,1)S(1)}, u32[]{:S(2)}, u32[]{:S(2)}) collective-permute-start(bf16[48,512]{1,0:T(8,128)(2,1)S(1)} %get-tuple-element.51), channel_id=1, source_target_pairs={{0,12},{4,8},{8,4},{12,0},{1,13},{5,9},{9,5},{13,1},{2,14},{6,10},... | collective-permute-start | bytes 147464 | tf_op jit(solution)/shard_map/ppermute | solution.py:390
  20.4 0.2 collective-permute-start.5
  20.6 1.8 %collective-permute-start.6 = (bf16[33,512]{1,0:T(8,128)(2,1)S(1)}, bf16[33,512]{1,0:T(8,128)(2,1)S(1)}, u32[]{:S(2)}, u32[]{:S(2)}) collective-permute-start(bf16[33,512]{1,0:T(8,128)(2,1)S(1)} %get-tuple-element.49.sums), channel_id=1, source_target_pairs={{0,8},{4,12},{8,0},{12,4},{1,9},{5,13},{9,1},{13,5},{2,10},{6,14},... | collective-permute-start | bytes 101384 | tf_op jit(solution)/shard_map/ppermute | solution.py:390
  22.4 1.4 %shard_map.149 = (bf16[96,1024]{1,0:T(8,128)(2,1)S(1)}, bf16[33,512]{1,0:T(8,128)(2,1)S(1)}) custom-call(f32[31,512]{1,0:T(8,128)S(1)} %get-tuple-element.38.refs_6_.kernel, f32[1,1024]{1,0:T(1,128)S(1)} %get-tuple-element.36.refs_4_.norm_gain, bf16[1024,1024]{1,0:T(8,128)(2,1)S(1)} %get-tuple-element.37.refs_5_.w_in, ...), custom_call_target="tpu_custom_call" | custom-call | tf_op jit(solution)/shard_map/pallas_call | solution.py:499
  23.8 1.7 %collective-permute-done.6 = bf16[33,512]{1,0:T(8,128)(2,1)S(1)} collective-permute-done((bf16[33,512]{1,0:T(8,128)(2,1)S(1)}, bf16[33,512]{1,0:T(8,128)(2,1)S(1)}, u32[]{:S(2)}, u32[]{:S(2)}) %collective-permute-start.6) | collective-permute-done | bytes 33824 | tf_op jit(solution)/shard_map/ppermute | solution.py:390
  25.5 0.0 collective-permute-done.4.from_b
  25.5 0.0 collective-permute-done.5.from_a
  25.6 0.1 collective-permute-start.9
  25.6 1.6 %collective-permute-start.8 = (bf16[33,512]{1,0:T(8,128)(2,1)S(1)}, bf16[33,512]{1,0:T(8,128)(2,1)S(1)}, u32[]{:S(2)}, u32[]{:S(2)}) collective-permute-start(bf16[33,512]{1,0:T(8,128)(2,1)S(1)} %add_convert_fusion.one), channel_id=1, source_target_pairs={{0,2},{1,3},{2,0},{3,1},{4,6},{5,7},{6,4},{7,5},{8,10},{9,11},{10,... | collective-permute-start | bytes 101384 | tf_op jit(solution)/shard_map/ppermute | solution.py:390
  27.2 0.3 collective-permute-start.7
  27.5 1.6 %shard_map.150 = bf16[128,1024]{1,0:T(8,128)(2,1)} custom-call(bf16[96,1024]{1,0:T(8,128)(2,1)S(1)} %get-tuple-element.50.inner, bf16[48,512]{1,0:T(8,128)(2,1)S(1)} %collective-permute-done.4.from_b, bf16[48,512]{1,0:T(8,128)(2,1)S(1)} %collective-permute-done.5.from_a, f32[31,512]{1,0:T(8,128)S(1)} %get-tuple-element.38.refs_6_.kernel, ...), custom_call_target="tpu_custom_call" | custom-call | tf_op jit(solution)/shard_map/pallas_call | solution.py:521
  29.1 0.3 %collective-permute-done.9.four = bf16[33,512]{1,0:T(8,128)(2,1)S(1)} collective-permute-done((bf16[33,512]{1,0:T(8,128)(2,1)S(1)}, bf16[33,512]{1,0:T(8,128)(2,1)S(1)}, u32[]{:S(2)}, u32[]{:S(2)}) %collective-permute-start.9) | collective-permute-done | bytes 33824 | tf_op jit(solution)/shard_map/ppermute | solution.py:390
  29.4 0.6 %collective-permute-done.8.three = bf16[33,512]{1,0:T(8,128)(2,1)S(1)} collective-permute-done((bf16[33,512]{1,0:T(8,128)(2,1)S(1)}, bf16[33,512]{1,0:T(8,128)(2,1)S(1)}, u32[]{:S(2)}, u32[]{:S(2)}) %collective-permute-start.8) | collective-permute-done | bytes 33824 | tf_op jit(solution)/shard_map/ppermute | solution.py:390
  30.0 0.0 collective-permute-done.7.two
  30.0 0.7 %shard_map.151 = (f32[31,512]{1,0:T(8,128)}, f32[1,512]{1,0:T(1,128)}, f32[1,512]{1,0:T(1,128)}) custom-call(bf16[33,512]{1,0:T(8,128)(2,1)S(1)} %add_convert_fusion.one, bf16[33,512]{1,0:T(8,128)(2,1)S(1)} %collective-permute-done.7.two, bf16[33,512]{1,0:T(8,128)(2,1)S(1)} %collective-permute-done.8.three, bf16[33,512]{1,0:T(8,128)(2,1)S(1)} %collective-permute-done.9.four), custom_call_target="tpu_custom_call" | custom-call | tf_op jit(solution)/shard_map/pallas_call | solution.py:539
  (1 shorter events, 0.0 us)
Async XLA Ops:
  1.9 12.7 %collective-permute-start.3 = (bf16[112,512]{1,0:T(8,128)(2,1)S(1)}, bf16[112,512]{1,0:T(8,128)(2,1)S(1)}, u32[]{:S(2)}, u32[]{:S(2)}) collective-permute-start(bf16[112,512]{1,0:T(8,128)(2,1)S(1)} %get-tuple-element.42), channel_id=1, source_target_pairs={{0,4},{4,0},{8,12},{12,8},{1,5},{5,1},{9,13},{13,9},{2,6},{6,2},{1... | collective-permute-start | bytes 344072 | tf_op jit(solution)/shard_map/ppermute | solution.py:390
  5.0 7.5 %collective-permute-start.1 = (bf16[64,512]{1,0:T(8,128)(2,1)S(1)}, bf16[64,512]{1,0:T(8,128)(2,1)S(1)}, u32[]{:S(2)}, u32[]{:S(2)}) collective-permute-start(bf16[64,512]{1,0:T(8,128)(2,1)S(1)} %get-tuple-element.31.after.refs_9_), channel_id=1, source_target_pairs={{0,12},{4,8},{8,4},{12,0},{1,13},{5,9},{9,5},{13,1},{2,14},{6,10},... | collective-permute-start | bytes 196616 | tf_op jit(solution)/shard_map/ppermute | solution.py:390
  7.5 7.1 %collective-permute-start = (bf16[64,512]{1,0:T(8,128)(2,1)S(1)}, bf16[64,512]{1,0:T(8,128)(2,1)S(1)}, u32[]{:S(2)}, u32[]{:S(2)}) collective-permute-start(bf16[64,512]{1,0:T(8,128)(2,1)S(1)} %get-tuple-element.31.after.refs_9_), channel_id=1, source_target_pairs={{0,8},{4,12},{8,0},{12,4},{1,9},{5,13},{9,1},{13,5},{2,10},{6,14},... | collective-permute-start | bytes 196616 | tf_op jit(solution)/shard_map/ppermute | solution.py:390
  7.6 2.9 %collective-permute-start.2 = (bf16[48,512]{1,0:T(8,128)(2,1)S(1)}, bf16[48,512]{1,0:T(8,128)(2,1)S(1)}, u32[]{:S(2)}, u32[]{:S(2)}) collective-permute-start(bf16[48,512]{1,0:T(8,128)(2,1)S(1)} %get-tuple-element.41), channel_id=1, source_target_pairs={{4,8},{8,4},{5,9},{9,5},{6,10},{10,6},{7,11},{11,7},{20,24},{24,20... | collective-permute-start | bytes 147464 | tf_op jit(solution)/shard_map/ppermute | solution.py:440
  18.0 7.6 %collective-permute-start.4 = (bf16[48,512]{1,0:T(8,128)(2,1)S(1)}, bf16[48,512]{1,0:T(8,128)(2,1)S(1)}, u32[]{:S(2)}, u32[]{:S(2)}) collective-permute-start(bf16[48,512]{1,0:T(8,128)(2,1)S(1)} %get-tuple-element.51), channel_id=1, source_target_pairs={{0,12},{4,8},{8,4},{12,0},{1,13},{5,9},{9,5},{13,1},{2,14},{6,10},... | collective-permute-start | bytes 147464 | tf_op jit(solution)/shard_map/ppermute | solution.py:390
  20.4 5.1 %collective-permute-start.5 = (bf16[48,512]{1,0:T(8,128)(2,1)S(1)}, bf16[48,512]{1,0:T(8,128)(2,1)S(1)}, u32[]{:S(2)}, u32[]{:S(2)}) collective-permute-start(bf16[48,512]{1,0:T(8,128)(2,1)S(1)} %get-tuple-element.52), channel_id=1, source_target_pairs={{0,4},{4,0},{8,12},{12,8},{1,5},{5,1},{9,13},{13,9},{2,6},{6,2},{1... | collective-permute-start | bytes 147464 | tf_op jit(solution)/shard_map/ppermute | solution.py:390
  20.6 4.9 %collective-permute-start.6 = (bf16[33,512]{1,0:T(8,128)(2,1)S(1)}, bf16[33,512]{1,0:T(8,128)(2,1)S(1)}, u32[]{:S(2)}, u32[]{:S(2)}) collective-permute-start(bf16[33,512]{1,0:T(8,128)(2,1)S(1)} %get-tuple-element.49.sums), channel_id=1, source_target_pairs={{0,8},{4,12},{8,0},{12,4},{1,9},{5,13},{9,1},{13,5},{2,10},{6,14},... | collective-permute-start | bytes 101384 | tf_op jit(solution)/shard_map/ppermute | solution.py:390
  25.6 3.9 %collective-permute-start.9 = (bf16[33,512]{1,0:T(8,128)(2,1)S(1)}, bf16[33,512]{1,0:T(8,128)(2,1)S(1)}, u32[]{:S(2)}, u32[]{:S(2)}) collective-permute-start(bf16[33,512]{1,0:T(8,128)(2,1)S(1)} %add_convert_fusion.one), channel_id=1, source_target_pairs={{0,3},{1,2},{2,1},{3,0},{4,7},{5,6},{6,5},{7,4},{8,11},{9,10},{10,... | collective-permute-start | bytes 101384 | tf_op jit(solution)/shard_map/ppermute | solution.py:390
  25.6 4.4 %collective-permute-start.8 = (bf16[33,512]{1,0:T(8,128)(2,1)S(1)}, bf16[33,512]{1,0:T(8,128)(2,1)S(1)}, u32[]{:S(2)}, u32[]{:S(2)}) collective-permute-start(bf16[33,512]{1,0:T(8,128)(2,1)S(1)} %add_convert_fusion.one), channel_id=1, source_target_pairs={{0,2},{1,3},{2,0},{3,1},{4,6},{5,7},{6,4},{7,5},{8,10},{9,11},{10,... | collective-permute-start | bytes 101384 | tf_op jit(solution)/shard_map/ppermute | solution.py:390
  27.2 2.8 %collective-permute-start.7 = (bf16[33,512]{1,0:T(8,128)(2,1)S(1)}, bf16[33,512]{1,0:T(8,128)(2,1)S(1)}, u32[]{:S(2)}, u32[]{:S(2)}) collective-permute-start(bf16[33,512]{1,0:T(8,128)(2,1)S(1)} %add_convert_fusion.one), channel_id=1, source_target_pairs={{0,1},{1,0},{2,3},{3,2},{4,5},{5,4},{6,7},{7,6},{8,9},{9,8},{10,11... | collective-permute-start | bytes 101384 | tf_op jit(solution)/shard_map/ppermute | solution.py:390

commit v6 on v5

--- a/solution.py
+++ b/solution.py
@@ -188,19 +188,23 @@
             hid[rows_in, cols] = (res.astype(F32) + out[rows_in]).astype(BF16).astype(F32)
 
     gain = norm_gain[...]
-    for r in range(0, rows, 32):
-        x = hid[r : r + 32, :]
+    for r in range(0, rows, 16):
+        x = hid[r : r + 16, :]
         x = x - row_mean(x)
         inv = lax.rsqrt(row_mean(x * x) + EPSILON)
         x = x * inv
-        normed[r : r + 32, :] = (x * gain).astype(BF16)
-        x_norm[r : r + 32, :] = x
-        inv_norm[r : r + 32, :] = jnp.broadcast_to(inv, (32, LANES))
+        normed[r : r + 16, :] = (x * gain).astype(BF16)
+        x_norm[r : r + 16, :] = x
+        inv_norm[r : r + 16, :] = jnp.broadcast_to(inv, (16, LANES))
 
     def project(c):
         pair = [w_in[:, at + c * LANES : at + (c + 1) * LANES] for at in (0, channels)]
         glu[c] = dot(normed[...], jnp.concatenate(pair, axis=1))
 
+    offsets = [divmod(HALO + t - rim, 8) for t in range(n_taps)]
+    by_offset = [
+        (at, [(q, t) for t, (q, s) in enumerate(offsets) if s == at]) for at in range(8)
+    ]
     project(0)
     for c in range(channels // LANES):
         cols = slice(c * LANES, (c + 1) * LANES)
@@ -218,10 +222,16 @@
                 left_out[r - HALO : r - HALO + 16, cols] = left
                 sig_out[r - HALO : r - HALO + 16, cols] = sig
             gated[c, r : r + 16, :] = out
-        acc = jnp.zeros((frames, LANES), F32)
-        for t in range(n_taps):
-            acc = acc + kernel[t : t + 1, cols] * gated[c, pl.ds(HALO + t - rim, frames), :]
-        conv[:, cols] = acc
+        accs = [jnp.zeros((8, LANES), F32) for _ in range(frames // 8)]
+        for at, taps_at in by_offset:
+            spread = {q: jnp.broadcast_to(kernel[t : t + 1, cols], (8, LANES)) for q, t in taps_at}
+            for j in range(frames // 8 + 3):
+                tile = gated[c, pl.ds(8 * j + at, 8), :]
+                for q, _ in taps_at:
+                    if 0 <= j - q < frames // 8:
+                        accs[j - q] = accs[j - q] + spread[q] * tile
+        for j, acc in enumerate(accs):
+            conv[8 * j : 8 * j + 8, cols] = acc
 
     gain = conv_gain[...]
     bias = conv_bias[...]
@@ -251,13 +261,16 @@
 
     for c in range(channels // LANES):
         cols = slice(c * LANES, (c + 1) * LANES)
-        accs = [jnp.zeros((8, LANES), F32) for _ in range(n_taps)]
-        for r in range(0, frames, 8):
-            d = d_conv[c, r : r + 8, :]
-            for t in range(n_taps):
-                accs[t] = accs[t] + d * gated[c, pl.ds(HALO + r + t - rim, 8), :]
-        for t in range(n_taps):
-            taps[t * 8 : t * 8 + 8, :] = accs[t]
+        d = [d_conv[c, 8 * j : 8 * j + 8, :] for j in range(frames // 8)]
+        for at, taps_at in by_offset:
+            accs = {q: jnp.zeros((8, LANES), F32) for q, _ in taps_at}
+            for j in range(frames // 8 + 3):
+                tile = gated[c, pl.ds(8 * j + at, 8), :]
+                for q in accs:
+                    if 0 <= j - q < frames // 8:
+                        accs[q] = accs[q] + d[j - q] * tile
+            for q, t in taps_at:
+                taps[t * 8 : t * 8 + 8, :] = accs[q]
         total = taps[pl.ds(0, n_taps, stride=8), :]
         for s in range(1, 8):
             total = total + taps[pl.ds(s, n_taps, stride=8), :]

time: 30.8 us -> 30.6 us (level)
  no operation moved by 1% of the time
where the time goes in v6:
time: 30.6 us; the launch traced here: 30.4 us
  starting transfers between devices  12.7 us (42%)
  Pallas kernels  10.3 us (34%)
  waiting for transfers between devices  6.67 us (22%)
  between operations  0.71 us (2%)
    ppermute x9, starting transfers between devices, flips(): lax.ppermute(array, axis, [(i, i ^ k) for i in range(4)])  12.1 us
    ppermute x9, waiting for transfers between devices, flips(): lax.ppermute(array, axis, [(i, i ^ k) for i in range(4)])  6.67 us
    pallas_call x1, Pallas kernels, per_device(): pl.pallas_call(functools.partial(main_kernel, pairwise, ctx, len(kvs)), o...  3.12 us
    pallas_call x1, Pallas kernels, per_device(): pl.pallas_call(functools.partial(fetch_kernel, len(operands)), out_shape=...  2.25 us
    pallas_call x1, Pallas kernels, per_device(): pl.pallas_call(functools.partial(edge_kernel, pairwise, ctx), out_shape=s...  1.6 us
    pallas_call x1, Pallas kernels, per_device(): pl.pallas_call(inner_kernel, out_shape=(shape((inner, model), BF16), shap...  1.39 us
    pallas_call x1, Pallas kernels, per_device(): pl.pallas_call(functools.partial(pack_kernel, pairwise), out_shape=(shape...  1.28 us
    pallas_call x1, Pallas kernels, per_device(): pl.pallas_call(functools.partial(total_kernel, factor), out_shape=(shape(...  0.65 us
  transfers between devices with their start and end apart: 10, of which 5 were waited for; matrix products, arithmetic and copies ran while one was open for 0% of the time, Pallas kernels for 17%

profile of v6, /device:TPU:0, one launch (start us, length us, event | category | flops | bytes accessed | tf_op | source)
XLA Modules:
  0.0 30.4 jit_solution(10270031491330500085)
XLA Ops:
  0.6 1.3 %shard_map.146 = (bf16[64,512]{1,0:T(8,128)(2,1)S(1)}, bf16[112,512]{1,0:T(8,128)(2,1)S(1)}, bf16[48,512]{1,0:T(8,128)(2,1)S(1)}) custom-call(bf16[128,512]{1,0:T(8,128)(2,1)} %bitcast.17, bf16[128,512]{1,0:T(8,128)(2,1)} %bitcast.18, bf16[128,512]{1,0:T(8,128)(2,1)} %bitcast.14, bf16[128,1024]{1,0:T(8,128)(2,1)} %bitcast.12), custom_call_target="tpu_custom_call" | custom-call | tf_op jit(solution)/shard_map/pallas_call | solution.py:433
  1.9 3.1 %collective-permute-start.3 = (bf16[112,512]{1,0:T(8,128)(2,1)S(1)}, bf16[112,512]{1,0:T(8,128)(2,1)S(1)}, u32[]{:S(2)}, u32[]{:S(2)}) collective-permute-start(bf16[112,512]{1,0:T(8,128)(2,1)S(1)} %get-tuple-element.42), channel_id=1, source_target_pairs={{0,4},{4,0},{8,12},{12,8},{1,5},{5,1},{9,13},{13,9},{2,6},{6,2},{1... | collective-permute-start | bytes 344072 | tf_op jit(solution)/shard_map/ppermute | solution.py:403
  5.0 2.5 %collective-permute-start.1 = (bf16[64,512]{1,0:T(8,128)(2,1)S(1)}, bf16[64,512]{1,0:T(8,128)(2,1)S(1)}, u32[]{:S(2)}, u32[]{:S(2)}) collective-permute-start(bf16[64,512]{1,0:T(8,128)(2,1)S(1)} %get-tuple-element.31.after.refs_9_), channel_id=1, source_target_pairs={{0,12},{4,8},{8,4},{12,0},{1,13},{5,9},{9,5},{13,1},{2,14},{6,10},... | collective-permute-start | bytes 196616 | tf_op jit(solution)/shard_map/ppermute | solution.py:403
  7.5 0.1 collective-permute-start
  7.6 0.7 %collective-permute-start.2 = (bf16[48,512]{1,0:T(8,128)(2,1)S(1)}, bf16[48,512]{1,0:T(8,128)(2,1)S(1)}, u32[]{:S(2)}, u32[]{:S(2)}) collective-permute-start(bf16[48,512]{1,0:T(8,128)(2,1)S(1)} %get-tuple-element.41), channel_id=1, source_target_pairs={{4,8},{8,4},{5,9},{9,5},{6,10},{10,6},{7,11},{11,7},{20,24},{24,20... | collective-permute-start | bytes 147464 | tf_op jit(solution)/shard_map/ppermute | solution.py:453
  8.3 2.2 %shard_map.147 = (bf16[128,512]{1,0:T(8,128)(2,1)S(1)}, bf16[128,1024]{1,0:T(8,128)(2,1)S(1)}, bf16[128,512]{1,0:T(8,128)(2,1)S(1)}, bf16[512,1024]{1,0:T(8,128)...) custom-call(bf16[64,512]{1,0:T(8,128)(2,1)S(1)} %get-tuple-element.3, ...), custom_call_target="tpu_custom_call" | custom-call | tf_op jit(solution)/shard_map/pallas_call | solution.py:464
  10.5 0.0 collective-permute-done.2.refs_12_
  10.5 2.0 %collective-permute-done.1.refs_11_ = bf16[64,512]{1,0:T(8,128)(2,1)S(1)} collective-permute-done((bf16[64,512]{1,0:T(8,128)(2,1)S(1)}, bf16[64,512]{1,0:T(8,128)(2,1)S(1)}, u32[]{:S(2)}, u32[]{:S(2)}) %collective-permute-start.1) | collective-permute-done | bytes 65568 | tf_op jit(solution)/shard_map/ppermute | solution.py:403
  12.5 2.0 %collective-permute-done.refs_10_ = bf16[64,512]{1,0:T(8,128)(2,1)S(1)} collective-permute-done((bf16[64,512]{1,0:T(8,128)(2,1)S(1)}, bf16[64,512]{1,0:T(8,128)(2,1)S(1)}, u32[]{:S(2)}, u32[]{:S(2)}) %collective-permute-start) | collective-permute-done | bytes 65568 | tf_op jit(solution)/shard_map/ppermute | solution.py:403
  14.6 0.0 collective-permute-done.3.refs_13_
  14.6 3.1 %shard_map.148 = (bf16[128,512]{1,0:T(8,128)(2,1)}, f32[160,1024]{1,0:T(8,128)S(1)}, f32[160,128]{1,0:T(8,128)S(1)}, f32[128,512]{1,0:T(8,128)S(1)}, f32[128,512...) custom-call(bf16[128,512]{1,0:T(8,128)(2,1)S(1)} %get-tuple-element., ...), custom_call_target="tpu_custom_call" | custom-call | tf_op jit(solution)/shard_map/pallas_call | solution.py:476
  17.7 2.4 %collective-permute-start.4 = (bf16[48,512]{1,0:T(8,128)(2,1)S(1)}, bf16[48,512]{1,0:T(8,128)(2,1)S(1)}, u32[]{:S(2)}, u32[]{:S(2)}) collective-permute-start(bf16[48,512]{1,0:T(8,128)(2,1)S(1)} %get-tuple-element.51), channel_id=1, source_target_pairs={{0,12},{4,8},{8,4},{12,0},{1,13},{5,9},{9,5},{13,1},{2,14},{6,10},... | collective-permute-start | bytes 147464 | tf_op jit(solution)/shard_map/ppermute | solution.py:403
  20.1 0.2 collective-permute-start.5
  20.4 1.8 %collective-permute-start.6 = (bf16[33,512]{1,0:T(8,128)(2,1)S(1)}, bf16[33,512]{1,0:T(8,128)(2,1)S(1)}, u32[]{:S(2)}, u32[]{:S(2)}) collective-permute-start(bf16[33,512]{1,0:T(8,128)(2,1)S(1)} %get-tuple-element.49.sums), channel_id=1, source_target_pairs={{0,8},{4,12},{8,0},{12,4},{1,9},{5,13},{9,1},{13,5},{2,10},{6,14},... | collective-permute-start | bytes 101384 | tf_op jit(solution)/shard_map/ppermute | solution.py:403
  22.2 1.4 %shard_map.149 = (bf16[96,1024]{1,0:T(8,128)(2,1)S(1)}, bf16[33,512]{1,0:T(8,128)(2,1)S(1)}) custom-call(f32[31,512]{1,0:T(8,128)S(1)} %get-tuple-element.38.refs_6_.kernel, f32[1,1024]{1,0:T(1,128)S(1)} %get-tuple-element.36.refs_4_.norm_gain, bf16[1024,1024]{1,0:T(8,128)(2,1)S(1)} %get-tuple-element.37.refs_5_.w_in, ...), custom_call_target="tpu_custom_call" | custom-call | tf_op jit(solution)/shard_map/pallas_call | solution.py:512
  23.6 1.7 %collective-permute-done.6 = bf16[33,512]{1,0:T(8,128)(2,1)S(1)} collective-permute-done((bf16[33,512]{1,0:T(8,128)(2,1)S(1)}, bf16[33,512]{1,0:T(8,128)(2,1)S(1)}, u32[]{:S(2)}, u32[]{:S(2)}) %collective-permute-start.6) | collective-permute-done | bytes 33824 | tf_op jit(solution)/shard_map/ppermute | solution.py:403
  25.3 0.0 collective-permute-done.4.from_b
  25.3 0.0 collective-permute-done.5.from_a
  25.3 0.1 collective-permute-start.9
  25.4 1.6 %collective-permute-start.8 = (bf16[33,512]{1,0:T(8,128)(2,1)S(1)}, bf16[33,512]{1,0:T(8,128)(2,1)S(1)}, u32[]{:S(2)}, u32[]{:S(2)}) collective-permute-start(bf16[33,512]{1,0:T(8,128)(2,1)S(1)} %add_convert_fusion.one), channel_id=1, source_target_pairs={{0,2},{1,3},{2,0},{3,1},{4,6},{5,7},{6,4},{7,5},{8,10},{9,11},{10,... | collective-permute-start | bytes 101384 | tf_op jit(solution)/shard_map/ppermute | solution.py:403
  26.9 0.3 collective-permute-start.7
  27.2 1.6 %shard_map.150 = bf16[128,1024]{1,0:T(8,128)(2,1)} custom-call(bf16[96,1024]{1,0:T(8,128)(2,1)S(1)} %get-tuple-element.50.inner, bf16[48,512]{1,0:T(8,128)(2,1)S(1)} %collective-permute-done.4.from_b, bf16[48,512]{1,0:T(8,128)(2,1)S(1)} %collective-permute-done.5.from_a, f32[31,512]{1,0:T(8,128)S(1)} %get-tuple-element.38.refs_6_.kernel, ...), custom_call_target="tpu_custom_call" | custom-call | tf_op jit(solution)/shard_map/pallas_call | solution.py:534
  28.8 0.3 %collective-permute-done.9.four = bf16[33,512]{1,0:T(8,128)(2,1)S(1)} collective-permute-done((bf16[33,512]{1,0:T(8,128)(2,1)S(1)}, bf16[33,512]{1,0:T(8,128)(2,1)S(1)}, u32[]{:S(2)}, u32[]{:S(2)}) %collective-permute-start.9) | collective-permute-done | bytes 33824 | tf_op jit(solution)/shard_map/ppermute | solution.py:403
  29.2 0.6 %collective-permute-done.8.three = bf16[33,512]{1,0:T(8,128)(2,1)S(1)} collective-permute-done((bf16[33,512]{1,0:T(8,128)(2,1)S(1)}, bf16[33,512]{1,0:T(8,128)(2,1)S(1)}, u32[]{:S(2)}, u32[]{:S(2)}) %collective-permute-start.8) | collective-permute-done | bytes 33824 | tf_op jit(solution)/shard_map/ppermute | solution.py:403
  29.7 0.0 collective-permute-done.7.two
  29.7 0.7 %shard_map.151 = (f32[31,512]{1,0:T(8,128)}, f32[1,512]{1,0:T(1,128)}, f32[1,512]{1,0:T(1,128)}) custom-call(bf16[33,512]{1,0:T(8,128)(2,1)S(1)} %add_convert_fusion.one, bf16[33,512]{1,0:T(8,128)(2,1)S(1)} %collective-permute-done.7.two, bf16[33,512]{1,0:T(8,128)(2,1)S(1)} %collective-permute-done.8.three, bf16[33,512]{1,0:T(8,128)(2,1)S(1)} %collective-permute-done.9.four), custom_call_target="tpu_custom_call" | custom-call | tf_op jit(solution)/shard_map/pallas_call | solution.py:552
  (1 shorter events, 0.0 us)
Async XLA Ops:
  1.9 12.7 %collective-permute-start.3 = (bf16[112,512]{1,0:T(8,128)(2,1)S(1)}, bf16[112,512]{1,0:T(8,128)(2,1)S(1)}, u32[]{:S(2)}, u32[]{:S(2)}) collective-permute-start(bf16[112,512]{1,0:T(8,128)(2,1)S(1)} %get-tuple-element.42), channel_id=1, source_target_pairs={{0,4},{4,0},{8,12},{12,8},{1,5},{5,1},{9,13},{13,9},{2,6},{6,2},{1... | collective-permute-start | bytes 344072 | tf_op jit(solution)/shard_map/ppermute | solution.py:403
  5.0 7.5 %collective-permute-start.1 = (bf16[64,512]{1,0:T(8,128)(2,1)S(1)}, bf16[64,512]{1,0:T(8,128)(2,1)S(1)}, u32[]{:S(2)}, u32[]{:S(2)}) collective-permute-start(bf16[64,512]{1,0:T(8,128)(2,1)S(1)} %get-tuple-element.31.after.refs_9_), channel_id=1, source_target_pairs={{0,12},{4,8},{8,4},{12,0},{1,13},{5,9},{9,5},{13,1},{2,14},{6,10},... | collective-permute-start | bytes 196616 | tf_op jit(solution)/shard_map/ppermute | solution.py:403
  7.5 7.1 %collective-permute-start = (bf16[64,512]{1,0:T(8,128)(2,1)S(1)}, bf16[64,512]{1,0:T(8,128)(2,1)S(1)}, u32[]{:S(2)}, u32[]{:S(2)}) collective-permute-start(bf16[64,512]{1,0:T(8,128)(2,1)S(1)} %get-tuple-element.31.after.refs_9_), channel_id=1, source_target_pairs={{0,8},{4,12},{8,0},{12,4},{1,9},{5,13},{9,1},{13,5},{2,10},{6,14},... | collective-permute-start | bytes 196616 | tf_op jit(solution)/shard_map/ppermute | solution.py:403
  7.6 2.9 %collective-permute-start.2 = (bf16[48,512]{1,0:T(8,128)(2,1)S(1)}, bf16[48,512]{1,0:T(8,128)(2,1)S(1)}, u32[]{:S(2)}, u32[]{:S(2)}) collective-permute-start(bf16[48,512]{1,0:T(8,128)(2,1)S(1)} %get-tuple-element.41), channel_id=1, source_target_pairs={{4,8},{8,4},{5,9},{9,5},{6,10},{10,6},{7,11},{11,7},{20,24},{24,20... | collective-permute-start | bytes 147464 | tf_op jit(solution)/shard_map/ppermute | solution.py:453
  17.7 7.6 %collective-permute-start.4 = (bf16[48,512]{1,0:T(8,128)(2,1)S(1)}, bf16[48,512]{1,0:T(8,128)(2,1)S(1)}, u32[]{:S(2)}, u32[]{:S(2)}) collective-permute-start(bf16[48,512]{1,0:T(8,128)(2,1)S(1)} %get-tuple-element.51), channel_id=1, source_target_pairs={{0,12},{4,8},{8,4},{12,0},{1,13},{5,9},{9,5},{13,1},{2,14},{6,10},... | collective-permute-start | bytes 147464 | tf_op jit(solution)/shard_map/ppermute | solution.py:403
  20.1 5.1 %collective-permute-start.5 = (bf16[48,512]{1,0:T(8,128)(2,1)S(1)}, bf16[48,512]{1,0:T(8,128)(2,1)S(1)}, u32[]{:S(2)}, u32[]{:S(2)}) collective-permute-start(bf16[48,512]{1,0:T(8,128)(2,1)S(1)} %get-tuple-element.52), channel_id=1, source_target_pairs={{0,4},{4,0},{8,12},{12,8},{1,5},{5,1},{9,13},{13,9},{2,6},{6,2},{1... | collective-permute-start | bytes 147464 | tf_op jit(solution)/shard_map/ppermute | solution.py:403
  20.4 4.9 %collective-permute-start.6 = (bf16[33,512]{1,0:T(8,128)(2,1)S(1)}, bf16[33,512]{1,0:T(8,128)(2,1)S(1)}, u32[]{:S(2)}, u32[]{:S(2)}) collective-permute-start(bf16[33,512]{1,0:T(8,128)(2,1)S(1)} %get-tuple-element.49.sums), channel_id=1, source_target_pairs={{0,8},{4,12},{8,0},{12,4},{1,9},{5,13},{9,1},{13,5},{2,10},{6,14},... | collective-permute-start | bytes 101384 | tf_op jit(solution)/shard_map/ppermute | solution.py:403
  25.3 3.9 %collective-permute-start.9 = (bf16[33,512]{1,0:T(8,128)(2,1)S(1)}, bf16[33,512]{1,0:T(8,128)(2,1)S(1)}, u32[]{:S(2)}, u32[]{:S(2)}) collective-permute-start(bf16[33,512]{1,0:T(8,128)(2,1)S(1)} %add_convert_fusion.one), channel_id=1, source_target_pairs={{0,3},{1,2},{2,1},{3,0},{4,7},{5,6},{6,5},{7,4},{8,11},{9,10},{10,... | collective-permute-start | bytes 101384 | tf_op jit(solution)/shard_map/ppermute | solution.py:403
  25.4 4.4 %collective-permute-start.8 = (bf16[33,512]{1,0:T(8,128)(2,1)S(1)}, bf16[33,512]{1,0:T(8,128)(2,1)S(1)}, u32[]{:S(2)}, u32[]{:S(2)}) collective-permute-start(bf16[33,512]{1,0:T(8,128)(2,1)S(1)} %add_convert_fusion.one), channel_id=1, source_target_pairs={{0,2},{1,3},{2,0},{3,1},{4,6},{5,7},{6,4},{7,5},{8,10},{9,11},{10,... | collective-permute-start | bytes 101384 | tf_op jit(solution)/shard_map/ppermute | solution.py:403
  26.9 2.8 %collective-permute-start.7 = (bf16[33,512]{1,0:T(8,128)(2,1)S(1)}, bf16[33,512]{1,0:T(8,128)(2,1)S(1)}, u32[]{:S(2)}, u32[]{:S(2)}) collective-permute-start(bf16[33,512]{1,0:T(8,128)(2,1)S(1)} %add_convert_fusion.one), channel_id=1, source_target_pairs={{0,1},{1,0},{2,3},{3,2},{4,5},{5,4},{6,7},{7,6},{8,9},{9,8},{10,11... | collective-permute-start | bytes 101384 | tf_op jit(solution)/shard_map/ppermute | solution.py:403

commit v7 on v6

--- a/solution.py
+++ b/solution.py
@@ -115,7 +115,7 @@
 
     pooled = frames // POOL
     if pairwise:
-        own, far, across = kvs
+        own, across, far = kvs
         for side, target in enumerate((k_all, v_all)):
             rows_in = pl.ds(side * pooled, pooled)
             target[0:pooled, :] = own[rows_in, :]
@@ -451,7 +451,7 @@
         (from_a,) = flips(to_a, "ctx", (1,))
         far, across = flips(own, "ctx", (2, 3))
         from_b = lax.ppermute(to_b, "ctx", [(1, 2), (2, 1)])
-        kvs = (own, far, across)
+        kvs = (own, across, far)
     else:
         from_a, from_b = to_neighbours(pairwise, ctx, to_a[2 * pooled :], to_b)
         kvs = tuple(

time: 30.6 us -> 30.3 us (level)
  no operation moved by 1% of the time
where the time goes in v7:
time: 30.3 us; the launch traced here: 30.1 us
  starting transfers between devices  12.7 us (42%)
  Pallas kernels  10.3 us (34%)
  waiting for transfers between devices  6.39 us (21%)
  between operations  0.71 us (2%)
    ppermute x9, starting transfers between devices, flips(): lax.ppermute(array, axis, [(i, i ^ k) for i in range(4)])  12.1 us
    ppermute x9, waiting for transfers between devices, flips(): lax.ppermute(array, axis, [(i, i ^ k) for i in range(4)])  6.39 us
    pallas_call x1, Pallas kernels, per_device(): pl.pallas_call(functools.partial(main_kernel, pairwise, ctx, len(kvs)), o...  3.12 us
    pallas_call x1, Pallas kernels, per_device(): pl.pallas_call(functools.partial(fetch_kernel, len(operands)), out_shape=...  2.25 us
    pallas_call x1, Pallas kernels, per_device(): pl.pallas_call(functools.partial(edge_kernel, pairwise, ctx), out_shape=s...  1.6 us
    pallas_call x1, Pallas kernels, per_device(): pl.pallas_call(inner_kernel, out_shape=(shape((inner, model), BF16), shap...  1.39 us
    pallas_call x1, Pallas kernels, per_device(): pl.pallas_call(functools.partial(pack_kernel, pairwise), out_shape=(shape...  1.28 us
    pallas_call x1, Pallas kernels, per_device(): pl.pallas_call(functools.partial(total_kernel, factor), out_shape=(shape(...  0.65 us
  transfers between devices with their start and end apart: 10, of which 5 were waited for; matrix products, arithmetic and copies ran while one was open for 0% of the time, Pallas kernels for 17%

profile of v7, /device:TPU:0, one launch (start us, length us, event | category | flops | bytes accessed | tf_op | source)
XLA Modules:
  0.0 30.1 jit_solution(5634996267556909578)
XLA Ops:
  0.6 1.3 %shard_map.146 = (bf16[64,512]{1,0:T(8,128)(2,1)S(1)}, bf16[112,512]{1,0:T(8,128)(2,1)S(1)}, bf16[48,512]{1,0:T(8,128)(2,1)S(1)}) custom-call(bf16[128,512]{1,0:T(8,128)(2,1)} %bitcast.17, bf16[128,512]{1,0:T(8,128)(2,1)} %bitcast.18, bf16[128,512]{1,0:T(8,128)(2,1)} %bitcast.14, bf16[128,1024]{1,0:T(8,128)(2,1)} %bitcast.12), custom_call_target="tpu_custom_call" | custom-call | tf_op jit(solution)/shard_map/pallas_call | solution.py:433
  1.9 3.1 %collective-permute-start.3 = (bf16[112,512]{1,0:T(8,128)(2,1)S(1)}, bf16[112,512]{1,0:T(8,128)(2,1)S(1)}, u32[]{:S(2)}, u32[]{:S(2)}) collective-permute-start(bf16[112,512]{1,0:T(8,128)(2,1)S(1)} %get-tuple-element.42), channel_id=1, source_target_pairs={{0,4},{4,0},{8,12},{12,8},{1,5},{5,1},{9,13},{13,9},{2,6},{6,2},{1... | collective-permute-start | bytes 344072 | tf_op jit(solution)/shard_map/ppermute | solution.py:403
  5.0 2.6 %collective-permute-start.1 = (bf16[64,512]{1,0:T(8,128)(2,1)S(1)}, bf16[64,512]{1,0:T(8,128)(2,1)S(1)}, u32[]{:S(2)}, u32[]{:S(2)}) collective-permute-start(bf16[64,512]{1,0:T(8,128)(2,1)S(1)} %get-tuple-element.31.after.refs_9_), channel_id=1, source_target_pairs={{0,8},{4,12},{8,0},{12,4},{1,9},{5,13},{9,1},{13,5},{2,10},{6,14},... | collective-permute-start | bytes 196616 | tf_op jit(solution)/shard_map/ppermute | solution.py:403
  7.6 0.0 collective-permute-start
  7.6 0.7 %collective-permute-start.2 = (bf16[48,512]{1,0:T(8,128)(2,1)S(1)}, bf16[48,512]{1,0:T(8,128)(2,1)S(1)}, u32[]{:S(2)}, u32[]{:S(2)}) collective-permute-start(bf16[48,512]{1,0:T(8,128)(2,1)S(1)} %get-tuple-element.41), channel_id=1, source_target_pairs={{4,8},{8,4},{5,9},{9,5},{6,10},{10,6},{7,11},{11,7},{20,24},{24,20... | collective-permute-start | bytes 147464 | tf_op jit(solution)/shard_map/ppermute | solution.py:453
  8.3 2.2 %shard_map.147 = (bf16[128,512]{1,0:T(8,128)(2,1)S(1)}, bf16[128,1024]{1,0:T(8,128)(2,1)S(1)}, bf16[128,512]{1,0:T(8,128)(2,1)S(1)}, bf16[512,1024]{1,0:T(8,128)...) custom-call(bf16[64,512]{1,0:T(8,128)(2,1)S(1)} %get-tuple-element.3, ...), custom_call_target="tpu_custom_call" | custom-call | tf_op jit(solution)/shard_map/pallas_call | solution.py:464
  10.5 0.0 collective-permute-done.2.refs_12_
  10.5 2.3 %collective-permute-done.1.refs_11_ = bf16[64,512]{1,0:T(8,128)(2,1)S(1)} collective-permute-done((bf16[64,512]{1,0:T(8,128)(2,1)S(1)}, bf16[64,512]{1,0:T(8,128)(2,1)S(1)}, u32[]{:S(2)}, u32[]{:S(2)}) %collective-permute-start.1) | collective-permute-done | bytes 65568 | tf_op jit(solution)/shard_map/ppermute | solution.py:403
  12.8 0.9 %collective-permute-done.refs_10_ = bf16[64,512]{1,0:T(8,128)(2,1)S(1)} collective-permute-done((bf16[64,512]{1,0:T(8,128)(2,1)S(1)}, bf16[64,512]{1,0:T(8,128)(2,1)S(1)}, u32[]{:S(2)}, u32[]{:S(2)}) %collective-permute-start) | collective-permute-done | bytes 65568 | tf_op jit(solution)/shard_map/ppermute | solution.py:403
  13.7 0.0 collective-permute-done.3.refs_13_
  13.7 3.1 %shard_map.148 = (bf16[128,512]{1,0:T(8,128)(2,1)}, f32[160,1024]{1,0:T(8,128)S(1)}, f32[160,128]{1,0:T(8,128)S(1)}, f32[128,512]{1,0:T(8,128)S(1)}, f32[128,512...) custom-call(bf16[128,512]{1,0:T(8,128)(2,1)S(1)} %get-tuple-element., ...), custom_call_target="tpu_custom_call" | custom-call | tf_op jit(solution)/shard_map/pallas_call | solution.py:476
  16.8 2.3 %collective-permute-start.4 = (bf16[48,512]{1,0:T(8,128)(2,1)S(1)}, bf16[48,512]{1,0:T(8,128)(2,1)S(1)}, u32[]{:S(2)}, u32[]{:S(2)}) collective-permute-start(bf16[48,512]{1,0:T(8,128)(2,1)S(1)} %get-tuple-element.51), channel_id=1, source_target_pairs={{0,12},{4,8},{8,4},{12,0},{1,13},{5,9},{9,5},{13,1},{2,14},{6,10},... | collective-permute-start | bytes 147464 | tf_op jit(solution)/shard_map/ppermute | solution.py:403
  19.2 0.9 %collective-permute-start.5 = (bf16[48,512]{1,0:T(8,128)(2,1)S(1)}, bf16[48,512]{1,0:T(8,128)(2,1)S(1)}, u32[]{:S(2)}, u32[]{:S(2)}) collective-permute-start(bf16[48,512]{1,0:T(8,128)(2,1)S(1)} %get-tuple-element.52), channel_id=1, source_target_pairs={{0,4},{4,0},{8,12},{12,8},{1,5},{5,1},{9,13},{13,9},{2,6},{6,2},{1... | collective-permute-start | bytes 147464 | tf_op jit(solution)/shard_map/ppermute | solution.py:403
  20.1 1.2 %collective-permute-start.6 = (bf16[33,512]{1,0:T(8,128)(2,1)S(1)}, bf16[33,512]{1,0:T(8,128)(2,1)S(1)}, u32[]{:S(2)}, u32[]{:S(2)}) collective-permute-start(bf16[33,512]{1,0:T(8,128)(2,1)S(1)} %get-tuple-element.49.sums), channel_id=1, source_target_pairs={{0,8},{4,12},{8,0},{12,4},{1,9},{5,13},{9,1},{13,5},{2,10},{6,14},... | collective-permute-start | bytes 101384 | tf_op jit(solution)/shard_map/ppermute | solution.py:403
  21.3 1.4 %shard_map.149 = (bf16[96,1024]{1,0:T(8,128)(2,1)S(1)}, bf16[33,512]{1,0:T(8,128)(2,1)S(1)}) custom-call(f32[31,512]{1,0:T(8,128)S(1)} %get-tuple-element.38.refs_6_.kernel, f32[1,1024]{1,0:T(1,128)S(1)} %get-tuple-element.36.refs_4_.norm_gain, bf16[1024,1024]{1,0:T(8,128)(2,1)S(1)} %get-tuple-element.37.refs_5_.w_in, ...), custom_call_target="tpu_custom_call" | custom-call | tf_op jit(solution)/shard_map/pallas_call | solution.py:512
  22.7 2.3 %collective-permute-done.6 = bf16[33,512]{1,0:T(8,128)(2,1)S(1)} collective-permute-done((bf16[33,512]{1,0:T(8,128)(2,1)S(1)}, bf16[33,512]{1,0:T(8,128)(2,1)S(1)}, u32[]{:S(2)}, u32[]{:S(2)}) %collective-permute-start.6) | collective-permute-done | bytes 33824 | tf_op jit(solution)/shard_map/ppermute | solution.py:403
  25.0 0.0 collective-permute-done.4.from_b
  25.0 0.0 collective-permute-done.5.from_a
  25.0 0.1 collective-permute-start.9
  25.1 1.6 %collective-permute-start.8 = (bf16[33,512]{1,0:T(8,128)(2,1)S(1)}, bf16[33,512]{1,0:T(8,128)(2,1)S(1)}, u32[]{:S(2)}, u32[]{:S(2)}) collective-permute-start(bf16[33,512]{1,0:T(8,128)(2,1)S(1)} %add_convert_fusion.one), channel_id=1, source_target_pairs={{0,2},{1,3},{2,0},{3,1},{4,6},{5,7},{6,4},{7,5},{8,10},{9,11},{10,... | collective-permute-start | bytes 101384 | tf_op jit(solution)/shard_map/ppermute | solution.py:403
  26.7 0.3 collective-permute-start.7
  26.9 1.6 %shard_map.150 = bf16[128,1024]{1,0:T(8,128)(2,1)} custom-call(bf16[96,1024]{1,0:T(8,128)(2,1)S(1)} %get-tuple-element.50.inner, bf16[48,512]{1,0:T(8,128)(2,1)S(1)} %collective-permute-done.4.from_b, bf16[48,512]{1,0:T(8,128)(2,1)S(1)} %collective-permute-done.5.from_a, f32[31,512]{1,0:T(8,128)S(1)} %get-tuple-element.38.refs_6_.kernel, ...), custom_call_target="tpu_custom_call" | custom-call | tf_op jit(solution)/shard_map/pallas_call | solution.py:534
  28.5 0.3 %collective-permute-done.9.four = bf16[33,512]{1,0:T(8,128)(2,1)S(1)} collective-permute-done((bf16[33,512]{1,0:T(8,128)(2,1)S(1)}, bf16[33,512]{1,0:T(8,128)(2,1)S(1)}, u32[]{:S(2)}, u32[]{:S(2)}) %collective-permute-start.9) | collective-permute-done | bytes 33824 | tf_op jit(solution)/shard_map/ppermute | solution.py:403
  28.9 0.6 %collective-permute-done.8.three = bf16[33,512]{1,0:T(8,128)(2,1)S(1)} collective-permute-done((bf16[33,512]{1,0:T(8,128)(2,1)S(1)}, bf16[33,512]{1,0:T(8,128)(2,1)S(1)}, u32[]{:S(2)}, u32[]{:S(2)}) %collective-permute-start.8) | collective-permute-done | bytes 33824 | tf_op jit(solution)/shard_map/ppermute | solution.py:403
  29.4 0.0 collective-permute-done.7.two
  29.5 0.7 %shard_map.151 = (f32[31,512]{1,0:T(8,128)}, f32[1,512]{1,0:T(1,128)}, f32[1,512]{1,0:T(1,128)}) custom-call(bf16[33,512]{1,0:T(8,128)(2,1)S(1)} %add_convert_fusion.one, bf16[33,512]{1,0:T(8,128)(2,1)S(1)} %collective-permute-done.7.two, bf16[33,512]{1,0:T(8,128)(2,1)S(1)} %collective-permute-done.8.three, bf16[33,512]{1,0:T(8,128)(2,1)S(1)} %collective-permute-done.9.four), custom_call_target="tpu_custom_call" | custom-call | tf_op jit(solution)/shard_map/pallas_call | solution.py:552
  (1 shorter events, 0.0 us)
Async XLA Ops:
  1.9 11.8 %collective-permute-start.3 = (bf16[112,512]{1,0:T(8,128)(2,1)S(1)}, bf16[112,512]{1,0:T(8,128)(2,1)S(1)}, u32[]{:S(2)}, u32[]{:S(2)}) collective-permute-start(bf16[112,512]{1,0:T(8,128)(2,1)S(1)} %get-tuple-element.42), channel_id=1, source_target_pairs={{0,4},{4,0},{8,12},{12,8},{1,5},{5,1},{9,13},{13,9},{2,6},{6,2},{1... | collective-permute-start | bytes 344072 | tf_op jit(solution)/shard_map/ppermute | solution.py:403
  5.0 7.8 %collective-permute-start.1 = (bf16[64,512]{1,0:T(8,128)(2,1)S(1)}, bf16[64,512]{1,0:T(8,128)(2,1)S(1)}, u32[]{:S(2)}, u32[]{:S(2)}) collective-permute-start(bf16[64,512]{1,0:T(8,128)(2,1)S(1)} %get-tuple-element.31.after.refs_9_), channel_id=1, source_target_pairs={{0,8},{4,12},{8,0},{12,4},{1,9},{5,13},{9,1},{13,5},{2,10},{6,14},... | collective-permute-start | bytes 196616 | tf_op jit(solution)/shard_map/ppermute | solution.py:403
  7.6 6.1 %collective-permute-start = (bf16[64,512]{1,0:T(8,128)(2,1)S(1)}, bf16[64,512]{1,0:T(8,128)(2,1)S(1)}, u32[]{:S(2)}, u32[]{:S(2)}) collective-permute-start(bf16[64,512]{1,0:T(8,128)(2,1)S(1)} %get-tuple-element.31.after.refs_9_), channel_id=1, source_target_pairs={{0,12},{4,8},{8,4},{12,0},{1,13},{5,9},{9,5},{13,1},{2,14},{6,10},... | collective-permute-start | bytes 196616 | tf_op jit(solution)/shard_map/ppermute | solution.py:403
  7.6 2.9 %collective-permute-start.2 = (bf16[48,512]{1,0:T(8,128)(2,1)S(1)}, bf16[48,512]{1,0:T(8,128)(2,1)S(1)}, u32[]{:S(2)}, u32[]{:S(2)}) collective-permute-start(bf16[48,512]{1,0:T(8,128)(2,1)S(1)} %get-tuple-element.41), channel_id=1, source_target_pairs={{4,8},{8,4},{5,9},{9,5},{6,10},{10,6},{7,11},{11,7},{20,24},{24,20... | collective-permute-start | bytes 147464 | tf_op jit(solution)/shard_map/ppermute | solution.py:453
  16.8 8.1 %collective-permute-start.4 = (bf16[48,512]{1,0:T(8,128)(2,1)S(1)}, bf16[48,512]{1,0:T(8,128)(2,1)S(1)}, u32[]{:S(2)}, u32[]{:S(2)}) collective-permute-start(bf16[48,512]{1,0:T(8,128)(2,1)S(1)} %get-tuple-element.51), channel_id=1, source_target_pairs={{0,12},{4,8},{8,4},{12,0},{1,13},{5,9},{9,5},{13,1},{2,14},{6,10},... | collective-permute-start | bytes 147464 | tf_op jit(solution)/shard_map/ppermute | solution.py:403
  19.2 5.8 %collective-permute-start.5 = (bf16[48,512]{1,0:T(8,128)(2,1)S(1)}, bf16[48,512]{1,0:T(8,128)(2,1)S(1)}, u32[]{:S(2)}, u32[]{:S(2)}) collective-permute-start(bf16[48,512]{1,0:T(8,128)(2,1)S(1)} %get-tuple-element.52), channel_id=1, source_target_pairs={{0,4},{4,0},{8,12},{12,8},{1,5},{5,1},{9,13},{13,9},{2,6},{6,2},{1... | collective-permute-start | bytes 147464 | tf_op jit(solution)/shard_map/ppermute | solution.py:403
  20.1 4.9 %collective-permute-start.6 = (bf16[33,512]{1,0:T(8,128)(2,1)S(1)}, bf16[33,512]{1,0:T(8,128)(2,1)S(1)}, u32[]{:S(2)}, u32[]{:S(2)}) collective-permute-start(bf16[33,512]{1,0:T(8,128)(2,1)S(1)} %get-tuple-element.49.sums), channel_id=1, source_target_pairs={{0,8},{4,12},{8,0},{12,4},{1,9},{5,13},{9,1},{13,5},{2,10},{6,14},... | collective-permute-start | bytes 101384 | tf_op jit(solution)/shard_map/ppermute | solution.py:403
  25.0 3.9 %collective-permute-start.9 = (bf16[33,512]{1,0:T(8,128)(2,1)S(1)}, bf16[33,512]{1,0:T(8,128)(2,1)S(1)}, u32[]{:S(2)}, u32[]{:S(2)}) collective-permute-start(bf16[33,512]{1,0:T(8,128)(2,1)S(1)} %add_convert_fusion.one), channel_id=1, source_target_pairs={{0,3},{1,2},{2,1},{3,0},{4,7},{5,6},{6,5},{7,4},{8,11},{9,10},{10,... | collective-permute-start | bytes 101384 | tf_op jit(solution)/shard_map/ppermute | solution.py:403
  25.1 4.4 %collective-permute-start.8 = (bf16[33,512]{1,0:T(8,128)(2,1)S(1)}, bf16[33,512]{1,0:T(8,128)(2,1)S(1)}, u32[]{:S(2)}, u32[]{:S(2)}) collective-permute-start(bf16[33,512]{1,0:T(8,128)(2,1)S(1)} %add_convert_fusion.one), channel_id=1, source_target_pairs={{0,2},{1,3},{2,0},{3,1},{4,6},{5,7},{6,4},{7,5},{8,10},{9,11},{10,... | collective-permute-start | bytes 101384 | tf_op jit(solution)/shard_map/ppermute | solution.py:403
  26.7 2.8 %collective-permute-start.7 = (bf16[33,512]{1,0:T(8,128)(2,1)S(1)}, bf16[33,512]{1,0:T(8,128)(2,1)S(1)}, u32[]{:S(2)}, u32[]{:S(2)}) collective-permute-start(bf16[33,512]{1,0:T(8,128)(2,1)S(1)} %add_convert_fusion.one), channel_id=1, source_target_pairs={{0,1},{1,0},{2,3},{3,2},{4,5},{5,4},{6,7},{7,6},{8,9},{9,8},{10,11... | collective-permute-start | bytes 101384 | tf_op jit(solution)/shard_map/ppermute | solution.py:403

commit v8 on v7

--- a/solution.py
+++ b/solution.py
@@ -98,7 +98,7 @@
     from_b, from_a = refs[9 + n_kv : 11 + n_kv]
     (conv_act, x_norm, inv_norm, left_out, sig_out, d_conv) = refs[11 + n_kv : 17 + n_kv]
     to_a, to_b, sums = refs[17 + n_kv : 20 + n_kv]
-    (q_all, r_edge, k_all, v_all, att, hid, normed, gated, conv, glu, taps, act_out, pack, sem) = (
+    (q_all, r_edge, k_all, v_all, att, hid, normed, gated, conv, glu, taps, act_out, pack, lines, sem) = (
         refs[20 + n_kv :]
     )
     frames, width = query.shape
@@ -277,16 +277,21 @@
         pack[0:n_taps, cols] = total
 
     used = n_taps + 2
+    blocks = channels // LANES
+    for c in range(blocks):
+        lines[c * used : (c + 1) * used, :] = pack[0:used, c * LANES : (c + 1) * LANES]
     if pairwise:
-        sums[...] = pack[0:used, :].astype(BF16)
+        sums[...] = lines[0 : blocks * used, :].astype(BF16)
     else:
         sums[...] = pack[0:used, :]
     for target, near in ((to_a, True), (to_b, False)):
-        for c in range(channels // LANES):
+        for c in range(blocks):
             tail, head = d_conv[c, frames - rim :, :], d_conv[c, 0:rim, :]
-            edge = jnp.where(swap, head, tail) if near else jnp.where(swap, tail, head)
-            pack[used : used + rim, c * LANES : (c + 1) * LANES] = edge
-        target[...] = pack[...].astype(BF16)
+            at = blocks * used + c * rim
+            lines[at : at + rim, :] = (
+                jnp.where(swap, head, tail) if near else jnp.where(swap, tail, head)
+            )
+        target[...] = lines[...].astype(BF16)
     write.wait()
 
 
@@ -349,7 +354,8 @@
     edges[1] = from_b[...].astype(F32)
     for c in range(channels // LANES):
         cols = slice(c * LANES, (c + 1) * LANES)
-        a, b = edges[0, used : used + rim, cols], edges[1, used : used + rim, cols]
+        at = channels // LANES * used + c * rim
+        a, b = edges[0, at : at + rim, :], edges[1, at : at + rim, :]
         padded[0, c, HALO - rim : HALO, :] = jnp.where(me == 0, 0.0, jnp.where(swap, a, b))
         padded[0, c, HALO:, :] = d_conv[c, 0 : 2 * HALO, :]
         padded[1, c, 0 : 2 * HALO, :] = d_conv[c, frames - 2 * HALO :, :]
@@ -394,9 +400,12 @@
         three[...].astype(F32) + four[...].astype(F32)
     )
     total = total * factor
-    d_kernel[...] = total[0:n_taps]
-    d_gain[...] = total[n_taps : n_taps + 1]
-    d_bias[...] = total[n_taps + 1 :]
+    used = n_taps + 2
+    for c in range(d_kernel.shape[1] // LANES):
+        cols = slice(c * LANES, (c + 1) * LANES)
+        d_kernel[:, cols] = total[c * used : c * used + n_taps]
+        d_gain[:, cols] = total[c * used + n_taps : c * used + n_taps + 1]
+        d_bias[:, cols] = total[c * used + n_taps + 1 : c * used + n_taps + 2]
 
 
 def flips(array, axis, which):
@@ -473,6 +482,8 @@
 
     rows = frames + 2 * HALO
     used = n_taps + 2
+    sum_rows = channels // LANES * used
+    line_rows = sum_rows + channels // LANES * rim
     conv_act, x_norm, inv_norm, left, sig, d_conv, to_a, to_b, sums = pl.pallas_call(
         functools.partial(main_kernel, pairwise, ctx, len(kvs)),
         out_shape=(
@@ -482,9 +493,9 @@
             shape((frames, channels), F32),
             shape((frames, channels), F32),
             shape((channels // LANES, frames, LANES), F32),
-            shape((used + rim, channels), BF16),
-            shape((used + rim, channels), BF16),
-            shape((used, channels), BF16 if pairwise else F32),
+            shape((line_rows, LANES), BF16),
+            shape((line_rows, LANES), BF16),
+            shape((sum_rows, LANES), BF16) if pairwise else shape((used, channels), F32),
         ),
         in_specs=[VMEM] * (11 + len(kvs)),
         out_specs=(HBM,) + (VMEM,) * 8,
@@ -501,7 +512,8 @@
             pltpu.VMEM((channels // LANES, rows, 2 * LANES), F32),
             pltpu.VMEM((n_taps * 8, LANES), F32),
             pltpu.VMEM((frames, channels), BF16),
-            pltpu.VMEM((used + rim, channels), F32),
+            pltpu.VMEM((used, channels), F32),
+            pltpu.VMEM((line_rows, LANES), F32),
             pltpu.SemaphoreType.DMA,
         ],
         compiler_params=pltpu.CompilerParams(vmem_limit_bytes=32 * 2**20),
@@ -524,7 +536,7 @@
         (from_b,) = flips(to_b, "ctx", (3,))
         (far,) = flips(sums, "ctx", (2,))
         (from_a,) = flips(to_a, "ctx", (1,))
-        near, across = (x[:used].astype(F32) for x in (from_a, from_b))
+        near, across = (x[:sum_rows].astype(F32) for x in (from_a, from_b))
         sums = ((same_sums.astype(F32) + near) + (far.astype(F32) + across)).astype(BF16)
         parts = [sums] + flips(sums, "dp", (1, 2, 3))
     else:
@@ -538,7 +550,7 @@
         out_specs=HBM,
         scratch_shapes=[
             pltpu.VMEM((2, channels // LANES, 3 * HALO, LANES), F32),
-            pltpu.VMEM((2, used + rim, channels), F32),
+            pltpu.VMEM((2, line_rows, LANES), F32),
             pltpu.VMEM((2 * HALO, 2 * channels), BF16),
             pltpu.VMEM((2 * HALO, model), F32),
             pltpu.VMEM((2 * HALO, model), BF16),

time: 30.3 us -> 30 us (0.990)
  waiting for transfers between devices: 6.39 us -> 6.06 us
    ppermute x9, waiting for transfers between devices: 6.39 us -> 6.06 us  [flips(): lax.ppermute(array, axis, [(i, i ^ k) for i in range(4)])]
  transfers between devices with their start and end apart: 10 -> 10, of which waited for: 5 -> 5; matrix products, arithmetic and copies ran while one was open for 0% -> 0% of each run, Pallas kernels for 17% -> 18%
where the time goes in v8:
time: 30 us; the launch traced here: 29.8 us
  starting transfers between devices  12.7 us (42%)
  Pallas kernels  10.3 us (34%)
  waiting for transfers between devices  6.06 us (20%)
  between operations  0.71 us (2%)
    ppermute x9, starting transfers between devices, flips(): lax.ppermute(array, axis, [(i, i ^ k) for i in range(4)])  12.1 us
    ppermute x9, waiting for transfers between devices, flips(): lax.ppermute(array, axis, [(i, i ^ k) for i in range(4)])  6.06 us
    pallas_call x1, Pallas kernels, per_device(): pl.pallas_call(functools.partial(main_kernel, pairwise, ctx, len(kvs)), o...  3.13 us
    pallas_call x1, Pallas kernels, per_device(): pl.pallas_call(functools.partial(fetch_kernel, len(operands)), out_shape=...  2.25 us
    pallas_call x1, Pallas kernels, per_device(): pl.pallas_call(functools.partial(edge_kernel, pairwise, ctx), out_shape=s...  1.6 us
    pallas_call x1, Pallas kernels, per_device(): pl.pallas_call(inner_kernel, out_shape=(shape((inner, model), BF16), shap...  1.39 us
    pallas_call x1, Pallas kernels, per_device(): pl.pallas_call(functools.partial(pack_kernel, pairwise), out_shape=(shape...  1.28 us
    pallas_call x1, Pallas kernels, per_device(): pl.pallas_call(functools.partial(total_kernel, factor), out_shape=(shape(...  0.66 us
  transfers between devices with their start and end apart: 10, of which 5 were waited for; matrix products, arithmetic and copies ran while one was open for 0% of the time, Pallas kernels for 18%

profile of v8, /device:TPU:0, one launch (start us, length us, event | category | flops | bytes accessed | tf_op | source)
XLA Modules:
  0.0 29.8 jit_solution(15062157790518104399)
XLA Ops:
  0.6 1.3 %shard_map.146 = (bf16[64,512]{1,0:T(8,128)(2,1)S(1)}, bf16[112,512]{1,0:T(8,128)(2,1)S(1)}, bf16[48,512]{1,0:T(8,128)(2,1)S(1)}) custom-call(bf16[128,512]{1,0:T(8,128)(2,1)} %bitcast.17, bf16[128,512]{1,0:T(8,128)(2,1)} %bitcast.18, bf16[128,512]{1,0:T(8,128)(2,1)} %bitcast.14, bf16[128,1024]{1,0:T(8,128)(2,1)} %bitcast.12), custom_call_target="tpu_custom_call" | custom-call | tf_op jit(solution)/shard_map/pallas_call | solution.py:442
  1.9 3.1 %collective-permute-start.3 = (bf16[112,512]{1,0:T(8,128)(2,1)S(1)}, bf16[112,512]{1,0:T(8,128)(2,1)S(1)}, u32[]{:S(2)}, u32[]{:S(2)}) collective-permute-start(bf16[112,512]{1,0:T(8,128)(2,1)S(1)} %get-tuple-element.42), channel_id=1, source_target_pairs={{0,4},{4,0},{8,12},{12,8},{1,5},{5,1},{9,13},{13,9},{2,6},{6,2},{1... | collective-permute-start | bytes 344072 | tf_op jit(solution)/shard_map/ppermute | solution.py:412
  5.0 2.6 %collective-permute-start.1 = (bf16[64,512]{1,0:T(8,128)(2,1)S(1)}, bf16[64,512]{1,0:T(8,128)(2,1)S(1)}, u32[]{:S(2)}, u32[]{:S(2)}) collective-permute-start(bf16[64,512]{1,0:T(8,128)(2,1)S(1)} %get-tuple-element.31.after.refs_9_), channel_id=1, source_target_pairs={{0,8},{4,12},{8,0},{12,4},{1,9},{5,13},{9,1},{13,5},{2,10},{6,14},... | collective-permute-start | bytes 196616 | tf_op jit(solution)/shard_map/ppermute | solution.py:412
  7.6 0.0 collective-permute-start
  7.6 0.7 %collective-permute-start.2 = (bf16[48,512]{1,0:T(8,128)(2,1)S(1)}, bf16[48,512]{1,0:T(8,128)(2,1)S(1)}, u32[]{:S(2)}, u32[]{:S(2)}) collective-permute-start(bf16[48,512]{1,0:T(8,128)(2,1)S(1)} %get-tuple-element.41), channel_id=1, source_target_pairs={{4,8},{8,4},{5,9},{9,5},{6,10},{10,6},{7,11},{11,7},{20,24},{24,20... | collective-permute-start | bytes 147464 | tf_op jit(solution)/shard_map/ppermute | solution.py:462
  8.3 2.2 %shard_map.147 = (bf16[128,512]{1,0:T(8,128)(2,1)S(1)}, bf16[128,1024]{1,0:T(8,128)(2,1)S(1)}, bf16[128,512]{1,0:T(8,128)(2,1)S(1)}, bf16[512,1024]{1,0:T(8,128)...) custom-call(bf16[64,512]{1,0:T(8,128)(2,1)S(1)} %get-tuple-element.3, ...), custom_call_target="tpu_custom_call" | custom-call | tf_op jit(solution)/shard_map/pallas_call | solution.py:473
  10.5 0.0 collective-permute-done.2.refs_12_
  10.5 2.3 %collective-permute-done.1.refs_11_ = bf16[64,512]{1,0:T(8,128)(2,1)S(1)} collective-permute-done((bf16[64,512]{1,0:T(8,128)(2,1)S(1)}, bf16[64,512]{1,0:T(8,128)(2,1)S(1)}, u32[]{:S(2)}, u32[]{:S(2)}) %collective-permute-start.1) | collective-permute-done | bytes 65568 | tf_op jit(solution)/shard_map/ppermute | solution.py:412
  12.8 0.9 %collective-permute-done.refs_10_ = bf16[64,512]{1,0:T(8,128)(2,1)S(1)} collective-permute-done((bf16[64,512]{1,0:T(8,128)(2,1)S(1)}, bf16[64,512]{1,0:T(8,128)(2,1)S(1)}, u32[]{:S(2)}, u32[]{:S(2)}) %collective-permute-start) | collective-permute-done | bytes 65568 | tf_op jit(solution)/shard_map/ppermute | solution.py:412
  13.7 0.0 collective-permute-done.3.refs_13_
  13.7 3.1 %shard_map.148 = (bf16[128,512]{1,0:T(8,128)(2,1)}, f32[160,1024]{1,0:T(8,128)S(1)}, f32[160,128]{1,0:T(8,128)S(1)}, f32[128,512]{1,0:T(8,128)S(1)}, f32[128,512...) custom-call(bf16[128,512]{1,0:T(8,128)(2,1)S(1)} %get-tuple-element., ...), custom_call_target="tpu_custom_call" | custom-call | tf_op jit(solution)/shard_map/pallas_call | solution.py:487
  16.9 2.3 %collective-permute-start.4 = (bf16[192,128]{1,0:T(8,128)(2,1)S(1)}, bf16[192,128]{1,0:T(8,128)(2,1)S(1)}, u32[]{:S(2)}, u32[]{:S(2)}) collective-permute-start(bf16[192,128]{1,0:T(8,128)(2,1)S(1)} %get-tuple-element.51), channel_id=1, source_target_pairs={{0,12},{4,8},{8,4},{12,0},{1,13},{5,9},{9,5},{13,1},{2,14},{6,10},... | collective-permute-start | bytes 147464 | tf_op jit(solution)/shard_map/ppermute | solution.py:412
  19.2 0.9 %collective-permute-start.5 = (bf16[192,128]{1,0:T(8,128)(2,1)S(1)}, bf16[192,128]{1,0:T(8,128)(2,1)S(1)}, u32[]{:S(2)}, u32[]{:S(2)}) collective-permute-start(bf16[192,128]{1,0:T(8,128)(2,1)S(1)} %get-tuple-element.52), channel_id=1, source_target_pairs={{0,4},{4,0},{8,12},{12,8},{1,5},{5,1},{9,13},{13,9},{2,6},{6,2},{1... | collective-permute-start | bytes 147464 | tf_op jit(solution)/shard_map/ppermute | solution.py:412
  20.1 1.2 %collective-permute-start.6 = (bf16[132,128]{1,0:T(8,128)(2,1)S(1)}, bf16[132,128]{1,0:T(8,128)(2,1)S(1)}, u32[]{:S(2)}, u32[]{:S(2)}) collective-permute-start(bf16[132,128]{1,0:T(8,128)(2,1)S(1)} %get-tuple-element.49.sums), channel_id=1, source_target_pairs={{0,8},{4,12},{8,0},{12,4},{1,9},{5,13},{9,1},{13,5},{2,10},{6,14},... | collective-permute-start | bytes 101384 | tf_op jit(solution)/shard_map/ppermute | solution.py:412
  21.3 1.4 %shard_map.149 = (bf16[96,1024]{1,0:T(8,128)(2,1)S(1)}, bf16[132,128]{1,0:T(8,128)(2,1)S(1)}) custom-call(f32[31,512]{1,0:T(8,128)S(1)} %get-tuple-element.38.refs_6_.kernel, f32[1,1024]{1,0:T(1,128)S(1)} %get-tuple-element.36.refs_4_.norm_gain, bf16[1024,1024]{1,0:T(8,128)(2,1)S(1)} %get-tuple-element.37.refs_5_.w_in, ...), custom_call_target="tpu_custom_call" | custom-call | tf_op jit(solution)/shard_map/pallas_call | solution.py:524
  22.7 2.2 %collective-permute-done.6 = bf16[132,128]{1,0:T(8,128)(2,1)S(1)} collective-permute-done((bf16[132,128]{1,0:T(8,128)(2,1)S(1)}, bf16[132,128]{1,0:T(8,128)(2,1)S(1)}, u32[]{:S(2)}, u32[]{:S(2)}) %collective-permute-start.6) | collective-permute-done | bytes 33824 | tf_op jit(solution)/shard_map/ppermute | solution.py:412
  24.9 0.0 collective-permute-done.4.from_b
  24.9 0.0 collective-permute-done.5.from_a
  25.0 0.1 collective-permute-start.9
  25.0 1.6 %collective-permute-start.8 = (bf16[132,128]{1,0:T(8,128)(2,1)S(1)}, bf16[132,128]{1,0:T(8,128)(2,1)S(1)}, u32[]{:S(2)}, u32[]{:S(2)}) collective-permute-start(bf16[132,128]{1,0:T(8,128)(2,1)S(1)} %add_convert_fusion.one), channel_id=1, source_target_pairs={{0,2},{1,3},{2,0},{3,1},{4,6},{5,7},{6,4},{7,5},{8,10},{9,11},{10,... | collective-permute-start | bytes 101384 | tf_op jit(solution)/shard_map/ppermute | solution.py:412
  26.6 0.3 collective-permute-start.7
  26.9 1.6 %shard_map.150 = bf16[128,1024]{1,0:T(8,128)(2,1)} custom-call(bf16[96,1024]{1,0:T(8,128)(2,1)S(1)} %get-tuple-element.50.inner, bf16[192,128]{1,0:T(8,128)(2,1)S(1)} %collective-permute-done.4.from_b, bf16[192,128]{1,0:T(8,128)(2,1)S(1)} %collective-permute-done.5.from_a, f32[31,512]{1,0:T(8,128)S(1)} %get-tuple-element.38.refs_6_.kernel, ...), custom_call_target="tpu_custom_call" | custom-call | tf_op jit(solution)/shard_map/pallas_call | solution.py:546
  28.5 0.2 collective-permute-done.9.four
  28.7 0.4 %collective-permute-done.8.three = bf16[132,128]{1,0:T(8,128)(2,1)S(1)} collective-permute-done((bf16[132,128]{1,0:T(8,128)(2,1)S(1)}, bf16[132,128]{1,0:T(8,128)(2,1)S(1)}, u32[]{:S(2)}, u32[]{:S(2)}) %collective-permute-start.8) | collective-permute-done | bytes 33824 | tf_op jit(solution)/shard_map/ppermute | solution.py:412
  29.1 0.0 collective-permute-done.7.two
  29.1 0.7 %shard_map.151 = (f32[31,512]{1,0:T(8,128)}, f32[1,512]{1,0:T(1,128)}, f32[1,512]{1,0:T(1,128)}) custom-call(bf16[132,128]{1,0:T(8,128)(2,1)S(1)} %add_convert_fusion.one, bf16[132,128]{1,0:T(8,128)(2,1)S(1)} %collective-permute-done.7.two, bf16[132,128]{1,0:T(8,128)(2,1)S(1)} %collective-permute-done.8.three, bf16[132,128]{1,0:T(8,128)(2,1)S(1)} %collective-permute-done.9.four), custom_call_target="tpu_custom_call" | custom-call | tf_op jit(solution)/shard_map/pallas_call | solution.py:564
  (1 shorter events, 0.0 us)
Async XLA Ops:
  1.9 11.8 %collective-permute-start.3 = (bf16[112,512]{1,0:T(8,128)(2,1)S(1)}, bf16[112,512]{1,0:T(8,128)(2,1)S(1)}, u32[]{:S(2)}, u32[]{:S(2)}) collective-permute-start(bf16[112,512]{1,0:T(8,128)(2,1)S(1)} %get-tuple-element.42), channel_id=1, source_target_pairs={{0,4},{4,0},{8,12},{12,8},{1,5},{5,1},{9,13},{13,9},{2,6},{6,2},{1... | collective-permute-start | bytes 344072 | tf_op jit(solution)/shard_map/ppermute | solution.py:412
  5.0 7.8 %collective-permute-start.1 = (bf16[64,512]{1,0:T(8,128)(2,1)S(1)}, bf16[64,512]{1,0:T(8,128)(2,1)S(1)}, u32[]{:S(2)}, u32[]{:S(2)}) collective-permute-start(bf16[64,512]{1,0:T(8,128)(2,1)S(1)} %get-tuple-element.31.after.refs_9_), channel_id=1, source_target_pairs={{0,8},{4,12},{8,0},{12,4},{1,9},{5,13},{9,1},{13,5},{2,10},{6,14},... | collective-permute-start | bytes 196616 | tf_op jit(solution)/shard_map/ppermute | solution.py:412
  7.6 6.1 %collective-permute-start = (bf16[64,512]{1,0:T(8,128)(2,1)S(1)}, bf16[64,512]{1,0:T(8,128)(2,1)S(1)}, u32[]{:S(2)}, u32[]{:S(2)}) collective-permute-start(bf16[64,512]{1,0:T(8,128)(2,1)S(1)} %get-tuple-element.31.after.refs_9_), channel_id=1, source_target_pairs={{0,12},{4,8},{8,4},{12,0},{1,13},{5,9},{9,5},{13,1},{2,14},{6,10},... | collective-permute-start | bytes 196616 | tf_op jit(solution)/shard_map/ppermute | solution.py:412
  7.6 2.9 %collective-permute-start.2 = (bf16[48,512]{1,0:T(8,128)(2,1)S(1)}, bf16[48,512]{1,0:T(8,128)(2,1)S(1)}, u32[]{:S(2)}, u32[]{:S(2)}) collective-permute-start(bf16[48,512]{1,0:T(8,128)(2,1)S(1)} %get-tuple-element.41), channel_id=1, source_target_pairs={{4,8},{8,4},{5,9},{9,5},{6,10},{10,6},{7,11},{11,7},{20,24},{24,20... | collective-permute-start | bytes 147464 | tf_op jit(solution)/shard_map/ppermute | solution.py:462
  16.9 8.1 %collective-permute-start.4 = (bf16[192,128]{1,0:T(8,128)(2,1)S(1)}, bf16[192,128]{1,0:T(8,128)(2,1)S(1)}, u32[]{:S(2)}, u32[]{:S(2)}) collective-permute-start(bf16[192,128]{1,0:T(8,128)(2,1)S(1)} %get-tuple-element.51), channel_id=1, source_target_pairs={{0,12},{4,8},{8,4},{12,0},{1,13},{5,9},{9,5},{13,1},{2,14},{6,10},... | collective-permute-start | bytes 147464 | tf_op jit(solution)/shard_map/ppermute | solution.py:412
  19.2 5.7 %collective-permute-start.5 = (bf16[192,128]{1,0:T(8,128)(2,1)S(1)}, bf16[192,128]{1,0:T(8,128)(2,1)S(1)}, u32[]{:S(2)}, u32[]{:S(2)}) collective-permute-start(bf16[192,128]{1,0:T(8,128)(2,1)S(1)} %get-tuple-element.52), channel_id=1, source_target_pairs={{0,4},{4,0},{8,12},{12,8},{1,5},{5,1},{9,13},{13,9},{2,6},{6,2},{1... | collective-permute-start | bytes 147464 | tf_op jit(solution)/shard_map/ppermute | solution.py:412
  20.1 4.8 %collective-permute-start.6 = (bf16[132,128]{1,0:T(8,128)(2,1)S(1)}, bf16[132,128]{1,0:T(8,128)(2,1)S(1)}, u32[]{:S(2)}, u32[]{:S(2)}) collective-permute-start(bf16[132,128]{1,0:T(8,128)(2,1)S(1)} %get-tuple-element.49.sums), channel_id=1, source_target_pairs={{0,8},{4,12},{8,0},{12,4},{1,9},{5,13},{9,1},{13,5},{2,10},{6,14},... | collective-permute-start | bytes 101384 | tf_op jit(solution)/shard_map/ppermute | solution.py:412
  25.0 3.8 %collective-permute-start.9 = (bf16[132,128]{1,0:T(8,128)(2,1)S(1)}, bf16[132,128]{1,0:T(8,128)(2,1)S(1)}, u32[]{:S(2)}, u32[]{:S(2)}) collective-permute-start(bf16[132,128]{1,0:T(8,128)(2,1)S(1)} %add_convert_fusion.one), channel_id=1, source_target_pairs={{0,3},{1,2},{2,1},{3,0},{4,7},{5,6},{6,5},{7,4},{8,11},{9,10},{10,... | collective-permute-start | bytes 101384 | tf_op jit(solution)/shard_map/ppermute | solution.py:412
  25.0 4.1 %collective-permute-start.8 = (bf16[132,128]{1,0:T(8,128)(2,1)S(1)}, bf16[132,128]{1,0:T(8,128)(2,1)S(1)}, u32[]{:S(2)}, u32[]{:S(2)}) collective-permute-start(bf16[132,128]{1,0:T(8,128)(2,1)S(1)} %add_convert_fusion.one), channel_id=1, source_target_pairs={{0,2},{1,3},{2,0},{3,1},{4,6},{5,7},{6,4},{7,5},{8,10},{9,11},{10,... | collective-permute-start | bytes 101384 | tf_op jit(solution)/shard_map/ppermute | solution.py:412
  26.6 2.5 %collective-permute-start.7 = (bf16[132,128]{1,0:T(8,128)(2,1)S(1)}, bf16[132,128]{1,0:T(8,128)(2,1)S(1)}, u32[]{:S(2)}, u32[]{:S(2)}) collective-permute-start(bf16[132,128]{1,0:T(8,128)(2,1)S(1)} %add_convert_fusion.one), channel_id=1, source_target_pairs={{0,1},{1,0},{2,3},{3,2},{4,5},{5,4},{6,7},{7,6},{8,9},{9,8},{10,11... | collective-permute-start | bytes 101384 | tf_op jit(solution)/shard_map/ppermute | solution.py:412
